TPU v7x, 32 devices: a whole 2x2x4 slice. The times are simulated.
32 devices in a mesh: wide: 8 (over z, core), narrow: 4 (over y, x).
Axes of the slice: x: 2, y: 2, z: 4, core: 2. Of those that a mesh axis runs over, the one named last changes fastest.
Arguments:
- activations: bfloat16 [6144, 4096], P('wide'), may hold values from -12 to 12
- gain: bfloat16 [4096], replicated, may hold values from 0.099609375 to 1.8984375
- w_query: bfloat16 [4096, 4096], P('wide', 'narrow'), may hold values from -0.5 to 0.5
- w_key: bfloat16 [4096, 1024], P('wide', 'narrow'), may hold values from -14 to 14
- w_value: bfloat16 [4096, 1024], P('wide', 'narrow'), may hold values from -0.09375 to 0.09375
- w_out: bfloat16 [4096, 4096], P('wide', 'narrow'), may hold values from -0.09375 to 0.09375
- cotangent: bfloat16 [6144, 4096], P('wide'), may hold values from -6 to 6
Outputs:
- outputs: bfloat16 [6144, 4096], P('wide', 'narrow')
- grad_query: float32 [4096, 4096], P('wide', 'narrow')
- grad_key: float32 [4096, 1024], P('wide', 'narrow')
- grad_value: float32 [4096, 1024], P('wide', 'narrow')
- grad_out: float32 [4096, 4096], P('wide', 'narrow')
All inputs are finite; a program needn't handle non-finite values.
Results may differ from a plain program's by a relative error of at most 0.017.
The roundings to bfloat16 on the way count: a program that leaves them out, or rounds other values in their place, can miss the bound.
Values may be sent and summed in bfloat16 or wider, within the bound.
No kernel may reach another device: no remote copies, remote signals or barrier semaphores. Data moves between devices by JAX's collectives and lax.ppermute only.
A program may use at most 192 MiB of HBM per device.

v0:
```python
import jax
import jax.numpy as jnp
from jax import lax
from jax.sharding import PartitionSpec as P

HEAD_DIM = 128


epsilon = 1e-05
masked_score = -1e30


def normalize(rows, gain):
    values32 = rows.astype(jnp.float32)
    mean_square = jnp.mean(values32 * values32, axis=-1, keepdims=True)
    return (values32 * lax.rsqrt(mean_square + epsilon) * gain.astype(jnp.float32)).astype(
        jnp.bfloat16
    )


def split_heads(queries, key_rows, value_rows, width):
    length = queries.shape[0]
    groups = key_rows.shape[1] // width
    members = queries.shape[1] // key_rows.shape[1]
    query_split = queries.reshape(length, groups, members, width)
    key_split = key_rows.reshape(length, groups, width)
    value_split = value_rows.reshape(length, groups, width)
    return (query_split, key_split, value_split)


def attend_forward(queries, key_rows, value_rows, width):
    length = queries.shape[0]
    query_split, key_split, value_split = split_heads(queries, key_rows, value_rows, width)
    scores = jnp.einsum(
        "sjgd,tjd->jgst", query_split, key_split, preferred_element_type=jnp.float32
    ) * width ** (-0.5)
    causal = lax.broadcasted_iota(jnp.int32, (length, length), 0) >= lax.broadcasted_iota(
        jnp.int32, (length, length), 1
    )
    scores = jnp.where(causal, scores, masked_score)
    highest = jnp.max(scores, axis=-1, keepdims=True)
    exponent = jnp.exp(scores - highest)
    attn_probs = exponent / jnp.sum(exponent, axis=-1, keepdims=True)
    rounded = attn_probs.astype(jnp.bfloat16)
    mixed = jnp.einsum("jgst,tjd->sjgd", rounded, value_split, preferred_element_type=jnp.float32)
    return (attn_probs, rounded, mixed.reshape(length, -1).astype(jnp.bfloat16))


def attend_backward(attn_probs, rounded, queries, key_rows, value_rows, grad_mixed, width):
    length = queries.shape[0]
    query_split, key_split, value_split = split_heads(queries, key_rows, value_rows, width)
    grad_split = grad_mixed.reshape(query_split.shape)
    grad_values = jnp.einsum(
        "jgst,sjgd->tjd", rounded, grad_split, preferred_element_type=jnp.float32
    )
    grad_probs = jnp.einsum(
        "sjgd,tjd->jgst", grad_split, value_split, preferred_element_type=jnp.float32
    )
    inner = jnp.sum(grad_probs * attn_probs, axis=-1, keepdims=True)
    grad_scores = (attn_probs * (grad_probs - inner) * width ** (-0.5)).astype(jnp.bfloat16)
    grad_queries = jnp.einsum(
        "jgst,tjd->sjgd", grad_scores, key_split, preferred_element_type=jnp.float32
    )
    grad_keys = jnp.einsum(
        "jgst,sjgd->tjd", grad_scores, query_split, preferred_element_type=jnp.float32
    )
    return (
        grad_queries.reshape(length, -1).astype(jnp.bfloat16),
        grad_keys.reshape(length, -1).astype(jnp.bfloat16),
        grad_values.reshape(length, -1).astype(jnp.bfloat16),
    )


def row_product(left_rows, right):
    return lax.dot_general(
        left_rows, right, (((0,), (0,)), ((), ())), preferred_element_type=jnp.float32
    )


def shards(activations, gain, w_query, w_key, w_value, w_out, cotangent):
    width = HEAD_DIM
    normed = normalize(activations, gain)
    pieces = (
        lax.all_gather(w_query, "wide", axis=0, tiled=True),
        lax.all_gather(w_key, "wide", axis=0, tiled=True),
        lax.all_gather(w_value, "wide", axis=0, tiled=True),
    )
    columns = normed
    sums_query, sums_key, sums_value = tuple(
        (jnp.dot(columns, portion, preferred_element_type=jnp.float32) for portion in pieces)
    )
    queries = sums_query.astype(jnp.bfloat16)
    key_rows = sums_key.astype(jnp.bfloat16)
    value_rows = sums_value.astype(jnp.bfloat16)
    attn_probs, rounded, mixed = attend_forward(queries, key_rows, value_rows, width)
    projected = lax.dot_general(
        mixed,
        lax.all_gather(w_out, "wide", axis=0, tiled=True),
        (((1,), (1,)), ((), ())),
        preferred_element_type=jnp.float32,
    )
    summed = lax.psum_scatter(
        projected.astype(jnp.bfloat16), "narrow", scatter_dimension=1, tiled=True
    ).astype(jnp.float32)
    share = summed.shape[1]
    own_columns = lax.dynamic_slice_in_dim(activations, lax.axis_index("narrow") * share, share, 1)
    outputs = (own_columns.astype(jnp.float32) + summed).astype(jnp.bfloat16)
    columns = cotangent
    grad_sums = jnp.dot(
        columns,
        lax.all_gather(w_out, "wide", axis=0, tiled=True),
        preferred_element_type=jnp.float32,
    )
    grad_mixed = grad_sums.astype(jnp.bfloat16)
    grad_queries, grad_keys, grad_values = attend_backward(
        attn_probs, rounded, queries, key_rows, value_rows, grad_mixed, width
    )
    query_cols = w_query.shape[1]
    key_cols = w_key.shape[1]
    columns = cotangent
    joined = lax.psum_scatter(
        jnp.concatenate(
            [
                jnp.concatenate(
                    [
                        row_product(normed, grad_queries),
                        row_product(normed, grad_keys),
                        row_product(normed, grad_values),
                    ],
                    axis=1,
                ),
                row_product(columns, mixed),
            ],
            axis=1,
        ).astype(jnp.bfloat16),
        "wide",
        scatter_dimension=0,
        tiled=True,
    ).astype(jnp.float32)
    grad_out = joined[:, query_cols + 2 * key_cols :]
    grad_query = joined[:, :query_cols]
    grad_key = joined[:, query_cols : query_cols + key_cols]
    grad_value = joined[:, query_cols + key_cols : query_cols + 2 * key_cols]
    return (outputs, grad_query, grad_key, grad_value, grad_out)


def solution(mesh):
    return jax.shard_map(
        shards,
        mesh=mesh,
        in_specs=(
            P("wide", None),
            P(),
            P("wide", "narrow"),
            P("wide", "narrow"),
            P("wide", "narrow"),
            P("wide", "narrow"),
            P("wide", None),
        ),
        out_specs=(
            P("wide", "narrow"),
            P("wide", "narrow"),
            P("wide", "narrow"),
            P("wide", "narrow"),
            P("wide", "narrow"),
        ),
        check_vma=False,
    )
```

profile of v0, /device:TPU:0, one launch (start us, length us, event | category | flops | bytes accessed | tf_op | source)
XLA Modules:
  0.0 601.5 jit_solution(1498754214516028831)
XLA Ops:
  7.2 0.0 all-gather.7.cloned.1.call-start
  7.2 0.7 all-gather.7.cloned.1.call-update
  7.9 0.0 all-gather.5.cloned.1.call-start
  7.9 0.7 all-gather.5.cloned.1.call-update
  8.6 0.0 all-gather.9.cloned.1.call-start
  8.7 0.7 all-gather.9.cloned.1.call-update
  9.4 0.0 all-gather.11.cloned.1.call-start
  9.4 0.5 all-gather.11.cloned.1.call-update
  10.0 0.0 reduce-scatter.3.cloned.1.call-start
  10.0 0.7 convert_element_type.81
  10.7 1.0 iota_compare_fusion
  11.7 4.1 fusion.6
  15.8 0.0 copy-start
  15.8 25.6 %all-gather.7.cloned.1.call-done = bf16[4096,256]{1,0:T(8,128)(2,1)} async-done(((bf16[512,256]{1,0:T(8,128)(2,1)}), bf16[4096,256]{1,0:T(8,128)(2,1)}) %all-gather.7.cloned.1.call-update) | async-done | bytes 2097168 | tf_op jit(solution)/shard_map/all_gather | solution.py:85
  41.4 6.3 %convolution_convert_fusion.6 = bf16[768,256]{0,1:T(8,128)(2,1)} fusion(bf16[4096,256]{1,0:T(8,128)(2,1)} %all-gather.7.cloned.1.call-done, bf16[768,4096]{1,0:T(8,128)(2,1)} %param.7, f32[4096]{0:T(1024)S(1)} %convert_element_type.81, f32[768]{0:T(1024)S(1)} %add_rsqrt_fusion), kind=kOutput, calls=%fused_computation.43 | convolution fusion | flops 1623392256 | bytes 8801280 | tf_op jit(solution)/shard_map/dot_general | solution.py:90
  47.7 23.9 %all-gather.5.cloned.1.call-done = bf16[4096,256]{1,0:T(8,128)(2,1)} async-done(((bf16[512,256]{1,0:T(8,128)(2,1)}), bf16[4096,256]{1,0:T(8,128)(2,1)}) %all-gather.5.cloned.1.call-update) | async-done | bytes 2097168 | tf_op jit(solution)/shard_map/all_gather | solution.py:86
  71.7 5.6 convolution_convert_fusion.7
  77.2 77.6 %all-gather.9.cloned.1.call-done = bf16[4096,1024]{1,0:T(8,128)(2,1)} async-done(((bf16[512,1024]{1,0:T(8,128)(2,1)}), bf16[4096,1024]{1,0:T(8,128)(2,1)}) %all-gather.9.cloned.1.call-update) | async-done | bytes 8388624 | tf_op jit(solution)/shard_map/all_gather | solution.py:84
  154.9 0.0 copy-done
  154.9 11.2 %convolution_convert_fusion.5 = bf16[768,1024]{1,0:T(8,128)(2,1)S(1)} fusion(bf16[4096,1024]{1,0:T(8,128)(2,1)} %all-gather.9.cloned.1.call-done, bf16[768,4096]{1,0:T(8,128)(2,1)} %param.7, f32[4096]{0:T(1024)S(1)} %convert_element_type.81, f32[768]{0:T(1024)S(1)} %add_rsqrt_fusion), kind=kOutput, calls=%fused_computation.38 | convolution fusion | flops 6455820288 | bytes 16272384 | tf_op jit(solution)/shard_map/dot_general | solution.py:90
  166.1 0.7 copy.40
  166.8 12.3 %fusion.47 = (f32[2,4,768]{2,1,0:T(4,128)}, f32[2,4,768,768]{2,3,1,0:T(8,128)}) fusion(bf16[768,2,128,1]{0,2,3,1:T(8,128)(2,1)} %bitcast.122, bf16[768,2,4,128]{0,3,2,1:T(8,128)(2,1)S(1)} %bitcast.113, pred[768,768]{0,1:T(8,128)(4,1)} %iota_compare_fusion), kind=kOutput, calls=%fused_computation.54 | convolution fusion | flops 1226834688 | bytes 21454848 | tf_op jit(solution)/shard_map/sub | solution.py:42
  179.1 8.0 %fusion.21 = bf16[2,128,4,768]{3,1,2,0:T(8,128)(2,1)S(1)} fusion(bf16[768,2,128,1]{0,2,3,1:T(8,128)(2,1)S(1)} %bitcast.115, f32[2,4,768,768]{2,3,1,0:T(8,128)} %get-tuple-element.15, f32[2,4,768]{2,1,0:T(4,128)} %get-tuple-element.14), kind=kOutput, calls=%fused_computation.35 | convolution fusion | flops 1218183168 | bytes 20865024 | tf_op jit(solution)/shard_map/jgst,tjd->sjgd/dot_general | solution.py:45
  187.0 0.0 copy-start.2
  187.1 49.9 %all-gather.11.cloned.1.call-done = bf16[4096,1024]{1,0:T(8,128)(2,1)} async-done(((bf16[512,1024]{1,0:T(8,128)(2,1)}), bf16[4096,1024]{1,0:T(8,128)(2,1)}) %all-gather.11.cloned.1.call-update) | async-done | bytes 8388624 | tf_op jit(solution)/shard_map/all_gather | solution.py:98
  236.9 12.2 %convolution_convert_fusion.1 = bf16[768,4096]{1,0:T(8,128)(2,1)} fusion(bf16[768,1024]{0,1:T(8,128)(2,1)S(1)} %bitcast.119, bf16[4096,1024]{1,0:T(8,128)(2,1)} %all-gather.11.cloned.1.call-done), kind=kOutput, calls=%fused_computation.26 | convolution fusion | flops 6445596672 | bytes 16252928 | tf_op jit(solution)/shard_map/dot_general | solution.py:96
  249.1 0.0 copy-done.2
  249.1 0.0 reduce-scatter.3.cloned.1.call-update
  249.1 0.0 reduce-scatter.5.cloned.1.call-start
  249.2 12.3 %convolution_convert_fusion.4 = bf16[768,1024]{1,0:T(8,128)(2,1)} fusion(bf16[768,4096]{1,0:T(8,128)(2,1)} %param.13, bf16[4096,1024]{1,0:T(8,128)(2,1)} %all-gather.11.cloned.1.call-done), kind=kOutput, calls=%fused_computation.37 | convolution fusion | flops 6443237376 | bytes 16252928 | tf_op jit(solution)/shard_map/dot_general | solution.py:109
  261.5 1.8 copy.41
  263.3 8.2 %fusion.48 = f32[2,768,768,4]{2,1,3,0:T(8,128)} fusion(bf16[768,2,128,1]{0,2,3,1:T(8,128)(2,1)S(1)} %bitcast.116, bf16[768,2,4,128]{0,3,2,1:T(8,128)(2,1)S(1)} %bitcast.111), kind=kOutput, calls=%fused_computation.55 | convolution fusion | flops 1207959552 | bytes 20840448 | tf_op jit(solution)/shard_map/sjgd,tjd->jgst/dot_general | solution.py:56
  271.5 27.3 %fusion.24 = bf16[2,128,4,768]{3,1,2,0:T(8,128)(2,1)} fusion(bf16[768,2,128,1]{0,2,3,1:T(8,128)(2,1)} %bitcast.123, f32[2,768,768,4]{2,1,3,0:T(8,128)} %fusion.48, f32[2,4,768,768]{2,3,1,0:T(8,128)} %get-tuple-element.15, f32[2,4,768]{2,1,0:T(4,128)} %get-tuple-element.14), kind=kOutput, calls=%fused_computation.36 | convolution fusion | flops 1241783040 | bytes 39739392 | tf_op jit(solution)/shard_map/jgst,tjd->sjgd/dot_general | solution.py:61
  298.8 0.0 copy-done.6
  298.8 26.5 %fusion.29 = bf16[2,128,768]{2,1,0:T(8,128)(2,1)} fusion(bf16[768,2,4,128]{0,3,2,1:T(8,128)(2,1)S(1)} %bitcast.114, f32[2,768,768,4]{2,1,3,0:T(8,128)} %fusion.48, f32[2,4,768,768]{2,3,1,0:T(8,128)} %get-tuple-element.15, f32[2,4,768]{2,1,0:T(4,128)S(1)} %copy-done.6), kind=kOutput, calls=%fused_computation.41 | convolution fusion | flops 1241193216 | bytes 39739392 | tf_op jit(solution)/shard_map/jgst,sjgd->tjd/dot_general | solution.py:64
  325.3 0.0 copy-start.1
  325.3 9.6 %fusion.30 = bf16[2,128,768]{2,1,0:T(8,128)(2,1)S(1)} fusion(bf16[768,2,4,128]{0,3,2,1:T(8,128)(2,1)S(1)} %bitcast.112, f32[2,4,768,768]{2,3,1,0:T(8,128)} %get-tuple-element.15, f32[2,4,768]{2,1,0:T(4,128)S(1)} %copy-done.6), kind=kOutput, calls=%fused_computation.42 | convolution fusion | flops 1217593344 | bytes 20865024 | tf_op jit(solution)/shard_map/jgst,sjgd->tjd/dot_general | solution.py:53
  334.9 0.0 slice-start
  334.9 0.0 copy-start.5
  334.9 0.0 copy-done.1
  334.9 0.0 slice-start.1
  334.9 5.1 convolution_convert_fusion.2
  340.0 0.0 slice-start.2
  340.0 0.0 copy-start.3
  340.0 0.0 slice-done
  340.0 0.0 copy-done.5
  340.1 0.0 slice-start.3
  340.1 2.1 convolution_convert_fusion.3
  342.2 0.0 slice-done.2
  342.2 0.5 copy-done.3
  342.7 0.7 slice-done.3
  343.4 9.0 %convert_bitcast_fusion = bf16[4096,1024]{0,1:T(8,128)(2,1)} fusion(bf16[768,1024]{0,1:T(8,128)(2,1)S(1)} %bitcast.120, bf16[768,4096]{1,0:T(8,128)(2,1)S(1)} %bitcast.118), kind=kOutput, calls=%fused_computation.21 | convolution fusion | flops 6446645248 | bytes 16252928 | tf_op jit(solution)/shard_map/dot_general | solution.py:75
  352.3 9.1 %convolution_convert_fusion = bf16[4096,1024]{0,1:T(8,128)(2,1)} fusion(bf16[768,1024]{0,1:T(8,128)(2,1)S(1)} %bitcast.121, bf16[768,4096]{1,0:T(8,128)(2,1)S(1)} %bitcast.110, f32[4096]{0:T(1024)S(1)} %convert_element_type.81, f32[768]{0:T(1024)S(1)} %copy-done.1), kind=kOutput, calls=%fused_computation.25 | convolution fusion | flops 6459228160 | bytes 16272384 | tf_op jit(solution)/shard_map/dot_general | solution.py:75
  361.5 13.8 %pad_maximum_fusion = bf16[4096,2560]{0,1:T(8,128)(2,1)} fusion(bf16[4096,1024]{0,1:T(8,128)(2,1)} %convert_bitcast_fusion, bf16[4096,256]{0,1:T(8,128)(2,1)S(1)} %convolution_convert_fusion.2, bf16[4096,256]{0,1:T(8,128)(2,1)S(1)} %convolution_convert_fusion.3, bf16[4096,1024]{0,1:T(8,128)(2,1)} %convolution_convert_fusion), kind=kLoop, calls=%fused_computation.2 | loop fusion | flops 83886080 | bytes 41943040 | tf_op jit(solution)/shard_map/concatenate | solution.py:122
  375.3 0.0 reduce-scatter.5.cloned.1.call-update
  375.3 0.0 reduce-scatter.3.cloned.1.call-done
  375.4 3.7 add_convert_fusion
  379.1 203.8 %reduce-scatter.5.cloned.1.call-done = bf16[512,2560]{0,1:T(8,128)(2,1)} async-done(((bf16[4096,2560]{0,1:T(8,128)(2,1)}), bf16[512,2560]{0,1:T(8,128)(2,1)}) %reduce-scatter.5.cloned.1.call-update) | async-done | bytes 2621456 | tf_op jit(solution)/shard_map/reduce_scatter | solution.py:121
  582.9 1.1 fusion.46
  584.1 1.0 copy.24
  585.1 1.0 copy.23
  586.1 3.5 fusion.45
  589.5 2.9 copy.25
  592.4 1.8 copy.22
  (7 shorter events, 0.0 us)
Async XLA Ops:
  7.2 34.3 %all-gather.7.cloned.1.call-start = ((), (), s32[]{:S(2)}) async-start(), calls=%async_computation.3 | async-start | bytes 2359296 | tf_op jit(solution)/shard_map/all_gather | solution.py:85
  7.9 63.8 %all-gather.5.cloned.1.call-start = ((), (), s32[]{:S(2)}) async-start(), calls=%async_computation.2 | async-start | bytes 2359296 | tf_op jit(solution)/shard_map/all_gather | solution.py:86
  8.6 146.2 %all-gather.9.cloned.1.call-start = ((), (), s32[]{:S(2)}) async-start(), calls=%async_computation.4 | async-start | bytes 9437184 | tf_op jit(solution)/shard_map/all_gather | solution.py:84
  9.4 227.5 %all-gather.11.cloned.1.call-start = ((), (), s32[]{:S(2)}) async-start(), calls=%async_computation.5 | async-start | bytes 9437184 | tf_op jit(solution)/shard_map/all_gather | solution.py:98
  10.0 365.4 %reduce-scatter.3.cloned.1.call-start = ((), (), s32[]{:S(2)}) async-start(), calls=%async_computation.6 | async-start | bytes 7864320 | tf_op jit(solution)/shard_map/reduce_scatter | solution.py:102
  15.8 139.1 %copy-start = (f32[768]{0:T(1024)}, f32[768]{0:T(1024)S(1)}, u32[]{:S(2)}) copy-start(f32[768]{0:T(1024)S(1)} %add_rsqrt_fusion) | copy-start | bytes 9220
  187.0 62.1 %copy-start.2 = (bf16[2,128,4,768]{3,1,2,0:T(8,128)(2,1)}, bf16[2,128,4,768]{3,1,2,0:T(8,128)(2,1)S(1)}, u32[]{:S(2)}) copy-start(bf16[2,128,4,768]{3,1,2,0:T(8,128)(2,1)S(1)} %fusion.21) | copy-start | bytes 4718596
  249.1 333.8 %reduce-scatter.5.cloned.1.call-start = ((), (), s32[]{:S(2)}) async-start(), calls=%async_computation.7 | async-start | bytes 23592960 | tf_op jit(solution)/shard_map/reduce_scatter | solution.py:121
  271.5 27.3 %copy-start.6 = (f32[2,4,768]{2,1,0:T(4,128)S(1)}, f32[2,4,768]{2,1,0:T(4,128)}, u32[]{:S(2)}) copy-start(f32[2,4,768]{2,1,0:T(4,128)} %get-tuple-element.14) | copy-start | bytes 73732
  325.3 9.6 %copy-start.1 = (f32[768]{0:T(1024)S(1)}, f32[768]{0:T(1024)}, u32[]{:S(2)}) copy-start(f32[768]{0:T(1024)} %copy-done) | copy-start | bytes 9220
  334.9 5.1 slice-start
  334.9 5.1 copy-start.5
  334.9 5.1 slice-start.1
  340.0 2.2 slice-start.2
  340.0 2.7 copy-start.3
  340.1 3.3 slice-start.3
  343.3 9.0 %copy-start.4 = (bf16[2,128,4,768]{3,1,2,0:T(8,128)(2,1)S(1)}, bf16[2,128,4,768]{3,1,2,0:T(8,128)(2,1)}, u32[]{:S(2)}) copy-start(bf16[2,128,4,768]{3,1,2,0:T(8,128)(2,1)} %fusion.24) | copy-start | bytes 4718596
Sparse Core Ops, SparseCore 0:
  9.6 31.7 all-gather.6
  43.0 28.5 all-gather.4
  73.3 81.5 all-gather.8
  156.3 80.5 all-gather.10
  249.3 68.7 reduce-scatter.2
  375.5 207.4 reduce-scatter.4
where the time goes:
time: 607 us; the launch traced here: 601 us
  waiting for transfers between devices  384 us (63%)
  matrix products  165 us (27%)
  other arithmetic  23.3 us (4%)
  local copies, waits for them, and re-layouts  15 us (2%)
  between operations  14.8 us (2%)
    reduce_scatter x1, waiting for transfers between devices, shards(): lax.psum_scatter(jnp.concatenate([jnp.concatenate([row_product(normed, gr...  204 us
    all_gather x1, waiting for transfers between devices, shards(): lax.all_gather(w_query, 'wide', axis=0, tiled=True)  77.6 us
    all_gather x1, waiting for transfers between devices, shards(): lax.all_gather(w_out, 'wide', axis=0, tiled=True)  49.9 us
    dot_general x1, matrix products, attend_backward(): jnp.einsum('jgst,tjd->sjgd', grad_scores, key_split, preferred_element_ty...  27.3 us
    dot_general x1, matrix products, attend_backward(): jnp.einsum('jgst,sjgd->tjd', grad_scores, query_split, preferred_element_...  26.5 us
    all_gather x1, waiting for transfers between devices, shards(): lax.all_gather(w_key, 'wide', axis=0, tiled=True)  25.6 us
    dot_general x4, matrix products, row_product(): lax.dot_general(left_rows, right, (((0,), (0,)), ((), ())), preferred_ele...  25.3 us
    all_gather x1, waiting for transfers between devices, shards(): lax.all_gather(w_value, 'wide', axis=0, tiled=True)  23.9 us
  transfers between devices with their start and end apart: 6, of which 5 were waited for; matrix products, arithmetic and copies ran while one was open for 30% of the time, Pallas kernels for 0%

commit v1 on v0

v1 whole, which is shorter than its diff:
```python
import functools
import jax
import jax.numpy as jnp
from jax import lax
from jax.experimental import pallas as pl
from jax.experimental.pallas import tpu as pltpu
from jax.sharding import PartitionSpec as P

HEAD_DIM = 128
BLOCK = 256
EPSILON = 1e-05
MASKED = -1e30
F32 = jnp.float32
BF16 = jnp.bfloat16


def normalize(rows, gain):
    values32 = rows.astype(F32)
    mean_square = jnp.mean(values32 * values32, axis=-1, keepdims=True)
    return (values32 * lax.rsqrt(mean_square + EPSILON) * gain.astype(F32)).astype(BF16)


def nt(a, b):
    return lax.dot_general(a, b, (((1,), (1,)), ((), ())), preferred_element_type=F32)


def nn(a, b):
    return lax.dot_general(a, b, (((1,), (0,)), ((), ())), preferred_element_type=F32)


def row_product(a, b):
    return lax.dot_general(a, b, (((0,), (0,)), ((), ())), preferred_element_type=F32)


def masked_scores(keys, queries, start, size):
    scores = nt(keys, queries) * HEAD_DIM ** (-0.5)
    key_at = lax.broadcasted_iota(jnp.int32, (size, size), 0)
    query_at = lax.broadcasted_iota(jnp.int32, (size, size), 1)
    last = jnp.where(key_at <= query_at, scores[start:], MASKED)
    if start == 0:
        return last
    return jnp.concatenate([scores[:start], last], axis=0)


def forward_kernel(members, block, qkv_ref, mixed_ref, lse_ref):
    length = qkv_ref.shape[0]
    width = HEAD_DIM
    key_col, value_col = members * width, (members + 1) * width
    values_t = qkv_ref[:, value_col : value_col + width].T
    for h in range(members):
        for start in range(0, length, block):
            stop = start + block
            queries = qkv_ref[start:stop, h * width : (h + 1) * width]
            keys = qkv_ref[:stop, key_col : key_col + width]
            scores = masked_scores(keys, queries, start, block)
            highest = jnp.max(scores, axis=0, keepdims=True)
            exponent = jnp.exp(scores - highest)
            total = jnp.sum(exponent, axis=0, keepdims=True)
            rounded = (exponent * (1.0 / total)).astype(BF16)
            mixed_t = nn(values_t[:, :stop], rounded)
            mixed_ref[start:stop, h * width : (h + 1) * width] = mixed_t.T.astype(BF16)
            lse_ref[h : h + 1, start:stop] = highest + jnp.log(total)


def attend_forward(qkv, members, block):
    length = qkv.shape[0]
    width = HEAD_DIM
    vmem = pl.BlockSpec(memory_space=pltpu.VMEM)
    return pl.pallas_call(
        functools.partial(forward_kernel, members, block),
        out_shape=(
            jax.ShapeDtypeStruct((length, members * width), BF16),
            jax.ShapeDtypeStruct((members, length), F32),
        ),
        in_specs=[vmem],
        out_specs=(vmem, vmem),
        compiler_params=pltpu.CompilerParams(vmem_limit_bytes=40 * 2**20),
        cost_estimate=pl.CostEstimate(
            flops=8 * members * length * length * width,
            bytes_accessed=8 * length * members * width,
            transcendentals=members * length * length,
        ),
        name="attend_forward",
    )(qkv)


def backward_kernel(members, block, qkv_ref, grad_ref, lse_ref, out_ref, gk_ref, gv_ref):
    length = qkv_ref.shape[0]
    width = HEAD_DIM
    key_col, value_col = members * width, (members + 1) * width
    keys_t = qkv_ref[:, key_col : key_col + width].T
    gk_ref[...] = jnp.zeros_like(gk_ref)
    gv_ref[...] = jnp.zeros_like(gv_ref)
    for h in range(members):
        cols = slice(h * width, (h + 1) * width)
        for start in range(0, length, block):
            stop = start + block
            queries = qkv_ref[start:stop, cols]
            grads = grad_ref[start:stop, cols]
            keys = qkv_ref[:stop, key_col : key_col + width]
            values = qkv_ref[:stop, value_col : value_col + width]
            scores = masked_scores(keys, queries, start, block)
            probs = jnp.exp(scores - lse_ref[h : h + 1, start:stop])
            grad_probs = nt(values, grads)
            gv_ref[:stop, :] += nn(probs.astype(BF16), grads)
            inner = jnp.sum(grad_probs * probs, axis=0, keepdims=True)
            grad_scores = (probs * (grad_probs - inner) * width ** (-0.5)).astype(BF16)
            gk_ref[:stop, :] += nn(grad_scores, queries)
            out_ref[start:stop, cols] = nn(keys_t[:, :stop], grad_scores).T.astype(BF16)
    out_ref[:, key_col : key_col + width] = gk_ref[...].astype(BF16)
    out_ref[:, value_col : value_col + width] = gv_ref[...].astype(BF16)


def attend_backward(qkv, grad_mixed, lse, members, block):
    length = qkv.shape[0]
    width = HEAD_DIM
    vmem = pl.BlockSpec(memory_space=pltpu.VMEM)
    return pl.pallas_call(
        functools.partial(backward_kernel, members, block),
        out_shape=jax.ShapeDtypeStruct(qkv.shape, BF16),
        in_specs=[vmem, vmem, vmem],
        out_specs=vmem,
        scratch_shapes=[pltpu.VMEM((length, width), F32), pltpu.VMEM((length, width), F32)],
        compiler_params=pltpu.CompilerParams(vmem_limit_bytes=40 * 2**20),
        cost_estimate=pl.CostEstimate(
            flops=20 * members * length * length * width,
            bytes_accessed=8 * length * members * width,
            transcendentals=members * length * length,
        ),
        name="attend_backward",
    )(qkv, grad_mixed, lse)


def take(blocks, at):
    return lax.dynamic_index_in_dim(blocks, at, 0, keepdims=False)


class Order:
    def __init__(self):
        self.last = None

    def __call__(self, compute, *operands):
        if self.last is not None:
            tied = lax.optimization_barrier((self.last, *operands))
            operands = tied[1:]
        result = compute(*operands)
        self.last = jax.tree.leaves(result)[0]
        return result

    def after(self, operand):
        return operand if self.last is None else lax.optimization_barrier((self.last, operand))[1]


class LineSum:
    def __init__(self, order, chips):
        self.order, self.chips = order, chips
        self.chip = lax.axis_index("wide") // 2
        self.up = self.down = None

    def swap(self, send):
        pairs = [(w, w ^ 1) for w in range(2 * self.chips)]
        self.received = lax.ppermute(send, "wide", pairs)

    def add_cores(self, keep):
        def add(keep, received):
            return (keep.astype(F32) + received.astype(F32)).astype(BF16)

        both = self.order(add, keep, self.received)
        self.both = both.reshape(self.chips, -1, both.shape[-1])

    def hop(self, t):
        chips, chip, far = self.chips, self.chip, self.chips - t

        def messages(both, *arrived):
            up = take(both, jnp.minimum(chip + far, chips - 1))
            down = take(both, jnp.maximum(chip - far, 0))
            if arrived:
                up = (up.astype(F32) + arrived[0].astype(F32)).astype(BF16)
                down = (down.astype(F32) + arrived[1].astype(F32)).astype(BF16)
            return up, down

        arrived = () if self.up is None else (self.up, self.down)
        up, down = self.order(messages, self.both, *arrived)
        self.up = lax.ppermute(up, "wide", [(w, w + 2) for w in range(2 * t)])
        self.down = lax.ppermute(down, "wide", [(w, w - 2) for w in range(2 * far, 2 * chips)])

    def total(self):
        def add(both, *arrived):
            result = take(both, self.chip).astype(F32)
            for part in arrived:
                result = result + part.astype(F32)
            return result

        arrived = () if self.up is None else (self.up, self.down)
        return self.order(add, self.both, *arrived)


def shards(wide, activations, gain, w_query, w_key, w_value, w_out, cotangent):
    width = HEAD_DIM
    length, features = activations.shape
    chips = wide // 2
    groups = w_key.shape[1] // width
    members = w_query.shape[1] // w_key.shape[1]
    block = BLOCK if length % BLOCK == 0 else length
    span = members * width
    rows = features // wide
    core = lax.axis_index("wide") % 2
    order = Order()

    def gathered(piece):
        return lax.all_gather(piece, "wide", axis=0, tiled=True)

    def columns(g):
        cols = slice(g * span, (g + 1) * span)
        heads = slice(g * width, (g + 1) * width)
        return jnp.concatenate([w_query[:, cols], w_key[:, heads], w_value[:, heads]], axis=1)

    def out_columns(g):
        return w_out[:, g * span : (g + 1) * span]

    def halves(array):
        split = array.reshape(length, chips, 2, rows)
        own = lax.dynamic_index_in_dim(split, core, 2, keepdims=False)
        other = lax.dynamic_index_in_dim(split, 1 - core, 2, keepdims=False)
        return own.reshape(length, chips * rows), other.reshape(length, chips * rows)

    def product(a, b):
        return jnp.dot(a, b, preferred_element_type=F32).astype(BF16)

    def term(a, b):
        return row_product(a, b).astype(BF16)

    weights = [None] * groups
    out_weights = [None] * groups
    weights[0] = gathered(columns(0))
    normed = order(normalize, activations, gain)
    out_weights[0] = gathered(order.after(out_columns(0)))
    normed_own, normed_other = order(halves, normed)
    cotangent_own, cotangent_other = order(halves, cotangent)

    projected = None
    pending = []

    def advance():
        for steps in list(pending):
            if next(steps, None) is None:
                pending.remove(steps)

    def steps_of(line, results):
        for t in range(1, chips):
            line.hop(t)
            yield True
        results.append(line.total())
        yield True

    def start(own, other, grads, results):
        line = LineSum(order, chips)
        line.swap(order(term, other, grads))
        line.add_cores(order(term, own, grads))
        steps = steps_of(line, results)
        next(steps)
        pending.append(steps)

    sums_out, sums_qkv = [], []
    for g in range(groups):
        qkv = order(product, normed, weights[g])
        if g + 1 < groups:
            weights[g + 1] = gathered(order.after(columns(g + 1)))
        mixed, lse = order(lambda a: attend_forward(a, members, block), qkv)
        start(cotangent_own, cotangent_other, mixed, sums_out)
        advance()
        grad_mixed = order(product, cotangent, out_weights[g])
        if g + 1 < groups:
            out_weights[g + 1] = gathered(order.after(out_columns(g + 1)))
        advance()
        if g + 1 == groups:

            def project(mixed, out_weights, *partial):
                result = nt(mixed, out_weights)
                for part in partial:
                    result = result + part
                return result.astype(BF16)

            partial = () if projected is None else (projected,)
            projected = order(project, mixed, out_weights[g], *partial)
            summed = lax.psum_scatter(projected, "narrow", scatter_dimension=1, tiled=True)
        grad_qkv = order(
            lambda a, b, c: attend_backward(a, b, c, members, block), qkv, grad_mixed, lse
        )
        advance()
        start(normed_own, normed_other, grad_qkv, sums_qkv)
        if g + 1 < groups:
            part = order(nt, mixed, out_weights[g])
            projected = part if projected is None else projected + part
            advance()
            advance()
    while pending:
        advance()

    share = summed.shape[1]
    own_columns = lax.dynamic_slice_in_dim(
        activations, lax.axis_index("narrow") * share, share, 1
    )
    outputs = (own_columns.astype(F32) + summed.astype(F32)).astype(BF16)

    def joined(pieces):
        return pieces[0] if len(pieces) == 1 else jnp.concatenate(pieces, axis=1)

    grad_query = joined([s[:, :span] for s in sums_qkv])
    grad_key = joined([s[:, span : span + width] for s in sums_qkv])
    grad_value = joined([s[:, span + width :] for s in sums_qkv])
    grad_out = joined(sums_out)
    return (outputs, grad_query, grad_key, grad_value, grad_out)


def solution(mesh):
    return jax.shard_map(
        functools.partial(shards, mesh.shape["wide"]),
        mesh=mesh,
        in_specs=(
            P("wide", None),
            P(),
            P("wide", "narrow"),
            P("wide", "narrow"),
            P("wide", "narrow"),
            P("wide", "narrow"),
            P("wide", None),
        ),
        out_specs=(
            P("wide", "narrow"),
            P("wide", "narrow"),
            P("wide", "narrow"),
            P("wide", "narrow"),
            P("wide", "narrow"),
        ),
        check_vma=False,
    )
```

time: 607 us -> 487 us (0.80)
  waiting for transfers between devices: 384 us -> 214 us
  matrix products: 165 us -> 72 us
  starting transfers between devices: 0.23 us -> 75.7 us
  local copies, waits for them, and re-layouts: 15 us -> 41.5 us
  Pallas kernels: 0 us -> 22.4 us
  other arithmetic: 23.3 us -> 40.2 us
    reduce_scatter x2 -> x1, waiting for transfers between devices: 204 us -> 0.01 us  [shards(): lax.psum_scatter(projected, 'narrow', scatter_dimension=1, tiled=True)]
    ppermute x0 -> x28, waiting for transfers between devices: none -> 186 us  [the longest x12 150 us: hop(): self.up = lax.ppermute(up, 'wide', [(w, w + 2) for w in range(2 * t)])]
    all_gather x4, waiting for transfers between devices: 177 us -> 27.4 us  [gathered(): return lax.all_gather(piece, 'wide', axis=0, tiled=True)]
    dot_general x14, matrix products: 152 us -> 72 us  [the longest x4 33.1 us: product(): return jnp.dot(a, b, preferred_element_type=F32).astype(BF16)]
    ppermute x0 -> x28, starting transfers between devices: none -> 75.3 us  [the longest x12 62.5 us: hop(): self.up = lax.ppermute(up, 'wide', [(w, w + 2) for w in range(2 * t)])]
    pallas_call x0 -> x4, Pallas kernels: none -> 22.4 us  [the longest x2 12.1 us: attend_backward(): pl.pallas_call(functools.partial(backward_kernel, members, block), out_sh...]
    convert_element_type x2 -> x15, other arithmetic: 4.41 us -> 21.4 us  [the longest x8 8.93 us: messages(): down = (down.astype(F32) + arrived[1].astype(F32)).astype(BF16)]
    sub x1 -> x0, matrix products: 12.3 us -> none  [attend_forward(): exponent = jnp.exp(scores - highest)]
  transfers between devices with their start and end apart: 6 -> 33, of which waited for: 5 -> 20; matrix products, arithmetic and copies ran while one was open for 30% -> 27% of each run, Pallas kernels for 0% -> 5%
where the time goes in v1:
time: 487 us; the launch traced here: 480 us
  waiting for transfers between devices  214 us (44%)
  starting transfers between devices  75.7 us (16%)
  matrix products  72 us (15%)
  local copies, waits for them, and re-layouts  41.5 us (9%)
  other arithmetic  40.2 us (8%)
  Pallas kernels  22.4 us (5%)
  between operations  14.7 us (3%)
    ppermute x12, waiting for transfers between devices, hop(): self.up = lax.ppermute(up, 'wide', [(w, w + 2) for w in range(2 * t)])  150 us
    ppermute x12, starting transfers between devices, hop(): self.up = lax.ppermute(up, 'wide', [(w, w + 2) for w in range(2 * t)])  62.5 us
    dot_general x4, matrix products, product(): return jnp.dot(a, b, preferred_element_type=F32).astype(BF16)  33.1 us
    ppermute x12, waiting for transfers between devices, hop(): lax.ppermute(down, 'wide', [(w, w - 2) for w in range(2 * far, 2 * chips)])  29.7 us
    all_gather x4, waiting for transfers between devices, gathered(): return lax.all_gather(piece, 'wide', axis=0, tiled=True)  27.4 us
    dot_general x8, matrix products, row_product(): lax.dot_general(a, b, (((0,), (0,)), ((), ())), preferred_element_type=F32)  21.7 us
    dot_general x2, matrix products, nt(): lax.dot_general(a, b, (((1,), (1,)), ((), ())), preferred_element_type=F32)  17.2 us
    unnamed x43, local copies, waits for them, and re-layouts  14 us
  transfers between devices with their start and end apart: 33, of which 20 were waited for; matrix products, arithmetic and copies ran while one was open for 27% of the time, Pallas kernels for 5%

profile of v1, /device:TPU:0, one launch (start us, length us, event | category | flops | bytes accessed | tf_op | source)
XLA Modules:
  0.0 480.4 jit_solution(9557772494141027451)
XLA Ops:
  10.7 8.7 %copy.12 = bf16[768,4096]{0,1:T(8,128)(2,1)} copy(bf16[768,4096]{1,0:T(8,128)(2,1)} %param.7) | data formatting | bytes 12582912 | tf_op args[0]
  19.4 4.8 fusion
  25.3 4.0 fusion.2
  29.3 5.9 %constant_dynamic-slice_fusion = (bf16[768,4,1,512]{0,3,2,1:T(8,128)(2,1)}, bf16[768,4,1,512]{0,3,2,1:T(8,128)(2,1)}) fusion(bf16[768,4,2,512]{0,3,2,1:T(8,128)(2,1)} %bitcast.114, s32[]{:T(128)S(6)} %select_n.67, s32[]{:T(128)S(6)} %select_n.66), kind=kLoop, calls=%fused_computation.77 | loop fusion | bytes 12582920 | tf_op jit(solution)/shard_map/jit(dynamic_index_in_dim)/dynamic_slice | solution.py:224
  35.3 8.7 %copy.13 = bf16[768,4096]{0,1:T(8,128)(2,1)} copy(bf16[768,4096]{1,0:T(8,128)(2,1)} %param.13) | data formatting | bytes 12582912 | tf_op jit(solution)/shard_map/optimization_barrier | solution.py:144
  44.9 6.0 %constant_dynamic-slice_fusion.1 = (bf16[768,4,1,512]{0,3,2,1:T(8,128)(2,1)}, bf16[768,4,1,512]{0,3,2,1:T(8,128)(2,1)}) fusion(bf16[768,4,2,512]{0,3,2,1:T(8,128)(2,1)} %bitcast.115, s32[]{:T(128)S(6)} %select_n.67, s32[]{:T(128)S(6)} %select_n.66), kind=kLoop, calls=%fused_computation.78 | loop fusion | bytes 12582920 | tf_op jit(solution)/shard_map/jit(dynamic_index_in_dim)/dynamic_slice | solution.py:224
  50.9 27.3 %all-gather.5.cloned.1.call-done = bf16[4096,768]{1,0:T(8,128)(2,1)} async-done(((bf16[512,768]{1,0:T(8,128)(2,1)}), bf16[4096,768]{1,0:T(8,128)(2,1)}) %all-gather.5.cloned.1.call-update) | async-done | bytes 6291472 | tf_op jit(solution)/shard_map/all_gather | solution.py:211
  78.2 9.0 %convolution_convert_fusion.9.qkv_ref = bf16[768,768]{1,0:T(8,128)(2,1)S(1)} fusion(bf16[768,4096]{0,1:T(8,128)(2,1)} %fusion.2, bf16[4096,768]{1,0:T(8,128)(2,1)} %all-gather.5.cloned.1.call-done), kind=kOutput, calls=%fused_computation.42 | convolution fusion | flops 4832428032 | bytes 13762560 | tf_op jit(solution)/shard_map/dot_general | solution.py:228
  87.5 5.2 %attend_forward.2 = (bf16[768,512]{1,0:T(8,128)(2,1)S(1)}, f32[4,768]{1,0:T(4,128)S(1)}) custom-call(bf16[768,768]{1,0:T(8,128)(2,1)S(1)} %convolution_convert_fusion.9.qkv_ref), custom_call_target="tpu_custom_call" | custom-call | flops 2415919104 | bytes 3145728 | tf_op jit(solution)/shard_map/attend_forward/pallas_call | solution.py:69
  92.7 3.1 convolution_convert_fusion.7
  96.1 3.7 convolution_convert_fusion.6
  100.5 2.2 add_convert_fusion.4
  107.0 22.8 %collective-permute-done.1 = bf16[512,512]{1,0:T(8,128)(2,1)S(1)} collective-permute-done((bf16[512,512]{1,0:T(8,128)(2,1)}, bf16[512,512]{1,0:T(8,128)(2,1)S(1)}, u32[]{:S(2)}, u32[]{:S(2)}) %collective-permute-start.1) | collective-permute-done | bytes 524320 | tf_op jit(solution)/shard_map/ppermute | solution.py:184
  129.8 2.3 fusion.21
  132.1 4.3 collective-permute-start.3
  137.3 7.4 %convolution_convert_fusion.11.grad_ref = bf16[768,512]{1,0:T(8,128)(2,1)S(1)} fusion(bf16[768,4096]{1,0:T(8,128)(2,1)} %param.13, bf16[4096,512]{1,0:T(8,128)(2,1)} %all-gather.7.cloned.1.call-done), kind=kOutput, calls=%fused_computation.44 | convolution fusion | flops 3221618688 | bytes 11272192 | tf_op jit(solution)/shard_map/dot_general | solution.py:228
  144.7 4.3 collective-permute-done.3
  149.3 15.8 %collective-permute-start.5 = (bf16[512,512]{1,0:T(8,128)(2,1)S(1)}, bf16[512,512]{1,0:T(8,128)(2,1)S(1)}, u32[]{:S(2)}, u32[]{:S(2)}) collective-permute-start(bf16[512,512]{1,0:T(8,128)(2,1)S(1)} %get-tuple-element.216), channel_id=1, source_target_pairs={{0,8},{4,12},{8,16},{12,20},{16,24},{20,28},{1,9},{5,13},{9,17},{1... | collective-permute-start | bytes 1572872 | tf_op jit(solution)/shard_map/ppermute | solution.py:184
  165.2 2.0 collective-permute-start.6
  167.1 6.1 %attend_backward.2 = bf16[768,768]{1,0:T(8,128)(2,1)S(1)} custom-call(bf16[768,768]{1,0:T(8,128)(2,1)S(1)} %convolution_convert_fusion.9.qkv_ref, bf16[768,512]{1,0:T(8,128)(2,1)S(1)} %convolution_convert_fusion.11.grad_ref, f32[4,768]{1,0:T(4,128)S(1)} %get-tuple-element.123.lse_ref), custom_call_target="tpu_custom_call" | custom-call | flops 6039797760 | bytes 3145728 | tf_op jit(solution)/shard_map/attend_backward/pallas_call | solution.py:118
  173.2 12.5 %collective-permute-done.5 = bf16[512,512]{1,0:T(8,128)(2,1)S(1)} collective-permute-done((bf16[512,512]{1,0:T(8,128)(2,1)S(1)}, bf16[512,512]{1,0:T(8,128)(2,1)S(1)}, u32[]{:S(2)}, u32[]{:S(2)}) %collective-permute-start.5) | collective-permute-done | bytes 524320 | tf_op jit(solution)/shard_map/ppermute | solution.py:184
  185.7 16.5 %collective-permute-done.6 = bf16[512,512]{1,0:T(8,128)(2,1)S(1)} collective-permute-done((bf16[512,512]{1,0:T(8,128)(2,1)S(1)}, bf16[512,512]{1,0:T(8,128)(2,1)S(1)}, u32[]{:S(2)}, u32[]{:S(2)}) %collective-permute-start.6) | collective-permute-done | bytes 524320 | tf_op jit(solution)/shard_map/ppermute | solution.py:185
  203.4 2.8 convolution_convert_fusion.3
  206.3 2.8 convolution_convert_fusion.2
  209.1 2.9 collective-permute-done.7
  215.6 3.0 collective-permute-start.8
  219.5 9.0 %fusion.29 = f32[768,4096]{1,0:T(8,128)} fusion(bf16[768,512]{1,0:T(8,128)(2,1)S(1)} %get-tuple-element.135, bf16[4096,512]{1,0:T(8,128)(2,1)} %all-gather.7.cloned.1.call-done), kind=kOutput, calls=%fused_computation.88 | convolution fusion | flops 3221225472 | bytes 17563648 | tf_op jit(solution)/shard_map/dot_general | solution.py:24
  228.4 18.1 %collective-permute-done.8 = bf16[512,768]{1,0:T(8,128)(2,1)S(1)} collective-permute-done((bf16[512,768]{1,0:T(8,128)(2,1)}, bf16[512,768]{1,0:T(8,128)(2,1)S(1)}, u32[]{:S(2)}, u32[]{:S(2)}) %collective-permute-start.8) | collective-permute-done | bytes 786464 | tf_op jit(solution)/shard_map/ppermute | solution.py:184
  246.9 4.3 collective-permute-start.10
  252.2 32.7 %collective-permute-done.10 = bf16[512,768]{1,0:T(8,128)(2,1)S(1)} collective-permute-done((bf16[512,768]{1,0:T(8,128)(2,1)S(1)}, bf16[512,768]{1,0:T(8,128)(2,1)S(1)}, u32[]{:S(2)}, u32[]{:S(2)}) %collective-permute-start.10) | collective-permute-done | bytes 786464 | tf_op jit(solution)/shard_map/ppermute | solution.py:184
  285.4 9.1 %convolution_convert_fusion.8.qkv_ref = bf16[768,768]{1,0:T(8,128)(2,1)S(1)} fusion(bf16[768,4096]{0,1:T(8,128)(2,1)} %fusion.2, bf16[4096,768]{1,0:T(8,128)(2,1)} %all-gather.9.cloned.1.call-done), kind=kOutput, calls=%fused_computation.41 | convolution fusion | flops 4832428032 | bytes 13762560 | tf_op jit(solution)/shard_map/dot_general | solution.py:228
  294.5 5.2 %attend_forward.3 = (bf16[768,512]{1,0:T(8,128)(2,1)S(1)}, f32[4,768]{1,0:T(4,128)S(1)}) custom-call(bf16[768,768]{1,0:T(8,128)(2,1)S(1)} %convolution_convert_fusion.8.qkv_ref), custom_call_target="tpu_custom_call" | custom-call | flops 2415919104 | bytes 3145728 | tf_op jit(solution)/shard_map/attend_forward/pallas_call | solution.py:69
  299.7 1.8 convolution_convert_fusion.5
  301.5 4.4 collective-permute-start.13
  307.3 1.8 convolution_convert_fusion.4
  309.9 4.6 collective-permute-start.15
  315.2 8.6 %collective-permute-done.13 = bf16[512,768]{1,0:T(8,128)(2,1)S(1)} collective-permute-done((bf16[512,768]{1,0:T(8,128)(2,1)S(1)}, bf16[512,768]{1,0:T(8,128)(2,1)S(1)}, u32[]{:S(2)}, u32[]{:S(2)}) %collective-permute-start.13) | collective-permute-done | bytes 786464 | tf_op jit(solution)/shard_map/ppermute | solution.py:184
  323.8 3.8 collective-permute-done.14
  327.5 2.5 fusion.8
  330.1 4.5 collective-permute-done.15
  335.9 4.4 collective-permute-start.17
  341.2 7.6 %convolution_convert_fusion.10.grad_ref = bf16[768,512]{1,0:T(8,128)(2,1)S(1)} fusion(bf16[768,4096]{1,0:T(8,128)(2,1)} %param.13, bf16[4096,512]{1,0:T(8,128)(2,1)} %all-gather.11.cloned.1.call-done), kind=kOutput, calls=%fused_computation.43 | convolution fusion | flops 3221618688 | bytes 11272192 | tf_op jit(solution)/shard_map/dot_general | solution.py:228
  348.7 2.9 collective-permute-done.17
  352.4 2.1 fusion.14
  354.5 8.3 %add_convert_fusion = bf16[768,4096]{1,0:T(8,128)(2,1)} fusion(f32[768,4096]{1,0:T(8,128)} %fusion.29, bf16[768,512]{1,0:T(8,128)(2,1)S(1)} %get-tuple-element.166, bf16[4096,512]{1,0:T(8,128)(2,1)S(1)} %copy-done.20), kind=kOutput, calls=%fused_computation.5 | convolution fusion | flops 3227516928 | bytes 23855104 | tf_op jit(solution)/shard_map/dot_general | solution.py:24
  363.8 6.0 %collective-permute-start.19 = (bf16[512,512]{1,0:T(8,128)(2,1)S(1)}, bf16[512,512]{1,0:T(8,128)(2,1)S(1)}, u32[]{:S(2)}, u32[]{:S(2)}) collective-permute-start(bf16[512,512]{1,0:T(8,128)(2,1)S(1)} %copy-done.17), channel_id=1, source_target_pairs={{0,8},{4,12},{8,16},{12,20},{16,24},{20,28},{1,9},{5,13},{9,17},{1... | collective-permute-start | bytes 1572872 | tf_op jit(solution)/shard_map/ppermute | solution.py:184
  369.8 1.8 collective-permute-start.20
  371.6 6.1 %attend_backward.3 = bf16[768,768]{1,0:T(8,128)(2,1)S(1)} custom-call(bf16[768,768]{1,0:T(8,128)(2,1)S(1)} %convolution_convert_fusion.8.qkv_ref, bf16[768,512]{1,0:T(8,128)(2,1)S(1)} %convolution_convert_fusion.10.grad_ref, f32[4,768]{1,0:T(4,128)S(1)} %get-tuple-element.172.lse_ref), custom_call_target="tpu_custom_call" | custom-call | flops 6039797760 | bytes 3145728 | tf_op jit(solution)/shard_map/attend_backward/pallas_call | solution.py:118
  377.6 2.0 collective-permute-done.19
  379.6 4.4 collective-permute-done.20
  384.0 2.2 fusion.13
  386.2 2.8 convolution_convert_fusion.1
  389.1 2.8 convolution_convert_fusion
  392.0 2.8 collective-permute-done.21
  395.8 2.3 collective-permute-start.22
  398.9 16.3 %collective-permute-done.22 = bf16[512,768]{1,0:T(8,128)(2,1)S(1)} collective-permute-done((bf16[512,768]{1,0:T(8,128)(2,1)S(1)}, bf16[512,768]{1,0:T(8,128)(2,1)S(1)}, u32[]{:S(2)}, u32[]{:S(2)}) %collective-permute-start.22) | collective-permute-done | bytes 786464 | tf_op jit(solution)/shard_map/ppermute | solution.py:184
  415.6 4.4 collective-permute-start.24
  420.8 15.5 %collective-permute-done.24 = bf16[512,768]{1,0:T(8,128)(2,1)S(1)} collective-permute-done((bf16[512,768]{1,0:T(8,128)(2,1)S(1)}, bf16[512,768]{1,0:T(8,128)(2,1)S(1)}, u32[]{:S(2)}, u32[]{:S(2)}) %collective-permute-start.24) | collective-permute-done | bytes 786464 | tf_op jit(solution)/shard_map/ppermute | solution.py:184
  436.3 1.6 fusion.4
  437.9 7.5 %collective-permute-start.26 = (bf16[512,768]{1,0:T(8,128)(2,1)}, bf16[512,768]{1,0:T(8,128)(2,1)}, u32[]{:S(2)}, u32[]{:S(2)}) collective-permute-start(bf16[512,768]{1,0:T(8,128)(2,1)} %get-tuple-element.198), channel_id=1, source_target_pairs={{0,8},{4,12},{8,16},{12,20},{16,24},{20,28},{1,9},{5,13},{9,17},{1... | collective-permute-start | bytes 2359304 | tf_op jit(solution)/shard_map/ppermute | solution.py:184
  449.9 10.0 %collective-permute-done.26 = bf16[512,768]{1,0:T(8,128)(2,1)} collective-permute-done((bf16[512,768]{1,0:T(8,128)(2,1)}, bf16[512,768]{1,0:T(8,128)(2,1)}, u32[]{:S(2)}, u32[]{:S(2)}) %collective-permute-start.26) | collective-permute-done | bytes 786464 | tf_op jit(solution)/shard_map/ppermute | solution.py:184
  459.9 5.0 %collective-permute-done.27 = bf16[512,768]{1,0:T(8,128)(2,1)} collective-permute-done((bf16[512,768]{1,0:T(8,128)(2,1)}, bf16[512,768]{1,0:T(8,128)(2,1)}, u32[]{:S(2)}, u32[]{:S(2)}) %collective-permute-start.27) | collective-permute-done | bytes 786464 | tf_op jit(solution)/shard_map/ppermute | solution.py:185
  464.9 1.6 fusion.3
  469.9 3.7 add_convert_fusion.5
  (110 shorter events, 37.0 us)
Async XLA Ops:
  7.2 71.0 %all-gather.5.cloned.1.call-start = ((), (), s32[]{:S(2)}) async-start(), calls=%async_computation.1 | async-start | bytes 7077888 | tf_op jit(solution)/shard_map/all_gather | solution.py:211
  10.6 8.8 %copy-start.19 = (bf16[4096]{0:T(1024)(128)(2,1)S(1)}, bf16[4096]{0:T(1024)(128)(2,1)}, u32[]{:S(2)}) copy-start(bf16[4096]{0:T(1024)(128)(2,1)} %param.8) | copy-start | bytes 24580
  10.6 125.9 %all-gather.7.cloned.1.call-start = ((), (), s32[]{:S(2)}) async-start(), calls=%async_computation.2 | async-start | bytes 4718592 | tf_op jit(solution)/shard_map/all_gather | solution.py:211
  10.7 13.6 %copy-start.16 = (bf16[512,1024]{1,0:T(8,128)(2,1)S(1)}, bf16[512,1024]{1,0:T(8,128)(2,1)}, u32[]{:S(2)}) copy-start(bf16[512,1024]{1,0:T(8,128)(2,1)} %param.12) | copy-start | bytes 3145732
  19.4 5.9 %copy-start = (bf16[768,4096]{0,1:T(8,128)(2,1)S(1)}, bf16[768,4096]{0,1:T(8,128)(2,1)}, u32[]{:S(2)}) copy-start(bf16[768,4096]{0,1:T(8,128)(2,1)} %copy.12) | copy-start | bytes 18874372
  29.3 256.1 %all-gather.9.cloned.1.call-start = ((), (), s32[]{:S(2)}) async-start(), calls=%async_computation.3 | async-start | bytes 7077888 | tf_op jit(solution)/shard_map/all_gather | solution.py:211
  87.3 253.0 %all-gather.11.cloned.1.call-start = ((), (), s32[]{:S(2)}) async-start(), calls=%async_computation.4 | async-start | bytes 4718592 | tf_op jit(solution)/shard_map/all_gather | solution.py:211
  87.5 5.2 %copy-start.14 = (bf16[768,4,1,512]{0,3,2,1:T(8,128)(2,1)S(1)}, bf16[768,4,1,512]{0,3,2,1:T(8,128)(2,1)}, u32[]{:S(2)}) copy-start(bf16[768,4,1,512]{0,3,2,1:T(8,128)(2,1)} %get-tuple-element.195) | copy-start | bytes 9437188
  95.8 4.7 collective-permute-start
  102.7 1.3 copy-start.3
  104.9 24.9 %collective-permute-start.1 = (bf16[512,512]{1,0:T(8,128)(2,1)}, bf16[512,512]{1,0:T(8,128)(2,1)S(1)}, u32[]{:S(2)}, u32[]{:S(2)}) collective-permute-start(bf16[512,512]{1,0:T(8,128)(2,1)} %get-tuple-element.220), channel_id=1, source_target_pairs={{0,8},{4,12},{1,9},{5,13},{2,10},{6,14},{3,11},{7,15}} | collective-permute-start | bytes 1572872 | tf_op jit(solution)/shard_map/ppermute | solution.py:184
  106.2 23.6 %collective-permute-start.2 = (bf16[512,512]{1,0:T(8,128)(2,1)S(1)}, bf16[512,512]{1,0:T(8,128)(2,1)S(1)}, u32[]{:S(2)}, u32[]{:S(2)}) collective-permute-start(bf16[512,512]{1,0:T(8,128)(2,1)S(1)} %get-tuple-element.219), channel_id=1, source_target_pairs={{24,16},{28,20},{25,17},{29,21},{26,18},{30,22},{27,19},{31,23}} | collective-permute-start | bytes 1572872 | tf_op jit(solution)/shard_map/ppermute | solution.py:185
  132.1 16.9 %collective-permute-start.3 = (bf16[512,512]{1,0:T(8,128)(2,1)}, bf16[512,512]{1,0:T(8,128)(2,1)S(1)}, u32[]{:S(2)}, u32[]{:S(2)}) collective-permute-start(bf16[512,512]{1,0:T(8,128)(2,1)} %get-tuple-element.218), channel_id=1, source_target_pairs={{0,8},{4,12},{8,16},{12,20},{1,9},{5,13},{9,17},{13,21},{2,10},{6,... | collective-permute-start | bytes 1572872 | tf_op jit(solution)/shard_map/ppermute | solution.py:184
  136.5 12.6 %copy-start.4 = (bf16[2048,512]{1,0:T(8,128)(2,1)S(1)}, bf16[2048,512]{1,0:T(8,128)(2,1)}, u32[]{:S(2)}) copy-start(bf16[2048,512]{1,0:T(8,128)(2,1)} %copy-done.3) | copy-start | bytes 6291460
  136.5 12.5 %collective-permute-start.4 = (bf16[512,512]{1,0:T(8,128)(2,1)S(1)}, bf16[512,512]{1,0:T(8,128)(2,1)S(1)}, u32[]{:S(2)}, u32[]{:S(2)}) collective-permute-start(bf16[512,512]{1,0:T(8,128)(2,1)S(1)} %get-tuple-element.217), channel_id=1, source_target_pairs={{16,8},{20,12},{24,16},{28,20},{17,9},{21,13},{25,17},{29,21},{18,... | collective-permute-start | bytes 1572872 | tf_op jit(solution)/shard_map/ppermute | solution.py:185
  149.3 36.4 %collective-permute-start.5 = (bf16[512,512]{1,0:T(8,128)(2,1)S(1)}, bf16[512,512]{1,0:T(8,128)(2,1)S(1)}, u32[]{:S(2)}, u32[]{:S(2)}) collective-permute-start(bf16[512,512]{1,0:T(8,128)(2,1)S(1)} %get-tuple-element.216), channel_id=1, source_target_pairs={{0,8},{4,12},{8,16},{12,20},{16,24},{20,28},{1,9},{5,13},{9,17},{1... | collective-permute-start | bytes 1572872 | tf_op jit(solution)/shard_map/ppermute | solution.py:184
  165.2 38.2 %copy-start.11 = (bf16[768,4,1,512]{0,3,2,1:T(8,128)(2,1)S(1)}, bf16[768,4,1,512]{0,3,2,1:T(8,128)(2,1)}, u32[]{:S(2)}) copy-start(bf16[768,4,1,512]{0,3,2,1:T(8,128)(2,1)} %get-tuple-element.193) | copy-start | bytes 9437188
  165.2 37.0 %collective-permute-start.6 = (bf16[512,512]{1,0:T(8,128)(2,1)S(1)}, bf16[512,512]{1,0:T(8,128)(2,1)S(1)}, u32[]{:S(2)}, u32[]{:S(2)}) collective-permute-start(bf16[512,512]{1,0:T(8,128)(2,1)S(1)} %get-tuple-element.215), channel_id=1, source_target_pairs={{8,0},{12,4},{16,8},{20,12},{24,16},{28,20},{9,1},{13,5},{17,9},{2... | collective-permute-start | bytes 1572872 | tf_op jit(solution)/shard_map/ppermute | solution.py:185
  203.4 2.9 copy-start.9
  206.2 5.8 %collective-permute-start.7 = (bf16[2048,768]{1,0:T(8,128)(2,1)S(1)}, bf16[2048,768]{1,0:T(8,128)(2,1)S(1)}, u32[]{:S(2)}, u32[]{:S(2)}) collective-permute-start(bf16[2048,768]{1,0:T(8,128)(2,1)S(1)} %convolution_convert_fusion.3), channel_id=1, source_target_pairs={{0,4},{4,0},{8,12},{12,8},{16,20},{20,16},{24,28},{28,24},{1,5},{5... | collective-permute-start | bytes 9437192 | tf_op jit(solution)/shard_map/ppermute | solution.py:162
  213.0 1.6 copy-start.1
  215.6 30.9 %collective-permute-start.8 = (bf16[512,768]{1,0:T(8,128)(2,1)}, bf16[512,768]{1,0:T(8,128)(2,1)S(1)}, u32[]{:S(2)}, u32[]{:S(2)}) collective-permute-start(bf16[512,768]{1,0:T(8,128)(2,1)} %get-tuple-element.208), channel_id=1, source_target_pairs={{0,8},{4,12},{1,9},{5,13},{2,10},{6,14},{3,11},{7,15}} | collective-permute-start | bytes 2359304 | tf_op jit(solution)/shard_map/ppermute | solution.py:184
  218.7 27.8 %collective-permute-start.9 = (bf16[512,768]{1,0:T(8,128)(2,1)S(1)}, bf16[512,768]{1,0:T(8,128)(2,1)S(1)}, u32[]{:S(2)}, u32[]{:S(2)}) collective-permute-start(bf16[512,768]{1,0:T(8,128)(2,1)S(1)} %get-tuple-element.207), channel_id=1, source_target_pairs={{24,16},{28,20},{25,17},{29,21},{26,18},{30,22},{27,19},{31,23}} | collective-permute-start | bytes 2359304 | tf_op jit(solution)/shard_map/ppermute | solution.py:185
  219.4 250.5 %reduce-scatter.2.cloned.1.call-start = ((), (), s32[]{:S(2)}) async-start(), calls=%async_computation.5 | async-start | bytes 7864320 | tf_op jit(solution)/shard_map/reduce_scatter | solution.py:286
  219.5 27.0 %copy-start.2 = (bf16[2048,768]{1,0:T(8,128)(2,1)S(1)}, bf16[2048,768]{1,0:T(8,128)(2,1)}, u32[]{:S(2)}) copy-start(bf16[2048,768]{1,0:T(8,128)(2,1)} %copy-done.1) | copy-start | bytes 9437188
  246.9 38.0 %collective-permute-start.10 = (bf16[512,768]{1,0:T(8,128)(2,1)S(1)}, bf16[512,768]{1,0:T(8,128)(2,1)S(1)}, u32[]{:S(2)}, u32[]{:S(2)}) collective-permute-start(bf16[512,768]{1,0:T(8,128)(2,1)S(1)} %get-tuple-element.206), channel_id=1, source_target_pairs={{0,8},{4,12},{8,16},{12,20},{1,9},{5,13},{9,17},{13,21},{2,10},{6,... | collective-permute-start | bytes 2359304 | tf_op jit(solution)/shard_map/ppermute | solution.py:184
  251.3 33.6 %collective-permute-start.11 = (bf16[512,768]{1,0:T(8,128)(2,1)S(1)}, bf16[512,768]{1,0:T(8,128)(2,1)S(1)}, u32[]{:S(2)}, u32[]{:S(2)}) collective-permute-start(bf16[512,768]{1,0:T(8,128)(2,1)S(1)} %get-tuple-element.205), channel_id=1, source_target_pairs={{16,8},{20,12},{24,16},{28,20},{17,9},{21,13},{25,17},{29,21},{18,... | collective-permute-start | bytes 2359304 | tf_op jit(solution)/shard_map/ppermute | solution.py:185
  294.5 5.2 %copy-start.15 = (bf16[768,4,1,512]{0,3,2,1:T(8,128)(2,1)S(1)}, bf16[768,4,1,512]{0,3,2,1:T(8,128)(2,1)}, u32[]{:S(2)}) copy-start(bf16[768,4,1,512]{0,3,2,1:T(8,128)(2,1)} %get-tuple-element.195) | copy-start | bytes 9437188
  299.6 7.7 %copy-start.13 = (bf16[768,4,1,512]{0,3,2,1:T(8,128)(2,1)S(1)}, bf16[768,4,1,512]{0,3,2,1:T(8,128)(2,1)}, u32[]{:S(2)}) copy-start(bf16[768,4,1,512]{0,3,2,1:T(8,128)(2,1)} %get-tuple-element.196) | copy-start | bytes 9437188
  301.5 7.7 %collective-permute-start.12 = (bf16[2048,512]{1,0:T(8,128)(2,1)S(1)}, bf16[2048,512]{1,0:T(8,128)(2,1)S(1)}, u32[]{:S(2)}, u32[]{:S(2)}) collective-permute-start(bf16[2048,512]{1,0:T(8,128)(2,1)S(1)} %convolution_convert_fusion.5), channel_id=1, source_target_pairs={{0,4},{4,0},{8,12},{12,8},{16,20},{20,16},{24,28},{28,24},{1,5},{5... | collective-permute-start | bytes 6291464 | tf_op jit(solution)/shard_map/ppermute | solution.py:162
  301.5 22.2 %collective-permute-start.13 = (bf16[512,768]{1,0:T(8,128)(2,1)S(1)}, bf16[512,768]{1,0:T(8,128)(2,1)S(1)}, u32[]{:S(2)}, u32[]{:S(2)}) collective-permute-start(bf16[512,768]{1,0:T(8,128)(2,1)S(1)} %get-tuple-element.204), channel_id=1, source_target_pairs={{0,8},{4,12},{8,16},{12,20},{16,24},{20,28},{1,9},{5,13},{9,17},{1... | collective-permute-start | bytes 2359304 | tf_op jit(solution)/shard_map/ppermute | solution.py:184
  306.0 21.5 %collective-permute-start.14 = (bf16[512,768]{1,0:T(8,128)(2,1)S(1)}, bf16[512,768]{1,0:T(8,128)(2,1)S(1)}, u32[]{:S(2)}, u32[]{:S(2)}) collective-permute-start(bf16[512,768]{1,0:T(8,128)(2,1)S(1)} %get-tuple-element.203), channel_id=1, source_target_pairs={{8,0},{12,4},{16,8},{20,12},{24,16},{28,20},{9,1},{13,5},{17,9},{2... | collective-permute-start | bytes 2359304 | tf_op jit(solution)/shard_map/ppermute | solution.py:185
  309.8 26.1 %copy-start.5 = (bf16[2048,512]{1,0:T(8,128)(2,1)}, bf16[2048,512]{1,0:T(8,128)(2,1)S(1)}, u32[]{:S(2)}) copy-start(bf16[2048,512]{1,0:T(8,128)(2,1)S(1)} %add_convert_fusion.3) | copy-start | bytes 6291460
  309.9 24.8 %collective-permute-start.15 = (bf16[512,512]{1,0:T(8,128)(2,1)S(1)}, bf16[512,512]{1,0:T(8,128)(2,1)S(1)}, u32[]{:S(2)}, u32[]{:S(2)}) collective-permute-start(bf16[512,512]{1,0:T(8,128)(2,1)S(1)} %get-tuple-element.214), channel_id=1, source_target_pairs={{0,8},{4,12},{1,9},{5,13},{2,10},{6,14},{3,11},{7,15}} | collective-permute-start | bytes 1572872 | tf_op jit(solution)/shard_map/ppermute | solution.py:184
  314.4 20.2 %collective-permute-start.16 = (bf16[512,512]{1,0:T(8,128)(2,1)S(1)}, bf16[512,512]{1,0:T(8,128)(2,1)S(1)}, u32[]{:S(2)}, u32[]{:S(2)}) collective-permute-start(bf16[512,512]{1,0:T(8,128)(2,1)S(1)} %get-tuple-element.213), channel_id=1, source_target_pairs={{24,16},{28,20},{25,17},{29,21},{26,18},{30,22},{27,19},{31,23}} | collective-permute-start | bytes 1572872 | tf_op jit(solution)/shard_map/ppermute | solution.py:185
  335.9 15.7 %collective-permute-start.17 = (bf16[512,512]{1,0:T(8,128)(2,1)}, bf16[512,512]{1,0:T(8,128)(2,1)S(1)}, u32[]{:S(2)}, u32[]{:S(2)}) collective-permute-start(bf16[512,512]{1,0:T(8,128)(2,1)} %get-tuple-element.212), channel_id=1, source_target_pairs={{0,8},{4,12},{8,16},{12,20},{1,9},{5,13},{9,17},{13,21},{2,10},{6,... | collective-permute-start | bytes 1572872 | tf_op jit(solution)/shard_map/ppermute | solution.py:184
  340.3 12.1 %copy-start.6 = (bf16[2048,512]{1,0:T(8,128)(2,1)S(1)}, bf16[2048,512]{1,0:T(8,128)(2,1)}, u32[]{:S(2)}) copy-start(bf16[2048,512]{1,0:T(8,128)(2,1)} %copy-done.5) | copy-start | bytes 6291460
  340.3 12.1 %collective-permute-start.18 = (bf16[512,512]{1,0:T(8,128)(2,1)}, bf16[512,512]{1,0:T(8,128)(2,1)S(1)}, u32[]{:S(2)}, u32[]{:S(2)}) collective-permute-start(bf16[512,512]{1,0:T(8,128)(2,1)} %get-tuple-element.211), channel_id=1, source_target_pairs={{16,8},{20,12},{24,16},{28,20},{17,9},{21,13},{25,17},{29,21},{18,... | collective-permute-start | bytes 1572872 | tf_op jit(solution)/shard_map/ppermute | solution.py:185
  341.2 13.4 %copy-start.20 = (bf16[4096,512]{1,0:T(8,128)(2,1)S(1)}, bf16[4096,512]{1,0:T(8,128)(2,1)}, u32[]{:S(2)}) copy-start(bf16[4096,512]{1,0:T(8,128)(2,1)} %all-gather.11.cloned.1.call-done) | copy-start | bytes 12582916
  351.6 0.8 copy-start.18
  362.8 1.0 copy-start.17
  363.8 15.8 %collective-permute-start.19 = (bf16[512,512]{1,0:T(8,128)(2,1)S(1)}, bf16[512,512]{1,0:T(8,128)(2,1)S(1)}, u32[]{:S(2)}, u32[]{:S(2)}) collective-permute-start(bf16[512,512]{1,0:T(8,128)(2,1)S(1)} %copy-done.17), channel_id=1, source_target_pairs={{0,8},{4,12},{8,16},{12,20},{16,24},{20,28},{1,9},{5,13},{9,17},{1... | collective-permute-start | bytes 1572872 | tf_op jit(solution)/shard_map/ppermute | solution.py:184
  369.8 16.4 %copy-start.12 = (bf16[768,4,1,512]{0,3,2,1:T(8,128)(2,1)S(1)}, bf16[768,4,1,512]{0,3,2,1:T(8,128)(2,1)}, u32[]{:S(2)}) copy-start(bf16[768,4,1,512]{0,3,2,1:T(8,128)(2,1)} %get-tuple-element.193) | copy-start | bytes 9437188
  369.8 14.2 %collective-permute-start.20 = (bf16[512,512]{1,0:T(8,128)(2,1)S(1)}, bf16[512,512]{1,0:T(8,128)(2,1)S(1)}, u32[]{:S(2)}, u32[]{:S(2)}) collective-permute-start(bf16[512,512]{1,0:T(8,128)(2,1)S(1)} %get-tuple-element.209), channel_id=1, source_target_pairs={{8,0},{12,4},{16,8},{20,12},{24,16},{28,20},{9,1},{13,5},{17,9},{2... | collective-permute-start | bytes 1572872 | tf_op jit(solution)/shard_map/ppermute | solution.py:185
  386.2 2.9 copy-start.10
  389.0 5.7 %collective-permute-start.21 = (bf16[2048,768]{1,0:T(8,128)(2,1)S(1)}, bf16[2048,768]{1,0:T(8,128)(2,1)S(1)}, u32[]{:S(2)}, u32[]{:S(2)}) collective-permute-start(bf16[2048,768]{1,0:T(8,128)(2,1)S(1)} %convolution_convert_fusion.1), channel_id=1, source_target_pairs={{0,4},{4,0},{8,12},{12,8},{16,20},{20,16},{24,28},{28,24},{1,5},{5... | collective-permute-start | bytes 9437192 | tf_op jit(solution)/shard_map/ppermute | solution.py:162
  395.8 19.4 %collective-permute-start.22 = (bf16[512,768]{1,0:T(8,128)(2,1)S(1)}, bf16[512,768]{1,0:T(8,128)(2,1)S(1)}, u32[]{:S(2)}, u32[]{:S(2)}) collective-permute-start(bf16[512,768]{1,0:T(8,128)(2,1)S(1)} %get-tuple-element.202), channel_id=1, source_target_pairs={{0,8},{4,12},{1,9},{5,13},{2,10},{6,14},{3,11},{7,15}} | collective-permute-start | bytes 2359304 | tf_op jit(solution)/shard_map/ppermute | solution.py:184
  398.2 17.0 %collective-permute-start.23 = (bf16[512,768]{1,0:T(8,128)(2,1)S(1)}, bf16[512,768]{1,0:T(8,128)(2,1)S(1)}, u32[]{:S(2)}, u32[]{:S(2)}) collective-permute-start(bf16[512,768]{1,0:T(8,128)(2,1)S(1)} %get-tuple-element.201), channel_id=1, source_target_pairs={{24,16},{28,20},{25,17},{29,21},{26,18},{30,22},{27,19},{31,23}} | collective-permute-start | bytes 2359304 | tf_op jit(solution)/shard_map/ppermute | solution.py:185
  415.6 20.6 %collective-permute-start.24 = (bf16[512,768]{1,0:T(8,128)(2,1)S(1)}, bf16[512,768]{1,0:T(8,128)(2,1)S(1)}, u32[]{:S(2)}, u32[]{:S(2)}) collective-permute-start(bf16[512,768]{1,0:T(8,128)(2,1)S(1)} %get-tuple-element.200), channel_id=1, source_target_pairs={{0,8},{4,12},{8,16},{12,20},{1,9},{5,13},{9,17},{13,21},{2,10},{6,... | collective-permute-start | bytes 2359304 | tf_op jit(solution)/shard_map/ppermute | solution.py:184
  420.1 16.2 %collective-permute-start.25 = (bf16[512,768]{1,0:T(8,128)(2,1)S(1)}, bf16[512,768]{1,0:T(8,128)(2,1)S(1)}, u32[]{:S(2)}, u32[]{:S(2)}) collective-permute-start(bf16[512,768]{1,0:T(8,128)(2,1)S(1)} %get-tuple-element.199), channel_id=1, source_target_pairs={{16,8},{20,12},{24,16},{28,20},{17,9},{21,13},{25,17},{29,21},{18,... | collective-permute-start | bytes 2359304 | tf_op jit(solution)/shard_map/ppermute | solution.py:185
  437.9 22.0 %collective-permute-start.26 = (bf16[512,768]{1,0:T(8,128)(2,1)}, bf16[512,768]{1,0:T(8,128)(2,1)}, u32[]{:S(2)}, u32[]{:S(2)}) collective-permute-start(bf16[512,768]{1,0:T(8,128)(2,1)} %get-tuple-element.198), channel_id=1, source_target_pairs={{0,8},{4,12},{8,16},{12,20},{16,24},{20,28},{1,9},{5,13},{9,17},{1... | collective-permute-start | bytes 2359304 | tf_op jit(solution)/shard_map/ppermute | solution.py:184
  445.5 19.5 %collective-permute-start.27 = (bf16[512,768]{1,0:T(8,128)(2,1)}, bf16[512,768]{1,0:T(8,128)(2,1)}, u32[]{:S(2)}, u32[]{:S(2)}) collective-permute-start(bf16[512,768]{1,0:T(8,128)(2,1)} %get-tuple-element.197), channel_id=1, source_target_pairs={{8,0},{12,4},{16,8},{20,12},{24,16},{28,20},{9,1},{13,5},{17,9},{2... | collective-permute-start | bytes 2359304 | tf_op jit(solution)/shard_map/ppermute | solution.py:185
  446.8 1.4 copy-start.7
  446.8 1.7 copy-start.8
  466.6 1.9 slice-start
Sparse Core Ops, SparseCore 0:
  10.7 67.4 all-gather.4
  80.4 52.2 all-gather.6
  134.9 81.9 all-gather.8
  219.5 67.0 all-gather.10
  362.9 71.7 reduce-scatter.1

commit v2 on v1

--- a/solution.py
+++ b/solution.py
@@ -135,31 +135,166 @@
     return lax.dynamic_index_in_dim(blocks, at, 0, keepdims=False)
 
 
+def split_kernel(chips, core_ref, x_ref, gain_ref, grad_ref, x_own, x_other, grad_own, grad_other):
+    features = x_ref.shape[1]
+    rows = features // (2 * chips)
+    core = core_ref[0]
+    total = None
+    for w in range(2 * chips):
+        values = x_ref[:, w * rows : (w + 1) * rows].astype(F32)
+        part = jnp.sum(values * values, axis=-1, keepdims=True)
+        total = part if total is None else total + part
+    scale = lax.rsqrt(total / features + EPSILON)
+    for side, x_out, grad_out in ((core, x_own, grad_own), (1 - core, x_other, grad_other)):
+        for chip in range(chips):
+            cols = pl.ds(pl.multiple_of((2 * chip + side) * rows, 128), rows)
+            to = slice(chip * rows, (chip + 1) * rows)
+            x_out[:, to] = (x_ref[:, cols].astype(F32) * scale * gain_ref[:, cols]).astype(BF16)
+            grad_out[:, to] = grad_ref[:, cols]
+
+
+def norm_and_split(core, activations, gain, cotangent, chips):
+    length, features = activations.shape
+    step = 128 if length % 128 == 0 else length
+    whole = pl.BlockSpec((step, features), lambda i: (i, 0))
+    half = pl.BlockSpec((step, features // 2), lambda i: (i, 0))
+    shape = jax.ShapeDtypeStruct((length, features // 2), BF16)
+    return pl.pallas_call(
+        functools.partial(split_kernel, chips),
+        grid=(length // step,),
+        out_shape=(shape,) * 4,
+        in_specs=[
+            pl.BlockSpec(memory_space=pltpu.SMEM),
+            whole,
+            pl.BlockSpec((1, features), lambda i: (0, 0)),
+            whole,
+        ],
+        out_specs=(half,) * 4,
+        compiler_params=pltpu.CompilerParams(vmem_limit_bytes=32 * 2**20),
+        cost_estimate=pl.CostEstimate(
+            flops=8 * length * features,
+            bytes_accessed=8 * length * features,
+            transcendentals=length,
+        ),
+        name="norm_and_split",
+    )(core.reshape(1), activations, gain.astype(F32).reshape(1, -1), cotangent)
+
+
+def collect_kernel(chips, chip_ref, *refs):
+    own, ups, downs = refs[0], refs[: chips], refs[chips : 2 * chips - 1]
+    out, sems = refs[-2], refs[-1]
+    rows = own.shape[0]
+    chip = chip_ref[0]
+
+    def place(source, r):
+        at = lax.rem(chip - r + chips, chips)
+        to = out.at[pl.ds(pl.multiple_of(at * rows, rows), rows), :]
+        return pltpu.make_async_copy(source, to, sems.at[r])
+
+    for r in range(chips):
+        if r == 0:
+            place(own, r).start()
+            continue
+        pl.when(chip >= r)(lambda r=r: place(ups[r], r).start())
+        pl.when(chip < r)(lambda r=r: place(downs[chips - r - 1], r).start())
+    for r in range(chips):
+        place(own, r).wait()
+
+
+def collect(chip, chips, ups, downs):
+    rows, cols = ups[0].shape
+    anywhere = pl.BlockSpec(memory_space=pl.ANY)
+    return pl.pallas_call(
+        functools.partial(collect_kernel, chips),
+        out_shape=jax.ShapeDtypeStruct((chips * rows, cols), BF16),
+        in_specs=[pl.BlockSpec(memory_space=pltpu.SMEM)] + [anywhere] * (len(ups) + len(downs)),
+        out_specs=anywhere,
+        scratch_shapes=[pltpu.SemaphoreType.DMA((chips,))],
+        cost_estimate=pl.CostEstimate(
+            flops=0, bytes_accessed=4 * chips * rows * cols, transcendentals=0
+        ),
+        name="collect",
+    )(chip.reshape(1), *ups, *downs)
+
+
 class Order:
     def __init__(self):
         self.last = None
 
     def __call__(self, compute, *operands):
-        if self.last is not None:
-            tied = lax.optimization_barrier((self.last, *operands))
-            operands = tied[1:]
-        result = compute(*operands)
+        result = compute(*self.after(*operands))
         self.last = jax.tree.leaves(result)[0]
         return result
 
-    def after(self, operand):
-        return operand if self.last is None else lax.optimization_barrier((self.last, operand))[1]
+    def after(self, *operands):
+        if self.last is None:
+            return operands
+        return lax.optimization_barrier((self.last, *operands))[1:]
+
+    def wait(self, *arrays):
+        if self.last is None:
+            return arrays
+        self.last, *arrays = lax.optimization_barrier((self.last, *arrays))
+        return arrays
+
+
+def swap_cores(array, chips):
+    return lax.ppermute(array, "wide", [(w, w ^ 1) for w in range(2 * chips)])
+
+
+class LineGather:
+    def __init__(self, order, chips, piece):
+        self.order, self.chips, self.piece = order, chips, piece
+        self.chip = lax.axis_index("wide") // 2
+        self.ups = []
+        self.downs = []
+
+    def hop(self):
+        chips, t = self.chips, len(self.ups) or 1
+        if not self.ups:
+            (self.piece,) = self.order.after(self.piece)
+            self.ups = [self.piece]
+            up = down = self.piece
+        else:
+            up, down = self.wait()
+        if t >= chips:
+            return False
+        self.ups.append(
+            lax.ppermute(up, "wide", [(w, w + 2) for w in range(2 * (t - 1), 2 * (chips - 1))])
+        )
+        self.downs.append(
+            lax.ppermute(down, "wide", [(w, w - 2) for w in range(2, 2 * (chips - t + 1))])
+        )
+        return True
+
+    def wait(self):
+        if not self.downs:
+            return self.piece, self.piece
+        self.ups[-1], self.downs[-1] = self.order.wait(self.ups[-1], self.downs[-1])
+        return self.ups[-1], self.downs[-1]
+
+    def finish(self):
+        while self.hop():
+            pass
+
+    def halves(self):
+        own = self.order(
+            lambda *refs: collect(self.chip, self.chips, refs[: self.chips], refs[self.chips :]),
+            *self.ups,
+            *self.downs,
+        )
+        return own, swap_cores(own, self.chips)
 
 
 class LineSum:
     def __init__(self, order, chips):
         self.order, self.chips = order, chips
         self.chip = lax.axis_index("wide") // 2
-        self.up = self.down = None
+        self.up = self.down = self.result = None
+        self.hops = 0
 
     def swap(self, send):
-        pairs = [(w, w ^ 1) for w in range(2 * self.chips)]
-        self.received = lax.ppermute(send, "wide", pairs)
+        self.received = swap_cores(send, self.chips)
 
     def add_cores(self, keep):
         def add(keep, received):
@@ -168,8 +303,15 @@
         both = self.order(add, keep, self.received)
         self.both = both.reshape(self.chips, -1, both.shape[-1])
 
-    def hop(self, t):
-        chips, chip, far = self.chips, self.chip, self.chips - t
+    def advance(self):
+        if self.result is not None:
+            return
+        self.hops += 1
+        if self.hops == self.chips:
+            self.result = self.total()
+            return
+        t, chips, chip = self.hops, self.chips, self.chip
+        far = chips - t
 
         def messages(both, *arrived):
             up = take(both, jnp.minimum(chip + far, chips - 1))
@@ -183,6 +325,10 @@
         up, down = self.order(messages, self.both, *arrived)
         self.up = lax.ppermute(up, "wide", [(w, w + 2) for w in range(2 * t)])
         self.down = lax.ppermute(down, "wide", [(w, w - 2) for w in range(2 * far, 2 * chips)])
+
+    def finish(self):
+        while self.result is None:
+            self.advance()
 
     def total(self):
         def add(both, *arrived):
@@ -207,96 +353,99 @@
     core = lax.axis_index("wide") % 2
     order = Order()
 
-    def gathered(piece):
-        return lax.all_gather(piece, "wide", axis=0, tiled=True)
-
     def columns(g):
         cols = slice(g * span, (g + 1) * span)
         heads = slice(g * width, (g + 1) * width)
         return jnp.concatenate([w_query[:, cols], w_key[:, heads], w_value[:, heads]], axis=1)
 
-    def out_columns(g):
-        return w_out[:, g * span : (g + 1) * span]
-
-    def halves(array):
-        split = array.reshape(length, chips, 2, rows)
-        own = lax.dynamic_index_in_dim(split, core, 2, keepdims=False)
-        other = lax.dynamic_index_in_dim(split, 1 - core, 2, keepdims=False)
-        return own.reshape(length, chips * rows), other.reshape(length, chips * rows)
-
-    def product(a, b):
-        return jnp.dot(a, b, preferred_element_type=F32).astype(BF16)
-
     def term(a, b):
         return row_product(a, b).astype(BF16)
 
-    weights = [None] * groups
-    out_weights = [None] * groups
-    weights[0] = gathered(columns(0))
-    normed = order(normalize, activations, gain)
-    out_weights[0] = gathered(order.after(out_columns(0)))
-    normed_own, normed_other = order(halves, normed)
-    cotangent_own, cotangent_other = order(halves, cotangent)
-
-    projected = None
-    pending = []
-
-    def advance():
-        for steps in list(pending):
-            if next(steps, None) is None:
-                pending.remove(steps)
-
-    def steps_of(line, results):
-        for t in range(1, chips):
-            line.hop(t)
-            yield True
-        results.append(line.total())
-        yield True
-
-    def start(own, other, grads, results):
+    def product(sides, own, other):
+        part = order(nn, sides[0], own)
+        return order(lambda a, b, c: (c + nn(a, b)).astype(BF16), sides[1], other, part)
+
+    def add_nt(a, b, part):
+        return part + nt(a, b)
+
+    def project(mixed, side, part):
+        if part is None:
+            return order(lambda a, b: nt(a, b).astype(BF16), mixed, side)
+        return order(lambda a, b, c: add_nt(a, b, c).astype(BF16), mixed, side, part)
+
+    def start_sum(sides, grads):
         line = LineSum(order, chips)
-        line.swap(order(term, other, grads))
-        line.add_cores(order(term, own, grads))
-        steps = steps_of(line, results)
-        next(steps)
-        pending.append(steps)
-
-    sums_out, sums_qkv = [], []
+        line.swap(order(term, sides[1], grads))
+        line.add_cores(order(term, sides[0], grads))
+        line.advance()
+        return line
+
+    qkv_gather = [LineGather(order, chips, columns(g)) for g in range(groups)]
+    out_gather = [
+        LineGather(order, chips, w_out[:, g * span : (g + 1) * span]) for g in range(groups)
+    ]
+    qkv_sum, out_sum = [], []
+    partial = [None, None]
+
+    qkv_gather[0].hop()
+    x_own, x_other, grad_own, grad_other = order(
+        lambda a, b, c: norm_and_split(core, a, b, c, chips), activations, gain, cotangent
+    )
+    x_sides, grad_sides = (x_own, x_other), (grad_own, grad_other)
+    out_gather[0].hop()
+    qkv_gather[0].hop()
+    qkv_gather[0].hop()
+    out_gather[0].hop()
     for g in range(groups):
-        qkv = order(product, normed, weights[g])
-        if g + 1 < groups:
-            weights[g + 1] = gathered(order.after(columns(g + 1)))
+        more = g + 1 < groups
+        qkv_gather[g].finish()
+        if more:
+            qkv_gather[g + 1].hop()
+        own, other = qkv_gather[g].halves()
+        qkv = product(x_sides, own, other)
+        if g:
+            qkv_sum[g - 1].advance()
         mixed, lse = order(lambda a: attend_forward(a, members, block), qkv)
-        start(cotangent_own, cotangent_other, mixed, sums_out)
-        advance()
-        grad_mixed = order(product, cotangent, out_weights[g])
-        if g + 1 < groups:
-            out_weights[g + 1] = gathered(order.after(out_columns(g + 1)))
-        advance()
-        if g + 1 == groups:
-
-            def project(mixed, out_weights, *partial):
-                result = nt(mixed, out_weights)
-                for part in partial:
-                    result = result + part
-                return result.astype(BF16)
-
-            partial = () if projected is None else (projected,)
-            projected = order(project, mixed, out_weights[g], *partial)
-            summed = lax.psum_scatter(projected, "narrow", scatter_dimension=1, tiled=True)
+        out_gather[g].hop()
+        out_sum.append(start_sum(grad_sides, mixed))
+        if g:
+            qkv_sum[g - 1].finish()
+        out_gather[g].finish()
+        if more:
+            qkv_gather[g + 1].hop()
+            out_gather[g + 1].hop()
+        own, other = out_gather[g].halves()
+        if not more:
+            projected = [project(mixed, side, partial[i]) for i, side in enumerate((own, other))]
+            summed = [
+                lax.psum_scatter(part, "narrow", scatter_dimension=1, tiled=True)
+                for part in projected
+            ]
+        grad_mixed = product(grad_sides, own, other)
+        out_sum[g].advance()
         grad_qkv = order(
             lambda a, b, c: attend_backward(a, b, c, members, block), qkv, grad_mixed, lse
         )
-        advance()
-        start(normed_own, normed_other, grad_qkv, sums_qkv)
-        if g + 1 < groups:
-            part = order(nt, mixed, out_weights[g])
-            projected = part if projected is None else projected + part
-            advance()
-            advance()
-    while pending:
-        advance()
-
+        out_sum[g].advance()
+        qkv_sum.append(start_sum(x_sides, grad_qkv))
+        if more:
+            qkv_gather[g + 1].hop()
+            partial = [
+                order(nt, mixed, side) if part is None else order(add_nt, mixed, side, part)
+                for side, part in zip((own, other), partial)
+            ]
+            qkv_sum[g].advance()
+            out_sum[g].finish()
+            out_gather[g + 1].hop()
+    out_sum[-1].finish()
+    qkv_sum[-1].finish()
+
+    own, other = (part.reshape(length, -1, 1, rows) for part in summed)
+    summed = jnp.where(
+        core == 0,
+        jnp.concatenate([own, other], axis=2),
+        jnp.concatenate([other, own], axis=2),
+    ).reshape(length, -1)
     share = summed.shape[1]
     own_columns = lax.dynamic_slice_in_dim(
         activations, lax.axis_index("narrow") * share, share, 1
@@ -306,10 +455,10 @@
     def joined(pieces):
         return pieces[0] if len(pieces) == 1 else jnp.concatenate(pieces, axis=1)
 
-    grad_query = joined([s[:, :span] for s in sums_qkv])
-    grad_key = joined([s[:, span : span + width] for s in sums_qkv])
-    grad_value = joined([s[:, span + width :] for s in sums_qkv])
-    grad_out = joined(sums_out)
+    grad_query = joined([s.result[:, :span] for s in qkv_sum])
+    grad_key = joined([s.result[:, span : span + width] for s in qkv_sum])
+    grad_value = joined([s.result[:, span + width :] for s in qkv_sum])
+    grad_out = joined([s.result for s in out_sum])
     return (outputs, grad_query, grad_key, grad_value, grad_out)
 
 

time: 487 us -> 861 us (1.77)
  Pallas kernels: 22.4 us -> 351 us
  starting transfers between devices: 75.7 us -> 110 us
  local copies, waits for them, and re-layouts: 41.5 us -> 32.7 us
    pallas_call x0 -> x5, Pallas kernels: none -> 328 us  [the longest x4 322 us: collect(): pl.pallas_call(functools.partial(collect_kernel, chips), out_shape=jax.Sh...]
    ppermute x28 -> x56, starting transfers between devices: 75.3 us -> 110 us  [the longest x12 49.8 us: advance(): self.up = lax.ppermute(up, 'wide', [(w, w + 2) for w in range(2 * t)])]
    ppermute x28 -> x56, waiting for transfers between devices: 186 us -> 220 us  [the longest x12 121 us: hop(): lax.ppermute(down, 'wide', [(w, w - 2) for w in range(2, 2 * (chips - t +...]
    all_gather x4 -> x0, waiting for transfers between devices: 27.4 us -> none  [gathered(): return lax.all_gather(piece, 'wide', axis=0, tiled=True)]
    dynamic_slice x2 -> x1, local copies, waits for them, and re-layouts: 11.9 us -> 2.67 us  [shards(): lax.dynamic_slice_in_dim(activations, lax.axis_index('narrow') * share, s...]
    optimization_barrier x1 -> x0, local copies, waits for them, and re-layouts: 8.67 us -> none  [__call__(): tied = lax.optimization_barrier((self.last, *operands))]
    unnamed x43 -> x94, local copies, waits for them, and re-layouts: 14 us -> 20.6 us
    dot_general x4 -> x8, matrix products: 33.1 us -> 27.6 us  [nn(): lax.dot_general(a, b, (((1,), (0,)), ((), ())), preferred_element_type=F32)]
  transfers between devices with their start and end apart: 33 -> 58, of which waited for: 20 -> 28; matrix products, arithmetic and copies ran while one was open for 27% -> 13% of each run, Pallas kernels for 5% -> 2%
where the time goes in v2:
time: 861 us; the launch traced here: 850 us
  Pallas kernels  351 us (41%)
  waiting for transfers between devices  220 us (26%)
  starting transfers between devices  110 us (13%)
  matrix products  76.8 us (9%)
  other arithmetic  44.2 us (5%)
  local copies, waits for them, and re-layouts  32.7 us (4%)
  between operations  15.4 us (2%)
    pallas_call x4, Pallas kernels, collect(): pl.pallas_call(functools.partial(collect_kernel, chips), out_shape=jax.Sh...  322 us
    ppermute x12, waiting for transfers between devices, hop(): lax.ppermute(down, 'wide', [(w, w - 2) for w in range(2, 2 * (chips - t +...  121 us
    ppermute x12, waiting for transfers between devices, advance(): self.up = lax.ppermute(up, 'wide', [(w, w + 2) for w in range(2 * t)])  62.3 us
    ppermute x12, starting transfers between devices, advance(): self.up = lax.ppermute(up, 'wide', [(w, w + 2) for w in range(2 * t)])  49.8 us
    ppermute x12, starting transfers between devices, hop(): lax.ppermute(up, 'wide', [(w, w + 2) for w in range(2 * (t - 1), 2 * (chi...  30.2 us
    dot_general x8, matrix products, row_product(): lax.dot_general(a, b, (((0,), (0,)), ((), ())), preferred_element_type=F32)  28 us
    dot_general x8, matrix products, nn(): lax.dot_general(a, b, (((1,), (0,)), ((), ())), preferred_element_type=F32)  27.6 us
    ppermute x12, waiting for transfers between devices, advance(): lax.ppermute(down, 'wide', [(w, w - 2) for w in range(2 * far, 2 * chips)])  24.2 us
  transfers between devices with their start and end apart: 58, of which 28 were waited for; matrix products, arithmetic and copies ran while one was open for 13% of the time, Pallas kernels for 2%

profile of v2, /device:TPU:0, one launch (start us, length us, event | category | flops | bytes accessed | tf_op | source)
XLA Modules:
  0.0 849.5 jit_solution(10106547200598569640)
XLA Ops:
  10.4 5.8 collective-permute-start
  20.3 6.1 norm_and_split.1
  32.4 5.0 collective-permute-done.1.refs_4_
  40.3 20.5 %collective-permute-done.3.refs_5_ = bf16[512,768]{1,0:T(8,128)(2,1)} collective-permute-done((bf16[512,768]{1,0:T(8,128)(2,1)}, bf16[512,768]{1,0:T(8,128)(2,1)}, u32[]{:S(2)}, u32[]{:S(2)}) %collective-permute-start.3) | collective-permute-done | bytes 786464 | tf_op jit(solution)/shard_map/ppermute | solution.py:266
  64.7 6.2 collective-permute-start.4
  72.2 7.0 collective-permute-done.4.refs_1_
  79.2 13.7 %collective-permute-done.5.refs_4_ = bf16[512,512]{1,0:T(8,128)(2,1)} collective-permute-done((bf16[512,512]{1,0:T(8,128)(2,1)}, bf16[512,512]{1,0:T(8,128)(2,1)}, u32[]{:S(2)}, u32[]{:S(2)}) %collective-permute-start.5) | collective-permute-done | bytes 524320 | tf_op jit(solution)/shard_map/ppermute | solution.py:266
  92.9 96.4 %collect.4 = bf16[2048,768]{1,0:T(8,128)(2,1)} custom-call(s32[1]{0:T(128)} %bitcast.chip_ref, bf16[512,768]{1,0:T(8,128)(2,1)} %pad_maximum_fusion.2.refs_0_, bf16[512,768]{1,0:T(8,128)(2,1)} %collective-permute-done.refs_1_, bf16[512,768]{1,0:T(8,128)(2,1)} %collective-permute-done.2.refs_2_, bf16[512,768]{1,0:T(8,128)(2,1)} %collective-permute-done.6.refs_3_, ...), custom_call_target="tpu_custom_call" | custom-call | bytes 6291456 | tf_op jit(solution)/shard_map/collect/pallas_call | solution.py:207
  189.5 4.6 fusion.28
  198.3 5.2 attend_forward.2
  203.5 3.2 convolution_convert_fusion.7
  209.7 4.6 collective-permute-start.14
  215.6 9.6 %collective-permute-done.11.refs_5_ = bf16[512,512]{1,0:T(8,128)(2,1)} collective-permute-done((bf16[512,512]{1,0:T(8,128)(2,1)}, bf16[512,512]{1,0:T(8,128)(2,1)}, u32[]{:S(2)}, u32[]{:S(2)}) %collective-permute-start.11) | collective-permute-done | bytes 524320 | tf_op jit(solution)/shard_map/ppermute | solution.py:266
  227.7 3.7 convolution_convert_fusion.6
  236.0 16.7 %collective-permute-done.13.refs_6_ = bf16[512,512]{1,0:T(8,128)(2,1)S(1)} collective-permute-done((bf16[512,512]{1,0:T(8,128)(2,1)}, bf16[512,512]{1,0:T(8,128)(2,1)S(1)}, u32[]{:S(2)}, u32[]{:S(2)}) %collective-permute-start.13) | collective-permute-done | bytes 524320 | tf_op jit(solution)/shard_map/ppermute | solution.py:266
  253.5 64.7 %collect.5 = bf16[2048,512]{1,0:T(8,128)(2,1)} custom-call(s32[1]{0:T(128)} %bitcast.chip_ref, bf16[512,512]{1,0:T(8,128)(2,1)} %get-tuple-element.222.refs_0_, bf16[512,512]{1,0:T(8,128)(2,1)} %collective-permute-done.4.refs_1_, bf16[512,512]{1,0:T(8,128)(2,1)} %collective-permute-done.10.refs_2_, bf16[512,512]{1,0:T(8,128)(2,1)} %copy-done.41, ...), custom_call_target="tpu_custom_call" | custom-call | bytes 4194304 | tf_op jit(solution)/shard_map/collect/pallas_call | solution.py:207
  320.7 4.4 fusion.32
  325.2 3.4 fusion.33
  329.0 3.0 collective-permute-done.17
  332.3 4.3 collective-permute-start.19
  337.3 6.1 attend_backward.2
  343.4 4.2 collective-permute-done.19
  348.9 2.9 convolution_convert_fusion.3
  353.9 3.0 convolution_convert_fusion.2
  361.4 16.3 %collective-permute-done.29.refs_5_ = bf16[512,768]{1,0:T(8,128)(2,1)S(1)} collective-permute-done((bf16[512,768]{1,0:T(8,128)(2,1)S(1)}, bf16[512,768]{1,0:T(8,128)(2,1)S(1)}, u32[]{:S(2)}, u32[]{:S(2)}) %collective-permute-start.29) | collective-permute-done | bytes 786464 | tf_op jit(solution)/shard_map/ppermute | solution.py:266
  380.9 19.0 %collective-permute-done.31.refs_6_ = bf16[512,768]{1,0:T(8,128)(2,1)} collective-permute-done((bf16[512,768]{1,0:T(8,128)(2,1)S(1)}, bf16[512,768]{1,0:T(8,128)(2,1)}, u32[]{:S(2)}, u32[]{:S(2)}) %collective-permute-start.31) | collective-permute-done | bytes 786464 | tf_op jit(solution)/shard_map/ppermute | solution.py:266
  400.0 96.4 %collect.6 = bf16[2048,768]{1,0:T(8,128)(2,1)} custom-call(s32[1]{0:T(128)} %bitcast.chip_ref, bf16[512,768]{1,0:T(8,128)(2,1)} %copy-done.27, bf16[512,768]{1,0:T(8,128)(2,1)} %copy-done.32, bf16[512,768]{1,0:T(8,128)(2,1)} %copy-done.35, bf16[512,768]{1,0:T(8,128)(2,1)} %copy-done.37, bf16[512,768]{1,0:T(8,128)(2,1)} %copy-done.33, ...), custom_call_target="tpu_custom_call" | custom-call | bytes 6291456 | tf_op jit(solution)/shard_map/collect/pallas_call | solution.py:207
  498.6 4.5 fusion.30
  503.1 6.2 fusion.31
  509.3 6.5 collective-permute-done.22
  516.3 4.3 collective-permute-start.33
  527.3 10.1 %collective-permute-done.33 = bf16[512,768]{1,0:T(8,128)(2,1)S(1)} collective-permute-done((bf16[512,768]{1,0:T(8,128)(2,1)S(1)}, bf16[512,768]{1,0:T(8,128)(2,1)S(1)}, u32[]{:S(2)}, u32[]{:S(2)}) %collective-permute-start.33) | collective-permute-done | bytes 786464 | tf_op jit(solution)/shard_map/ppermute | solution.py:326
  538.7 5.2 attend_forward.3
  543.9 3.2 convolution_convert_fusion.5
  547.1 7.4 collective-permute-start.24
  555.8 5.4 collective-permute-start.26
  562.5 3.8 collective-permute-done.24
  566.2 5.2 collective-permute-done.25
  574.0 3.0 collective-permute-done.26.refs_1_
  577.0 5.0 collective-permute-done.27.refs_4_
  584.0 4.6 collective-permute-start.38
  588.6 9.4 %collective-permute-done.36.refs_5_ = bf16[512,512]{1,0:T(8,128)(2,1)S(1)} collective-permute-done((bf16[512,512]{1,0:T(8,128)(2,1)}, bf16[512,512]{1,0:T(8,128)(2,1)S(1)}, u32[]{:S(2)}, u32[]{:S(2)}) %collective-permute-start.36) | collective-permute-done | bytes 524320 | tf_op jit(solution)/shard_map/ppermute | solution.py:266
  601.5 3.7 convolution_convert_fusion.4
  608.7 11.7 %collective-permute-done.39 = bf16[512,768]{1,0:T(8,128)(2,1)S(1)} collective-permute-done((bf16[512,768]{1,0:T(8,128)(2,1)S(1)}, bf16[512,768]{1,0:T(8,128)(2,1)S(1)}, u32[]{:S(2)}, u32[]{:S(2)}) %collective-permute-start.39) | collective-permute-done | bytes 786464 | tf_op jit(solution)/shard_map/ppermute | solution.py:327
  623.7 5.5 collective-permute-done.41.refs_6_
  629.2 64.7 %collect.7 = bf16[2048,512]{1,0:T(8,128)(2,1)} custom-call(s32[1]{0:T(128)} %bitcast.chip_ref, bf16[512,512]{1,0:T(8,128)(2,1)} %get-tuple-element.300.refs_0_, bf16[512,512]{1,0:T(8,128)(2,1)} %collective-permute-done.26.refs_1_, bf16[512,512]{1,0:T(8,128)(2,1)} %copy-done.38, bf16[512,512]{1,0:T(8,128)(2,1)} %copy-done.40, ...), custom_call_target="tpu_custom_call" | custom-call | bytes 4194304 | tf_op jit(solution)/shard_map/collect/pallas_call | solution.py:207
  693.9 6.9 add_convert_fusion.2
  704.5 3.6 fusion.36
  708.2 5.7 add_convert_fusion.1
  713.8 3.8 fusion.37
  717.7 3.4 fusion.38
  726.7 6.1 attend_backward.3
  732.8 5.0 collective-permute-done.45
  739.1 4.1 convolution_convert_fusion.1
  743.4 5.5 collective-permute-start.48
  750.2 4.2 convolution_convert_fusion
  754.4 2.9 add_convert_fusion
  757.4 4.6 collective-permute-start.50
  767.1 11.5 %collective-permute-done.50 = bf16[512,768]{1,0:T(8,128)(2,1)S(1)} collective-permute-done((bf16[512,768]{1,0:T(8,128)(2,1)S(1)}, bf16[512,768]{1,0:T(8,128)(2,1)S(1)}, u32[]{:S(2)}, u32[]{:S(2)}) %collective-permute-start.50) | collective-permute-done | bytes 786464 | tf_op jit(solution)/shard_map/ppermute | solution.py:326
  779.1 4.4 collective-permute-start.52
  784.3 15.1 %collective-permute-done.52 = bf16[512,768]{1,0:T(8,128)(2,1)S(1)} collective-permute-done((bf16[512,768]{1,0:T(8,128)(2,1)S(1)}, bf16[512,768]{1,0:T(8,128)(2,1)S(1)}, u32[]{:S(2)}, u32[]{:S(2)}) %collective-permute-start.52) | collective-permute-done | bytes 786464 | tf_op jit(solution)/shard_map/ppermute | solution.py:326
  801.0 8.3 collective-permute-start.54
  820.5 3.1 collective-permute-done.54
  823.6 5.1 collective-permute-done.55
  (221 shorter events, 125.4 us)
Async XLA Ops:
  7.2 826.4 %reduce-scatter.3.cloned.1.call-start = ((), (), s32[]{:S(2)}) async-start(), calls=%async_computation.2 | async-start | bytes 3932160 | tf_op jit(solution)/shard_map/reduce_scatter | solution.py:421
  10.4 22.0 %collective-permute-start = (bf16[512,768]{1,0:T(8,128)(2,1)}, bf16[512,768]{1,0:T(8,128)(2,1)}, u32[]{:S(2)}, u32[]{:S(2)}) collective-permute-start(bf16[512,768]{1,0:T(8,128)(2,1)} %pad_maximum_fusion.2.refs_0_), channel_id=1, source_target_pairs={{0,8},{4,12},{8,16},{12,20},{16,24},{20,28},{1,9},{5,13},{9,17},{1... | collective-permute-start | bytes 2359304 | tf_op jit(solution)/shard_map/ppermute | solution.py:263
  16.2 21.2 %collective-permute-start.1 = (bf16[512,768]{1,0:T(8,128)(2,1)}, bf16[512,768]{1,0:T(8,128)(2,1)}, u32[]{:S(2)}, u32[]{:S(2)}) collective-permute-start(bf16[512,768]{1,0:T(8,128)(2,1)} %pad_maximum_fusion.2.refs_0_), channel_id=1, source_target_pairs={{8,0},{12,4},{16,8},{20,12},{24,16},{28,20},{9,1},{13,5},{17,9},{2... | collective-permute-start | bytes 2359304 | tf_op jit(solution)/shard_map/ppermute | solution.py:266
  20.3 43.3 %copy-start.31 = (bf16[512,1024]{1,0:T(8,128)(2,1)S(1)}, bf16[512,1024]{1,0:T(8,128)(2,1)}, u32[]{:S(2)}) copy-start(bf16[512,1024]{1,0:T(8,128)(2,1)} %param.12) | copy-start | bytes 3145732
  31.6 157.8 %copy-start.1 = (bf16[768,2048]{1,0:T(8,128)(2,1)}, bf16[768,2048]{1,0:T(8,128)(2,1)S(1)}, u32[]{:S(2)}) copy-start(bf16[768,2048]{1,0:T(8,128)(2,1)S(1)} %get-tuple-element.329) | copy-start | bytes 9437188
  37.4 2.9 collective-permute-start.2
  39.0 21.8 %collective-permute-start.3 = (bf16[512,768]{1,0:T(8,128)(2,1)}, bf16[512,768]{1,0:T(8,128)(2,1)}, u32[]{:S(2)}, u32[]{:S(2)}) collective-permute-start(bf16[512,768]{1,0:T(8,128)(2,1)} %collective-permute-done.1.refs_4_), channel_id=1, source_target_pairs={{8,0},{12,4},{16,8},{20,12},{9,1},{13,5},{17,9},{21,13},{10,2},{14... | collective-permute-start | bytes 2359304 | tf_op jit(solution)/shard_map/ppermute | solution.py:266
  60.8 32.1 %collective-permute-start.6 = (bf16[512,768]{1,0:T(8,128)(2,1)}, bf16[512,768]{1,0:T(8,128)(2,1)}, u32[]{:S(2)}, u32[]{:S(2)}) collective-permute-start(bf16[512,768]{1,0:T(8,128)(2,1)} %collective-permute-done.2.refs_2_), channel_id=1, source_target_pairs={{16,24},{20,28},{17,25},{21,29},{18,26},{22,30},{19,27},{23,31}} | collective-permute-start | bytes 2359304 | tf_op jit(solution)/shard_map/ppermute | solution.py:263
  62.3 30.6 %collective-permute-start.7 = (bf16[512,768]{1,0:T(8,128)(2,1)}, bf16[512,768]{1,0:T(8,128)(2,1)}, u32[]{:S(2)}, u32[]{:S(2)}) collective-permute-start(bf16[512,768]{1,0:T(8,128)(2,1)} %collective-permute-done.3.refs_5_), channel_id=1, source_target_pairs={{8,0},{12,4},{9,1},{13,5},{10,2},{14,6},{11,3},{15,7}} | collective-permute-start | bytes 2359304 | tf_op jit(solution)/shard_map/ppermute | solution.py:266
  64.7 14.5 %collective-permute-start.4 = (bf16[512,512]{1,0:T(8,128)(2,1)}, bf16[512,512]{1,0:T(8,128)(2,1)}, u32[]{:S(2)}, u32[]{:S(2)}) collective-permute-start(bf16[512,512]{1,0:T(8,128)(2,1)} %get-tuple-element.222.refs_0_), channel_id=1, source_target_pairs={{0,8},{4,12},{8,16},{12,20},{16,24},{20,28},{1,9},{5,13},{9,17},{1... | collective-permute-start | bytes 1572872 | tf_op jit(solution)/shard_map/ppermute | solution.py:263
  70.9 22.0 %collective-permute-start.5 = (bf16[512,512]{1,0:T(8,128)(2,1)}, bf16[512,512]{1,0:T(8,128)(2,1)}, u32[]{:S(2)}, u32[]{:S(2)}) collective-permute-start(bf16[512,512]{1,0:T(8,128)(2,1)} %get-tuple-element.222.refs_0_), channel_id=1, source_target_pairs={{8,0},{12,4},{16,8},{20,12},{24,16},{28,20},{9,1},{13,5},{17,9},{2... | collective-permute-start | bytes 1572872 | tf_op jit(solution)/shard_map/ppermute | solution.py:266
  189.4 5.9 collective-permute-start.8
  206.7 24.8 %collective-permute-start.9 = (bf16[2048,512]{1,0:T(8,128)(2,1)}, bf16[2048,512]{1,0:T(8,128)(2,1)}, u32[]{:S(2)}, u32[]{:S(2)}) collective-permute-start(bf16[2048,512]{1,0:T(8,128)(2,1)} %convolution_convert_fusion.7), channel_id=1, source_target_pairs={{0,4},{4,0},{8,12},{12,8},{16,20},{20,16},{24,28},{28,24},{1,5},{5... | collective-permute-start | bytes 6291464 | tf_op jit(solution)/shard_map/ppermute | solution.py:242
  206.8 8.8 %collective-permute-start.10 = (bf16[512,512]{1,0:T(8,128)(2,1)}, bf16[512,512]{1,0:T(8,128)(2,1)}, u32[]{:S(2)}, u32[]{:S(2)}) collective-permute-start(bf16[512,512]{1,0:T(8,128)(2,1)} %collective-permute-done.4.refs_1_), channel_id=1, source_target_pairs={{8,16},{12,20},{16,24},{20,28},{9,17},{13,21},{17,25},{21,29},{10,... | collective-permute-start | bytes 1572872 | tf_op jit(solution)/shard_map/ppermute | solution.py:263
  208.3 17.0 %collective-permute-start.11 = (bf16[512,512]{1,0:T(8,128)(2,1)}, bf16[512,512]{1,0:T(8,128)(2,1)}, u32[]{:S(2)}, u32[]{:S(2)}) collective-permute-start(bf16[512,512]{1,0:T(8,128)(2,1)} %collective-permute-done.5.refs_4_), channel_id=1, source_target_pairs={{8,0},{12,4},{16,8},{20,12},{9,1},{13,5},{17,9},{21,13},{10,2},{14... | collective-permute-start | bytes 1572872 | tf_op jit(solution)/shard_map/ppermute | solution.py:266
  209.7 21.8 %copy-start.27 = (bf16[512,768]{1,0:T(8,128)(2,1)}, bf16[512,768]{1,0:T(8,128)(2,1)S(1)}, u32[]{:S(2)}) copy-start(bf16[512,768]{1,0:T(8,128)(2,1)S(1)} %pad_maximum_fusion.3.refs_0_) | copy-start | bytes 2359300
  209.7 43.0 %collective-permute-start.14 = (bf16[512,768]{1,0:T(8,128)(2,1)S(1)}, bf16[512,768]{1,0:T(8,128)(2,1)S(1)}, u32[]{:S(2)}, u32[]{:S(2)}) collective-permute-start(bf16[512,768]{1,0:T(8,128)(2,1)S(1)} %pad_maximum_fusion.3.refs_0_), channel_id=1, source_target_pairs={{0,8},{4,12},{8,16},{12,20},{16,24},{20,28},{1,9},{5,13},{9,17},{1... | collective-permute-start | bytes 2359304 | tf_op jit(solution)/shard_map/ppermute | solution.py:263
  214.3 39.2 %collective-permute-start.15 = (bf16[512,768]{1,0:T(8,128)(2,1)S(1)}, bf16[512,768]{1,0:T(8,128)(2,1)S(1)}, u32[]{:S(2)}, u32[]{:S(2)}) collective-permute-start(bf16[512,768]{1,0:T(8,128)(2,1)S(1)} %pad_maximum_fusion.3.refs_0_), channel_id=1, source_target_pairs={{8,0},{12,4},{16,8},{20,12},{24,16},{28,20},{9,1},{13,5},{17,9},{2... | collective-permute-start | bytes 2359304 | tf_op jit(solution)/shard_map/ppermute | solution.py:266
  225.2 10.8 %collective-permute-start.12 = (bf16[512,512]{1,0:T(8,128)(2,1)}, bf16[512,512]{1,0:T(8,128)(2,1)S(1)}, u32[]{:S(2)}, u32[]{:S(2)}) collective-permute-start(bf16[512,512]{1,0:T(8,128)(2,1)} %collective-permute-done.10.refs_2_), channel_id=1, source_target_pairs={{16,24},{20,28},{17,25},{21,29},{18,26},{22,30},{19,27},{23,31}} | collective-permute-start | bytes 1572872 | tf_op jit(solution)/shard_map/ppermute | solution.py:263
  225.9 26.7 %collective-permute-start.13 = (bf16[512,512]{1,0:T(8,128)(2,1)}, bf16[512,512]{1,0:T(8,128)(2,1)S(1)}, u32[]{:S(2)}, u32[]{:S(2)}) collective-permute-start(bf16[512,512]{1,0:T(8,128)(2,1)} %collective-permute-done.11.refs_5_), channel_id=1, source_target_pairs={{8,0},{12,4},{9,1},{13,5},{10,2},{14,6},{11,3},{15,7}} | collective-permute-start | bytes 1572872 | tf_op jit(solution)/shard_map/ppermute | solution.py:266
  253.5 98.4 %copy-start.32 = (bf16[512,768]{1,0:T(8,128)(2,1)}, bf16[512,768]{1,0:T(8,128)(2,1)S(1)}, u32[]{:S(2)}) copy-start(bf16[512,768]{1,0:T(8,128)(2,1)S(1)} %collective-permute-done.14.refs_1_) | copy-start | bytes 2359300
  253.5 99.1 %copy-start.33 = (bf16[512,768]{1,0:T(8,128)(2,1)}, bf16[512,768]{1,0:T(8,128)(2,1)S(1)}, u32[]{:S(2)}) copy-start(bf16[512,768]{1,0:T(8,128)(2,1)S(1)} %collective-permute-done.15.refs_4_) | copy-start | bytes 2359300
  318.2 7.0 collective-permute-start.16
  318.3 13.7 %collective-permute-start.17 = (bf16[512,512]{1,0:T(8,128)(2,1)}, bf16[512,512]{1,0:T(8,128)(2,1)S(1)}, u32[]{:S(2)}, u32[]{:S(2)}) collective-permute-start(bf16[512,512]{1,0:T(8,128)(2,1)} %get-tuple-element.218), channel_id=1, source_target_pairs={{0,8},{4,12},{1,9},{5,13},{2,10},{6,14},{3,11},{7,15}} | collective-permute-start | bytes 1572872 | tf_op jit(solution)/shard_map/ppermute | solution.py:326
  319.9 12.1 %collective-permute-start.18 = (bf16[512,512]{1,0:T(8,128)(2,1)}, bf16[512,512]{1,0:T(8,128)(2,1)S(1)}, u32[]{:S(2)}, u32[]{:S(2)}) collective-permute-start(bf16[512,512]{1,0:T(8,128)(2,1)} %get-tuple-element.374), channel_id=1, source_target_pairs={{24,16},{28,20},{25,17},{29,21},{26,18},{30,22},{27,19},{31,23}} | collective-permute-start | bytes 1572872 | tf_op jit(solution)/shard_map/ppermute | solution.py:327
  332.3 15.3 %collective-permute-start.19 = (bf16[512,512]{1,0:T(8,128)(2,1)S(1)}, bf16[512,512]{1,0:T(8,128)(2,1)S(1)}, u32[]{:S(2)}, u32[]{:S(2)}) collective-permute-start(bf16[512,512]{1,0:T(8,128)(2,1)S(1)} %get-tuple-element.373), channel_id=1, source_target_pairs={{0,8},{4,12},{8,16},{12,20},{1,9},{5,13},{9,17},{13,21},{2,10},{6,... | collective-permute-start | bytes 1572872 | tf_op jit(solution)/shard_map/ppermute | solution.py:326
  336.6 11.0 %collective-permute-start.20 = (bf16[512,512]{1,0:T(8,128)(2,1)S(1)}, bf16[512,512]{1,0:T(8,128)(2,1)S(1)}, u32[]{:S(2)}, u32[]{:S(2)}) collective-permute-start(bf16[512,512]{1,0:T(8,128)(2,1)S(1)} %get-tuple-element.372), channel_id=1, source_target_pairs={{16,8},{20,12},{24,16},{28,20},{17,9},{21,13},{25,17},{29,21},{18,... | collective-permute-start | bytes 1572872 | tf_op jit(solution)/shard_map/ppermute | solution.py:327
  351.8 5.7 collective-permute-start.21
  351.9 9.5 %collective-permute-start.28 = (bf16[512,768]{1,0:T(8,128)(2,1)S(1)}, bf16[512,768]{1,0:T(8,128)(2,1)S(1)}, u32[]{:S(2)}, u32[]{:S(2)}) collective-permute-start(bf16[512,768]{1,0:T(8,128)(2,1)S(1)} %collective-permute-done.14.refs_1_), channel_id=1, source_target_pairs={{8,16},{12,20},{16,24},{20,28},{9,17},{13,21},{17,25},{21,29},{10,... | collective-permute-start | bytes 2359304 | tf_op jit(solution)/shard_map/ppermute | solution.py:263
  352.6 25.1 %collective-permute-start.29 = (bf16[512,768]{1,0:T(8,128)(2,1)S(1)}, bf16[512,768]{1,0:T(8,128)(2,1)S(1)}, u32[]{:S(2)}, u32[]{:S(2)}) collective-permute-start(bf16[512,768]{1,0:T(8,128)(2,1)S(1)} %collective-permute-done.15.refs_4_), channel_id=1, source_target_pairs={{8,0},{12,4},{16,8},{20,12},{9,1},{13,5},{17,9},{21,13},{10,2},{14... | collective-permute-start | bytes 2359304 | tf_op jit(solution)/shard_map/ppermute | solution.py:266
  377.7 120.9 %copy-start.23 = (bf16[2048,512]{1,0:T(8,128)(2,1)S(1)}, bf16[2048,512]{1,0:T(8,128)(2,1)}, u32[]{:S(2)}) copy-start(bf16[2048,512]{1,0:T(8,128)(2,1)} %collect.5) | copy-start | bytes 6291460
  377.7 2.3 collective-permute-start.30
  378.6 21.4 %collective-permute-start.31 = (bf16[512,768]{1,0:T(8,128)(2,1)S(1)}, bf16[512,768]{1,0:T(8,128)(2,1)}, u32[]{:S(2)}, u32[]{:S(2)}) collective-permute-start(bf16[512,768]{1,0:T(8,128)(2,1)S(1)} %collective-permute-done.29.refs_5_), channel_id=1, source_target_pairs={{8,0},{12,4},{9,1},{13,5},{10,2},{14,6},{11,3},{15,7}} | collective-permute-start | bytes 2359304 | tf_op jit(solution)/shard_map/ppermute | solution.py:266
  496.4 27.9 %collective-permute-start.32 = (bf16[2048,768]{1,0:T(8,128)(2,1)}, bf16[2048,768]{1,0:T(8,128)(2,1)S(1)}, u32[]{:S(2)}, u32[]{:S(2)}) collective-permute-start(bf16[2048,768]{1,0:T(8,128)(2,1)} %collect.6), channel_id=1, source_target_pairs={{0,4},{4,0},{8,12},{12,8},{16,20},{20,16},{24,28},{28,24},{1,5},{5... | collective-permute-start | bytes 9437192 | tf_op jit(solution)/shard_map/ppermute | solution.py:242
  496.5 19.3 %collective-permute-start.22 = (bf16[512,768]{1,0:T(8,128)(2,1)}, bf16[512,768]{1,0:T(8,128)(2,1)S(1)}, u32[]{:S(2)}, u32[]{:S(2)}) collective-permute-start(bf16[512,768]{1,0:T(8,128)(2,1)} %get-tuple-element.363), channel_id=1, source_target_pairs={{0,8},{4,12},{1,9},{5,13},{2,10},{6,14},{3,11},{7,15}} | collective-permute-start | bytes 2359304 | tf_op jit(solution)/shard_map/ppermute | solution.py:326
  497.9 17.9 %collective-permute-start.23 = (bf16[512,768]{1,0:T(8,128)(2,1)}, bf16[512,768]{1,0:T(8,128)(2,1)S(1)}, u32[]{:S(2)}, u32[]{:S(2)}) collective-permute-start(bf16[512,768]{1,0:T(8,128)(2,1)} %get-tuple-element.362), channel_id=1, source_target_pairs={{24,16},{28,20},{25,17},{29,21},{26,18},{30,22},{27,19},{31,23}} | collective-permute-start | bytes 2359304 | tf_op jit(solution)/shard_map/ppermute | solution.py:327
  516.3 21.1 %collective-permute-start.33 = (bf16[512,768]{1,0:T(8,128)(2,1)S(1)}, bf16[512,768]{1,0:T(8,128)(2,1)S(1)}, u32[]{:S(2)}, u32[]{:S(2)}) collective-permute-start(bf16[512,768]{1,0:T(8,128)(2,1)S(1)} %get-tuple-element.361), channel_id=1, source_target_pairs={{0,8},{4,12},{8,16},{12,20},{1,9},{5,13},{9,17},{13,21},{2,10},{6,... | collective-permute-start | bytes 2359304 | tf_op jit(solution)/shard_map/ppermute | solution.py:326
  520.6 16.7 %collective-permute-start.34 = (bf16[512,768]{1,0:T(8,128)(2,1)S(1)}, bf16[512,768]{1,0:T(8,128)(2,1)S(1)}, u32[]{:S(2)}, u32[]{:S(2)}) collective-permute-start(bf16[512,768]{1,0:T(8,128)(2,1)S(1)} %get-tuple-element.360), channel_id=1, source_target_pairs={{16,8},{20,12},{24,16},{28,20},{17,9},{21,13},{25,17},{29,21},{18,... | collective-permute-start | bytes 2359304 | tf_op jit(solution)/shard_map/ppermute | solution.py:327
  547.1 58.2 %collective-permute-start.37 = (bf16[2048,512]{1,0:T(8,128)(2,1)}, bf16[2048,512]{1,0:T(8,128)(2,1)}, u32[]{:S(2)}, u32[]{:S(2)}) collective-permute-start(bf16[2048,512]{1,0:T(8,128)(2,1)} %convolution_convert_fusion.5), channel_id=1, source_target_pairs={{0,4},{4,0},{8,12},{12,8},{16,20},{20,16},{24,28},{28,24},{1,5},{5... | collective-permute-start | bytes 6291464 | tf_op jit(solution)/shard_map/ppermute | solution.py:242
  547.1 19.1 %collective-permute-start.24 = (bf16[512,512]{1,0:T(8,128)(2,1)}, bf16[512,512]{1,0:T(8,128)(2,1)}, u32[]{:S(2)}, u32[]{:S(2)}) collective-permute-start(bf16[512,512]{1,0:T(8,128)(2,1)} %get-tuple-element.371), channel_id=1, source_target_pairs={{0,8},{4,12},{8,16},{12,20},{16,24},{20,28},{1,9},{5,13},{9,17},{1... | collective-permute-start | bytes 1572872 | tf_op jit(solution)/shard_map/ppermute | solution.py:326
  554.5 17.0 %collective-permute-start.25 = (bf16[512,512]{1,0:T(8,128)(2,1)}, bf16[512,512]{1,0:T(8,128)(2,1)}, u32[]{:S(2)}, u32[]{:S(2)}) collective-permute-start(bf16[512,512]{1,0:T(8,128)(2,1)} %get-tuple-element.370), channel_id=1, source_target_pairs={{8,0},{12,4},{16,8},{20,12},{24,16},{28,20},{9,1},{13,5},{17,9},{2... | collective-permute-start | bytes 1572872 | tf_op jit(solution)/shard_map/ppermute | solution.py:327
  555.8 21.2 %collective-permute-start.26 = (bf16[512,512]{1,0:T(8,128)(2,1)S(1)}, bf16[512,512]{1,0:T(8,128)(2,1)}, u32[]{:S(2)}, u32[]{:S(2)}) collective-permute-start(bf16[512,512]{1,0:T(8,128)(2,1)S(1)} %copy-done.29), channel_id=1, source_target_pairs={{0,8},{4,12},{8,16},{12,20},{16,24},{20,28},{1,9},{5,13},{9,17},{1... | collective-permute-start | bytes 1572872 | tf_op jit(solution)/shard_map/ppermute | solution.py:263
  561.1 20.8 %collective-permute-start.27 = (bf16[512,512]{1,0:T(8,128)(2,1)S(1)}, bf16[512,512]{1,0:T(8,128)(2,1)}, u32[]{:S(2)}, u32[]{:S(2)}) collective-permute-start(bf16[512,512]{1,0:T(8,128)(2,1)S(1)} %copy-done.29), channel_id=1, source_target_pairs={{8,0},{12,4},{16,8},{20,12},{24,16},{28,20},{9,1},{13,5},{17,9},{2... | collective-permute-start | bytes 1572872 | tf_op jit(solution)/shard_map/ppermute | solution.py:266
  582.0 6.6 collective-permute-start.35
  582.7 15.3 %collective-permute-start.36 = (bf16[512,512]{1,0:T(8,128)(2,1)}, bf16[512,512]{1,0:T(8,128)(2,1)S(1)}, u32[]{:S(2)}, u32[]{:S(2)}) collective-permute-start(bf16[512,512]{1,0:T(8,128)(2,1)} %collective-permute-done.27.refs_4_), channel_id=1, source_target_pairs={{8,0},{12,4},{16,8},{20,12},{9,1},{13,5},{17,9},{21,13},{10,2},{14... | collective-permute-start | bytes 1572872 | tf_op jit(solution)/shard_map/ppermute | solution.py:266
  584.0 24.7 %collective-permute-start.38 = (bf16[512,768]{1,0:T(8,128)(2,1)S(1)}, bf16[512,768]{1,0:T(8,128)(2,1)S(1)}, u32[]{:S(2)}, u32[]{:S(2)}) collective-permute-start(bf16[512,768]{1,0:T(8,128)(2,1)S(1)} %copy-done.34), channel_id=1, source_target_pairs={{0,8},{4,12},{8,16},{12,20},{16,24},{20,28},{1,9},{5,13},{9,17},{1... | collective-permute-start | bytes 2359304 | tf_op jit(solution)/shard_map/ppermute | solution.py:326
  598.0 22.4 %collective-permute-start.39 = (bf16[512,768]{1,0:T(8,128)(2,1)S(1)}, bf16[512,768]{1,0:T(8,128)(2,1)S(1)}, u32[]{:S(2)}, u32[]{:S(2)}) collective-permute-start(bf16[512,768]{1,0:T(8,128)(2,1)S(1)} %get-tuple-element.358), channel_id=1, source_target_pairs={{8,0},{12,4},{16,8},{20,12},{24,16},{28,20},{9,1},{13,5},{17,9},{2... | collective-permute-start | bytes 2359304 | tf_op jit(solution)/shard_map/ppermute | solution.py:327
  599.3 23.6 %collective-permute-start.40 = (bf16[512,512]{1,0:T(8,128)(2,1)S(1)}, bf16[512,512]{1,0:T(8,128)(2,1)S(1)}, u32[]{:S(2)}, u32[]{:S(2)}) collective-permute-start(bf16[512,512]{1,0:T(8,128)(2,1)S(1)} %collective-permute-done.35.refs_2_), channel_id=1, source_target_pairs={{16,24},{20,28},{17,25},{21,29},{18,26},{22,30},{19,27},{23,31}} | collective-permute-start | bytes 1572872 | tf_op jit(solution)/shard_map/ppermute | solution.py:263
  600.0 29.2 %collective-permute-start.41 = (bf16[512,512]{1,0:T(8,128)(2,1)S(1)}, bf16[512,512]{1,0:T(8,128)(2,1)}, u32[]{:S(2)}, u32[]{:S(2)}) collective-permute-start(bf16[512,512]{1,0:T(8,128)(2,1)S(1)} %collective-permute-done.36.refs_5_), channel_id=1, source_target_pairs={{8,0},{12,4},{9,1},{13,5},{10,2},{14,6},{11,3},{15,7}} | collective-permute-start | bytes 1572872 | tf_op jit(solution)/shard_map/ppermute | solution.py:266
  693.8 10.7 %collective-permute-start.42 = (bf16[2048,512]{1,0:T(8,128)(2,1)}, bf16[2048,512]{1,0:T(8,128)(2,1)}, u32[]{:S(2)}, u32[]{:S(2)}) collective-permute-start(bf16[2048,512]{1,0:T(8,128)(2,1)} %collect.7), channel_id=1, source_target_pairs={{0,4},{4,0},{8,12},{12,8},{16,20},{20,16},{24,28},{28,24},{1,5},{5... | collective-permute-start | bytes 6291464 | tf_op jit(solution)/shard_map/ppermute | solution.py:242
  700.9 132.7 %reduce-scatter.5.cloned.1.call-start = ((), (), s32[]{:S(2)}) async-start(), calls=%async_computation.3 | async-start | bytes 3932160 | tf_op jit(solution)/shard_map/reduce_scatter | solution.py:421
  700.9 20.6 %collective-permute-start.43 = (bf16[512,512]{1,0:T(8,128)(2,1)}, bf16[512,512]{1,0:T(8,128)(2,1)}, u32[]{:S(2)}, u32[]{:S(2)}) collective-permute-start(bf16[512,512]{1,0:T(8,128)(2,1)} %get-tuple-element.369), channel_id=1, source_target_pairs={{0,8},{4,12},{1,9},{5,13},{2,10},{6,14},{3,11},{7,15}} | collective-permute-start | bytes 1572872 | tf_op jit(solution)/shard_map/ppermute | solution.py:326
  703.1 18.5 %collective-permute-start.44 = (bf16[512,512]{1,0:T(8,128)(2,1)}, bf16[512,512]{1,0:T(8,128)(2,1)}, u32[]{:S(2)}, u32[]{:S(2)}) collective-permute-start(bf16[512,512]{1,0:T(8,128)(2,1)} %get-tuple-element.368), channel_id=1, source_target_pairs={{24,16},{28,20},{25,17},{29,21},{26,18},{30,22},{27,19},{31,23}} | collective-permute-start | bytes 1572872 | tf_op jit(solution)/shard_map/ppermute | solution.py:327
  724.3 13.5 %collective-permute-start.45 = (bf16[512,512]{1,0:T(8,128)(2,1)S(1)}, bf16[512,512]{1,0:T(8,128)(2,1)S(1)}, u32[]{:S(2)}, u32[]{:S(2)}) collective-permute-start(bf16[512,512]{1,0:T(8,128)(2,1)S(1)} %get-tuple-element.367), channel_id=1, source_target_pairs={{0,8},{4,12},{8,16},{12,20},{1,9},{5,13},{9,17},{13,21},{2,10},{6,... | collective-permute-start | bytes 1572872 | tf_op jit(solution)/shard_map/ppermute | solution.py:326
  725.6 12.2 %collective-permute-start.46 = (bf16[512,512]{1,0:T(8,128)(2,1)S(1)}, bf16[512,512]{1,0:T(8,128)(2,1)S(1)}, u32[]{:S(2)}, u32[]{:S(2)}) collective-permute-start(bf16[512,512]{1,0:T(8,128)(2,1)S(1)} %get-tuple-element.366), channel_id=1, source_target_pairs={{16,8},{20,12},{24,16},{28,20},{17,9},{21,13},{25,17},{29,21},{18,... | collective-permute-start | bytes 1572872 | tf_op jit(solution)/shard_map/ppermute | solution.py:327
  743.2 11.2 %collective-permute-start.47 = (bf16[2048,768]{1,0:T(8,128)(2,1)}, bf16[2048,768]{1,0:T(8,128)(2,1)}, u32[]{:S(2)}, u32[]{:S(2)}) collective-permute-start(bf16[2048,768]{1,0:T(8,128)(2,1)} %convolution_convert_fusion.1), channel_id=1, source_target_pairs={{0,4},{4,0},{8,12},{12,8},{16,20},{20,16},{24,28},{28,24},{1,5},{5... | collective-permute-start | bytes 9437192 | tf_op jit(solution)/shard_map/ppermute | solution.py:242
  743.4 19.3 %collective-permute-start.48 = (bf16[512,512]{1,0:T(8,128)(2,1)}, bf16[512,512]{1,0:T(8,128)(2,1)S(1)}, u32[]{:S(2)}, u32[]{:S(2)}) collective-permute-start(bf16[512,512]{1,0:T(8,128)(2,1)} %get-tuple-element.365), channel_id=1, source_target_pairs={{0,8},{4,12},{8,16},{12,20},{16,24},{20,28},{1,9},{5,13},{9,17},{1... | collective-permute-start | bytes 1572872 | tf_op jit(solution)/shard_map/ppermute | solution.py:326
  748.9 16.0 %collective-permute-start.49 = (bf16[512,512]{1,0:T(8,128)(2,1)}, bf16[512,512]{1,0:T(8,128)(2,1)S(1)}, u32[]{:S(2)}, u32[]{:S(2)}) collective-permute-start(bf16[512,512]{1,0:T(8,128)(2,1)} %get-tuple-element.364), channel_id=1, source_target_pairs={{8,0},{12,4},{16,8},{20,12},{24,16},{28,20},{9,1},{13,5},{17,9},{2... | collective-permute-start | bytes 1572872 | tf_op jit(solution)/shard_map/ppermute | solution.py:327
  757.4 21.3 %collective-permute-start.50 = (bf16[512,768]{1,0:T(8,128)(2,1)S(1)}, bf16[512,768]{1,0:T(8,128)(2,1)S(1)}, u32[]{:S(2)}, u32[]{:S(2)}) collective-permute-start(bf16[512,768]{1,0:T(8,128)(2,1)S(1)} %get-tuple-element.357), channel_id=1, source_target_pairs={{0,8},{4,12},{1,9},{5,13},{2,10},{6,14},{3,11},{7,15}} | collective-permute-start | bytes 2359304 | tf_op jit(solution)/shard_map/ppermute | solution.py:326
  762.0 16.7 %collective-permute-start.51 = (bf16[512,768]{1,0:T(8,128)(2,1)S(1)}, bf16[512,768]{1,0:T(8,128)(2,1)S(1)}, u32[]{:S(2)}, u32[]{:S(2)}) collective-permute-start(bf16[512,768]{1,0:T(8,128)(2,1)S(1)} %get-tuple-element.356), channel_id=1, source_target_pairs={{24,16},{28,20},{25,17},{29,21},{26,18},{30,22},{27,19},{31,23}} | collective-permute-start | bytes 2359304 | tf_op jit(solution)/shard_map/ppermute | solution.py:327
  779.1 20.3 %collective-permute-start.52 = (bf16[512,768]{1,0:T(8,128)(2,1)S(1)}, bf16[512,768]{1,0:T(8,128)(2,1)S(1)}, u32[]{:S(2)}, u32[]{:S(2)}) collective-permute-start(bf16[512,768]{1,0:T(8,128)(2,1)S(1)} %get-tuple-element.355), channel_id=1, source_target_pairs={{0,8},{4,12},{8,16},{12,20},{1,9},{5,13},{9,17},{13,21},{2,10},{6,... | collective-permute-start | bytes 2359304 | tf_op jit(solution)/shard_map/ppermute | solution.py:326
  783.6 15.8 %collective-permute-start.53 = (bf16[512,768]{1,0:T(8,128)(2,1)S(1)}, bf16[512,768]{1,0:T(8,128)(2,1)S(1)}, u32[]{:S(2)}, u32[]{:S(2)}) collective-permute-start(bf16[512,768]{1,0:T(8,128)(2,1)S(1)} %get-tuple-element.354), channel_id=1, source_target_pairs={{16,8},{20,12},{24,16},{28,20},{17,9},{21,13},{25,17},{29,21},{18,... | collective-permute-start | bytes 2359304 | tf_op jit(solution)/shard_map/ppermute | solution.py:327
  801.0 22.6 %collective-permute-start.54 = (bf16[512,768]{1,0:T(8,128)(2,1)}, bf16[512,768]{1,0:T(8,128)(2,1)}, u32[]{:S(2)}, u32[]{:S(2)}) collective-permute-start(bf16[512,768]{1,0:T(8,128)(2,1)} %get-tuple-element.353), channel_id=1, source_target_pairs={{0,8},{4,12},{8,16},{12,20},{16,24},{20,28},{1,9},{5,13},{9,17},{1... | collective-permute-start | bytes 2359304 | tf_op jit(solution)/shard_map/ppermute | solution.py:326
  809.3 19.4 %collective-permute-start.55 = (bf16[512,768]{1,0:T(8,128)(2,1)}, bf16[512,768]{1,0:T(8,128)(2,1)}, u32[]{:S(2)}, u32[]{:S(2)}) collective-permute-start(bf16[512,768]{1,0:T(8,128)(2,1)} %get-tuple-element.352), channel_id=1, source_target_pairs={{8,0},{12,4},{16,8},{20,12},{24,16},{28,20},{9,1},{13,5},{17,9},{2... | collective-permute-start | bytes 2359304 | tf_op jit(solution)/shard_map/ppermute | solution.py:327
  (41 other events, 264.8 us)
Sparse Core Ops, SparseCore 0:
  701.0 42.2 reduce-scatter.2
  746.3 43.9 reduce-scatter.4

commit v3 on v2

--- a/solution.py
+++ b/solution.py
@@ -181,40 +181,64 @@
 
 
 def collect_kernel(chips, chip_ref, *refs):
-    own, ups, downs = refs[0], refs[: chips], refs[chips : 2 * chips - 1]
-    out, sems = refs[-2], refs[-1]
-    rows = own.shape[0]
+    ups, downs, out = refs[:chips], refs[chips:-1], refs[-1]
+    rows = ups[0].shape[0]
     chip = chip_ref[0]
 
-    def place(source, r):
-        at = lax.rem(chip - r + chips, chips)
-        to = out.at[pl.ds(pl.multiple_of(at * rows, rows), rows), :]
-        return pltpu.make_async_copy(source, to, sems.at[r])
-
-    for r in range(chips):
-        if r == 0:
-            place(own, r).start()
-            continue
-        pl.when(chip >= r)(lambda r=r: place(ups[r], r).start())
-        pl.when(chip < r)(lambda r=r: place(downs[chips - r - 1], r).start())
-    for r in range(chips):
-        place(own, r).wait()
+    def store(source, at):
+        out[pl.ds(pl.multiple_of(at * rows, rows), rows), :] = source[...]
+
+    store(ups[0], chip)
+    for r in range(1, chips):
+        pl.when(chip >= r)(functools.partial(store, ups[r], chip - r))
+        pl.when(chip < r)(functools.partial(store, downs[chips - r - 1], chip - r + chips))
 
 
 def collect(chip, chips, ups, downs):
     rows, cols = ups[0].shape
-    anywhere = pl.BlockSpec(memory_space=pl.ANY)
+    vmem = pl.BlockSpec(memory_space=pltpu.VMEM)
     return pl.pallas_call(
         functools.partial(collect_kernel, chips),
         out_shape=jax.ShapeDtypeStruct((chips * rows, cols), BF16),
-        in_specs=[pl.BlockSpec(memory_space=pltpu.SMEM)] + [anywhere] * (len(ups) + len(downs)),
-        out_specs=anywhere,
-        scratch_shapes=[pltpu.SemaphoreType.DMA((chips,))],
+        in_specs=[pl.BlockSpec(memory_space=pltpu.SMEM)] + [vmem] * (len(ups) + len(downs)),
+        out_specs=vmem,
+        compiler_params=pltpu.CompilerParams(vmem_limit_bytes=24 * 2**20),
         cost_estimate=pl.CostEstimate(
-            flops=0, bytes_accessed=4 * chips * rows * cols, transcendentals=0
+            flops=0, bytes_accessed=6 * chips * rows * cols, transcendentals=0
         ),
         name="collect",
     )(chip.reshape(1), *ups, *downs)
+
+
+def project_kernel(count, *refs):
+    out = refs[-1]
+    total = None
+    for mixed, side in zip(refs[:count], refs[count : 2 * count]):
+        part = nt(mixed[...], side[...])
+        total = part if total is None else total + part
+    out[...] = total.astype(BF16)
+
+
+def project(mixed, sides):
+    length, span = mixed[0].shape
+    features = sides[0].shape[0]
+    step = 512 if features % 512 == 0 else features
+    count = len(mixed)
+    return pl.pallas_call(
+        functools.partial(project_kernel, count),
+        grid=(features // step,),
+        out_shape=jax.ShapeDtypeStruct((length, features), BF16),
+        in_specs=[pl.BlockSpec((length, span), lambda i: (0, 0))] * count
+        + [pl.BlockSpec((step, span), lambda i: (i, 0))] * count,
+        out_specs=pl.BlockSpec((length, step), lambda i: (0, i)),
+        compiler_params=pltpu.CompilerParams(vmem_limit_bytes=32 * 2**20),
+        cost_estimate=pl.CostEstimate(
+            flops=2 * count * length * span * features,
+            bytes_accessed=4 * length * features,
+            transcendentals=0,
+        ),
+        name="project",
+    )(*mixed, *sides)
 
 
 class Order:
@@ -229,7 +253,9 @@
     def after(self, *operands):
         if self.last is None:
             return operands
-        return lax.optimization_barrier((self.last, *operands))[1:]
+        least = min(range(len(operands)), key=lambda i: operands[i].size)
+        tied = lax.optimization_barrier((self.last, operands[least]))[1]
+        return operands[:least] + (tied,) + operands[least + 1 :]
 
     def wait(self, *arrays):
         if self.last is None:
@@ -365,92 +391,103 @@
         part = order(nn, sides[0], own)
         return order(lambda a, b, c: (c + nn(a, b)).astype(BF16), sides[1], other, part)
 
-    def add_nt(a, b, part):
-        return part + nt(a, b)
-
-    def project(mixed, side, part):
-        if part is None:
-            return order(lambda a, b: nt(a, b).astype(BF16), mixed, side)
-        return order(lambda a, b, c: add_nt(a, b, c).astype(BF16), mixed, side, part)
-
-    def start_sum(sides, grads):
+    def start_sum(sides, grads, between=None):
         line = LineSum(order, chips)
         line.swap(order(term, sides[1], grads))
+        if between is not None:
+            between()
         line.add_cores(order(term, sides[0], grads))
         line.advance()
         return line
 
-    qkv_gather = [LineGather(order, chips, columns(g)) for g in range(groups)]
-    out_gather = [
-        LineGather(order, chips, w_out[:, g * span : (g + 1) * span]) for g in range(groups)
-    ]
+    def scattered(side):
+        sides = [halves[side] for halves in out_weights]
+        part = order(lambda *a: project(a[:groups], a[groups:]), *all_mixed, *sides)
+        return lax.psum_scatter(part, "narrow", scatter_dimension=1, tiled=True)
+
+    gathers = []
+    for g in range(groups):
+        gathers.append(LineGather(order, chips, columns(g)))
+        gathers.append(LineGather(order, chips, w_out[:, g * span : (g + 1) * span]))
+
+    def hop(k):
+        if k < len(gathers):
+            gathers[k].hop()
+
     qkv_sum, out_sum = [], []
-    partial = [None, None]
-
-    qkv_gather[0].hop()
+    all_mixed, out_weights = [], []
+
+    hop(0)
     x_own, x_other, grad_own, grad_other = order(
         lambda a, b, c: norm_and_split(core, a, b, c, chips), activations, gain, cotangent
     )
     x_sides, grad_sides = (x_own, x_other), (grad_own, grad_other)
-    out_gather[0].hop()
-    qkv_gather[0].hop()
-    qkv_gather[0].hop()
-    out_gather[0].hop()
+    hop(0)
+    hop(1)
+    hop(0)
+    hop(1)
     for g in range(groups):
+        a, b = 2 * g, 2 * g + 1
         more = g + 1 < groups
-        qkv_gather[g].finish()
-        if more:
-            qkv_gather[g + 1].hop()
-        own, other = qkv_gather[g].halves()
+        gathers[a].finish()
+        hop(b)
+        hop(a + 2)
+        own, other = gathers[a].halves()
         qkv = product(x_sides, own, other)
         if g:
             qkv_sum[g - 1].advance()
         mixed, lse = order(lambda a: attend_forward(a, members, block), qkv)
-        out_gather[g].hop()
+        all_mixed.append(mixed)
         out_sum.append(start_sum(grad_sides, mixed))
         if g:
+            qkv_sum[g - 1].advance()
+        gathers[b].finish()
+        hop(a + 2)
+        hop(b + 2)
+        out_weights.append(gathers[b].halves())
+        own, other = out_weights[g]
+        if not more:
+            first = scattered(0)
+        grad_mixed = product(grad_sides, own, other)
+        if g:
             qkv_sum[g - 1].finish()
-        out_gather[g].finish()
-        if more:
-            qkv_gather[g + 1].hop()
-            out_gather[g + 1].hop()
-        own, other = out_gather[g].halves()
-        if not more:
-            projected = [project(mixed, side, partial[i]) for i, side in enumerate((own, other))]
-            summed = [
-                lax.psum_scatter(part, "narrow", scatter_dimension=1, tiled=True)
-                for part in projected
-            ]
-        grad_mixed = product(grad_sides, own, other)
         out_sum[g].advance()
         grad_qkv = order(
             lambda a, b, c: attend_backward(a, b, c, members, block), qkv, grad_mixed, lse
         )
-        out_sum[g].advance()
-        qkv_sum.append(start_sum(x_sides, grad_qkv))
+        hop(a + 2)
         if more:
-            qkv_gather[g + 1].hop()
-            partial = [
-                order(nt, mixed, side) if part is None else order(add_nt, mixed, side, part)
-                for side, part in zip((own, other), partial)
-            ]
-            qkv_sum[g].advance()
-            out_sum[g].finish()
-            out_gather[g + 1].hop()
-    out_sum[-1].finish()
+            qkv_sum.append(start_sum(x_sides, grad_qkv, out_sum[g].advance))
+        else:
+            second = []
+            qkv_sum.append(
+                start_sum(x_sides, grad_qkv, lambda: second.append(scattered(1)))
+            )
+            out_sum[g].advance()
+        hop(b + 2)
+        out_sum[g].finish()
+    qkv_sum[-1].advance()
+    grad_out = [line.result for line in out_sum]
+    if groups > 1:
+        grad_out = order(lambda *a: jnp.concatenate(a, axis=1), *grad_out)
+    else:
+        grad_out = grad_out[0]
+    qkv_sum[-1].advance()
+
+    def finish_outputs(activations, own, other):
+        left, right = jnp.where(core == 0, own, other), jnp.where(core == 0, other, own)
+        pieces = []
+        for at in range(0, own.shape[1], rows):
+            pieces += [left[:, at : at + rows], right[:, at : at + rows]]
+        summed = jnp.concatenate(pieces, axis=1)
+        share = summed.shape[1]
+        own_columns = lax.dynamic_slice_in_dim(
+            activations, lax.axis_index("narrow") * share, share, 1
+        )
+        return (own_columns.astype(F32) + summed.astype(F32)).astype(BF16)
+
+    outputs = order(finish_outputs, activations, first, second[0])
     qkv_sum[-1].finish()
-
-    own, other = (part.reshape(length, -1, 1, rows) for part in summed)
-    summed = jnp.where(
-        core == 0,
-        jnp.concatenate([own, other], axis=2),
-        jnp.concatenate([other, own], axis=2),
-    ).reshape(length, -1)
-    share = summed.shape[1]
-    own_columns = lax.dynamic_slice_in_dim(
-        activations, lax.axis_index("narrow") * share, share, 1
-    )
-    outputs = (own_columns.astype(F32) + summed.astype(F32)).astype(BF16)
 
     def joined(pieces):
         return pieces[0] if len(pieces) == 1 else jnp.concatenate(pieces, axis=1)
@@ -458,7 +495,6 @@
     grad_query = joined([s.result[:, :span] for s in qkv_sum])
     grad_key = joined([s.result[:, span : span + width] for s in qkv_sum])
     grad_value = joined([s.result[:, span + width :] for s in qkv_sum])
-    grad_out = joined([s.result for s in out_sum])
     return (outputs, grad_query, grad_key, grad_value, grad_out)
 
 

time: 861 us -> 582 us (0.68)
  Pallas kernels: 351 us -> 47 us
  starting transfers between devices: 110 us -> 157 us
  waiting for transfers between devices: 220 us -> 248 us
  matrix products: 76.8 us -> 49.2 us
  local copies, waits for them, and re-layouts: 32.7 us -> 21.9 us
    pallas_call x4, Pallas kernels: 322 us -> 6.98 us  [collect(): pl.pallas_call(functools.partial(collect_kernel, chips), out_shape=jax.Sh...]
    ppermute x12, waiting for transfers between devices: 62.3 us -> 103 us  [advance(): self.up = lax.ppermute(up, 'wide', [(w, w + 2) for w in range(2 * t)])]
    ppermute x12, starting transfers between devices: 49.8 us -> 80.5 us  [advance(): self.up = lax.ppermute(up, 'wide', [(w, w + 2) for w in range(2 * t)])]
    dot_general x4 -> x0, matrix products: 21.2 us -> none  [nt(): lax.dot_general(a, b, (((1,), (1,)), ((), ())), preferred_element_type=F32)]
    ppermute x12, starting transfers between devices: 30.2 us -> 46.8 us  [hop(): lax.ppermute(up, 'wide', [(w, w + 2) for w in range(2 * (t - 1), 2 * (chi...]
    pallas_call x0 -> x2, Pallas kernels: none -> 11.4 us  [project(): pl.pallas_call(functools.partial(project_kernel, count), grid=(features /...]
    ppermute x12, waiting for transfers between devices: 24.2 us -> 13.4 us  [advance(): lax.ppermute(down, 'wide', [(w, w - 2) for w in range(2 * far, 2 * chips)])]
    unnamed x94 -> x90, local copies, waits for them, and re-layouts: 20.6 us -> 13.6 us
  transfers between devices with their start and end apart: 58 -> 58, of which waited for: 28 -> 25; matrix products, arithmetic and copies ran while one was open for 13% -> 12% of each run, Pallas kernels for 2% -> 4%
where the time goes in v3:
time: 582 us; the launch traced here: 578 us
  waiting for transfers between devices  248 us (43%)
  starting transfers between devices  157 us (27%)
  matrix products  49.2 us (8%)
  Pallas kernels  47 us (8%)
  other arithmetic  39.4 us (7%)
  local copies, waits for them, and re-layouts  21.9 us (4%)
  between operations  15.7 us (3%)
    ppermute x12, waiting for transfers between devices, hop(): lax.ppermute(down, 'wide', [(w, w - 2) for w in range(2, 2 * (chips - t +...  117 us
    ppermute x12, waiting for transfers between devices, advance(): self.up = lax.ppermute(up, 'wide', [(w, w + 2) for w in range(2 * t)])  103 us
    ppermute x12, starting transfers between devices, advance(): self.up = lax.ppermute(up, 'wide', [(w, w + 2) for w in range(2 * t)])  80.5 us
    ppermute x12, starting transfers between devices, hop(): lax.ppermute(up, 'wide', [(w, w + 2) for w in range(2 * (t - 1), 2 * (chi...  46.8 us
    dot_general x8, matrix products, row_product(): lax.dot_general(a, b, (((0,), (0,)), ((), ())), preferred_element_type=F32)  26 us
    dot_general x8, matrix products, nn(): lax.dot_general(a, b, (((1,), (0,)), ((), ())), preferred_element_type=F32)  23.2 us
    ppermute x12, starting transfers between devices, hop(): lax.ppermute(down, 'wide', [(w, w - 2) for w in range(2, 2 * (chips - t +...  15.9 us
    unnamed x90, local copies, waits for them, and re-layouts  13.6 us
  transfers between devices with their start and end apart: 58, of which 25 were waited for; matrix products, arithmetic and copies ran while one was open for 12% of the time, Pallas kernels for 4%

profile of v3, /device:TPU:0, one launch (start us, length us, event | category | flops | bytes accessed | tf_op | source)
XLA Modules:
  0.0 577.5 jit_solution(6136618315479805728)
XLA Ops:
  11.1 5.0 collective-permute-start
  17.5 2.8 copy-done
  20.2 6.1 %norm_and_split.1 = (bf16[768,2048]{1,0:T(8,128)(2,1)S(1)}, bf16[768,2048]{1,0:T(8,128)(2,1)S(1)}, bf16[768,2048]{1,0:T(8,128)(2,1)S(1)}, bf16[768,2048]{1,0:T(8,128)(2,1)S(1)}) custom-call(s32[1]{0:T(128)} %bitcast.core_ref, bf16[768,4096]{1,0:T(8,128)(2,1)S(1)} %copy-done, f32[1,4096]{1,0:T(1,128)S(1)} %bitcast.115, bf16[768,4096]{1,0:T(8,128)(2,1)} %grad_ref.1), custom_call_target="tpu_custom_call" | custom-call | flops 25165824 | bytes 25165824 | tf_op jit(solution)/shard_map/norm_and_split/pallas_call | solution.py:162
  32.9 4.2 collective-permute-done.1.refs_4_
  40.0 7.7 %collective-permute-start.4 = (bf16[512,512]{1,0:T(8,128)(2,1)S(1)}, bf16[512,512]{1,0:T(8,128)(2,1)}, u32[]{:S(2)}, u32[]{:S(2)}) collective-permute-start(bf16[512,512]{1,0:T(8,128)(2,1)S(1)} %get-tuple-element.114.refs_0_), channel_id=1, source_target_pairs={{0,8},{4,12},{8,16},{12,20},{16,24},{20,28},{1,9},{5,13},{9,17},{1... | collective-permute-start | bytes 1572872 | tf_op jit(solution)/shard_map/ppermute | solution.py:289
  49.0 14.4 %collective-permute-done.3.refs_5_ = bf16[512,768]{1,0:T(8,128)(2,1)} collective-permute-done((bf16[512,768]{1,0:T(8,128)(2,1)S(1)}, bf16[512,768]{1,0:T(8,128)(2,1)}, u32[]{:S(2)}, u32[]{:S(2)}) %collective-permute-start.3) | collective-permute-done | bytes 786464 | tf_op jit(solution)/shard_map/ppermute | solution.py:292
  66.2 8.4 %collective-permute-done.5.refs_4_ = bf16[512,512]{1,0:T(8,128)(2,1)} collective-permute-done((bf16[512,512]{1,0:T(8,128)(2,1)S(1)}, bf16[512,512]{1,0:T(8,128)(2,1)}, u32[]{:S(2)}, u32[]{:S(2)}) %collective-permute-start.5) | collective-permute-done | bytes 524320 | tf_op jit(solution)/shard_map/ppermute | solution.py:292
  77.4 14.1 %collective-permute-done.7.refs_6_ = bf16[512,768]{1,0:T(8,128)(2,1)} collective-permute-done((bf16[512,768]{1,0:T(8,128)(2,1)}, bf16[512,768]{1,0:T(8,128)(2,1)}, u32[]{:S(2)}, u32[]{:S(2)}) %collective-permute-start.7) | collective-permute-done | bytes 786464 | tf_op jit(solution)/shard_map/ppermute | solution.py:292
  91.5 8.8 %collective-permute-done.9.refs_5_ = bf16[512,512]{1,0:T(8,128)(2,1)} collective-permute-done((bf16[512,512]{1,0:T(8,128)(2,1)}, bf16[512,512]{1,0:T(8,128)(2,1)}, u32[]{:S(2)}, u32[]{:S(2)}) %collective-permute-start.9) | collective-permute-done | bytes 524320 | tf_op jit(solution)/shard_map/ppermute | solution.py:292
  103.2 2.6 fusion.26
  105.8 2.7 collective-permute-done.10
  108.5 2.6 add_convert_fusion.6.qkv_ref
  111.2 5.2 attend_forward.2
  116.4 3.2 convolution_convert_fusion.7
  126.0 3.7 convolution_convert_fusion.6
  132.9 22.0 %collective-permute-done.13.refs_6_ = bf16[512,512]{1,0:T(8,128)(2,1)S(1)} collective-permute-done((bf16[512,512]{1,0:T(8,128)(2,1)}, bf16[512,512]{1,0:T(8,128)(2,1)S(1)}, u32[]{:S(2)}, u32[]{:S(2)}) %collective-permute-start.13) | collective-permute-done | bytes 524320 | tf_op jit(solution)/shard_map/ppermute | solution.py:292
  158.6 3.7 fusion.27
  162.3 3.5 add_convert_fusion.8.grad_ref
  165.8 5.0 collective-permute-done.17
  172.8 6.0 %attend_backward.2 = bf16[768,768]{1,0:T(8,128)(2,1)S(1)} custom-call(bf16[768,768]{1,0:T(8,128)(2,1)S(1)} %copy-done.29, bf16[768,512]{1,0:T(8,128)(2,1)S(1)} %add_convert_fusion.8.grad_ref, f32[4,768]{1,0:T(4,128)S(1)} %get-tuple-element.120.lse_ref), custom_call_target="tpu_custom_call" | custom-call | flops 6039797760 | bytes 3145728 | tf_op jit(solution)/shard_map/attend_backward/pallas_call | solution.py:118
  178.9 4.1 convolution_convert_fusion.3
  183.0 5.1 collective-permute-start.20
  189.5 9.9 %collective-permute-done.20 = bf16[512,512]{1,0:T(8,128)(2,1)} collective-permute-done((bf16[512,512]{1,0:T(8,128)(2,1)}, bf16[512,512]{1,0:T(8,128)(2,1)}, u32[]{:S(2)}, u32[]{:S(2)}) %collective-permute-start.20) | collective-permute-done | bytes 524320 | tf_op jit(solution)/shard_map/ppermute | solution.py:352
  199.4 2.8 fusion.17
  206.4 9.6 %collective-permute-start.21 = (bf16[512,512]{1,0:T(8,128)(2,1)}, bf16[512,512]{1,0:T(8,128)(2,1)}, u32[]{:S(2)}, u32[]{:S(2)}) collective-permute-start(bf16[512,512]{1,0:T(8,128)(2,1)} %get-tuple-element.173), channel_id=1, source_target_pairs={{0,8},{4,12},{8,16},{12,20},{16,24},{20,28},{1,9},{5,13},{9,17},{1... | collective-permute-start | bytes 1572872 | tf_op jit(solution)/shard_map/ppermute | solution.py:352
  219.5 12.6 %collective-permute-done.19.refs_5_ = bf16[512,768]{1,0:T(8,128)(2,1)} collective-permute-done((bf16[512,768]{1,0:T(8,128)(2,1)}, bf16[512,768]{1,0:T(8,128)(2,1)}, u32[]{:S(2)}, u32[]{:S(2)}) %collective-permute-start.19) | collective-permute-done | bytes 786464 | tf_op jit(solution)/shard_map/ppermute | solution.py:292
  234.9 8.4 %collective-permute-done.24 = bf16[512,512]{1,0:T(8,128)(2,1)} collective-permute-done((bf16[512,512]{1,0:T(8,128)(2,1)}, bf16[512,512]{1,0:T(8,128)(2,1)}, u32[]{:S(2)}, u32[]{:S(2)}) %collective-permute-start.24) | collective-permute-done | bytes 524320 | tf_op jit(solution)/shard_map/ppermute | solution.py:353
  243.3 2.6 fusion.18
  245.9 12.7 %collective-permute-done.26.refs_6_ = bf16[512,768]{1,0:T(8,128)(2,1)} collective-permute-done((bf16[512,768]{1,0:T(8,128)(2,1)}, bf16[512,768]{1,0:T(8,128)(2,1)}, u32[]{:S(2)}, u32[]{:S(2)}) %collective-permute-start.26) | collective-permute-done | bytes 786464 | tf_op jit(solution)/shard_map/ppermute | solution.py:292
  258.5 2.7 collect.6
  261.4 2.9 convolution_convert_fusion.2
  264.3 2.9 add_convert_fusion.1
  270.6 2.6 fusion.28
  273.3 2.7 add_convert_fusion.5.qkv_ref
  275.9 11.1 %collective-permute-done.33 = bf16[512,768]{1,0:T(8,128)(2,1)S(1)} collective-permute-done((bf16[512,768]{1,0:T(8,128)(2,1)S(1)}, bf16[512,768]{1,0:T(8,128)(2,1)S(1)}, u32[]{:S(2)}, u32[]{:S(2)}) %collective-permute-start.33) | collective-permute-done | bytes 786464 | tf_op jit(solution)/shard_map/ppermute | solution.py:352
  288.4 5.2 attend_forward.3
  295.5 22.1 %collective-permute-start.29 = (bf16[512,512]{1,0:T(8,128)(2,1)S(1)}, bf16[512,512]{1,0:T(8,128)(2,1)S(1)}, u32[]{:S(2)}, u32[]{:S(2)}) collective-permute-start(bf16[512,512]{1,0:T(8,128)(2,1)S(1)} %get-tuple-element.128.refs_0_), channel_id=1, source_target_pairs={{0,8},{4,12},{8,16},{12,20},{16,24},{20,28},{1,9},{5,13},{9,17},{1... | collective-permute-start | bytes 1572872 | tf_op jit(solution)/shard_map/ppermute | solution.py:289
  318.9 10.5 %collective-permute-done.29.refs_1_ = bf16[512,512]{1,0:T(8,128)(2,1)S(1)} collective-permute-done((bf16[512,512]{1,0:T(8,128)(2,1)S(1)}, bf16[512,512]{1,0:T(8,128)(2,1)S(1)}, u32[]{:S(2)}, u32[]{:S(2)}) %collective-permute-start.29) | collective-permute-done | bytes 524320 | tf_op jit(solution)/shard_map/ppermute | solution.py:289
  329.4 4.1 collective-permute-done.30.refs_4_
  335.6 15.3 %collective-permute-done.32.refs_5_ = bf16[512,512]{1,0:T(8,128)(2,1)S(1)} collective-permute-done((bf16[512,512]{1,0:T(8,128)(2,1)S(1)}, bf16[512,512]{1,0:T(8,128)(2,1)S(1)}, u32[]{:S(2)}, u32[]{:S(2)}) %collective-permute-start.32) | collective-permute-done | bytes 524320 | tf_op jit(solution)/shard_map/ppermute | solution.py:292
  352.9 4.8 collective-permute-start.35
  361.4 11.6 %collective-permute-done.35 = bf16[512,768]{1,0:T(8,128)(2,1)S(1)} collective-permute-done((bf16[512,768]{1,0:T(8,128)(2,1)S(1)}, bf16[512,768]{1,0:T(8,128)(2,1)S(1)}, u32[]{:S(2)}, u32[]{:S(2)}) %collective-permute-start.35) | collective-permute-done | bytes 786464 | tf_op jit(solution)/shard_map/ppermute | solution.py:352
  375.2 5.0 project.2
  384.9 5.1 collective-permute-start.39
  389.9 3.9 collective-permute-start.43
  393.8 3.7 fusion.29
  399.4 8.6 %collective-permute-done.39 = bf16[512,768]{1,0:T(8,128)(2,1)S(1)} collective-permute-done((bf16[512,768]{1,0:T(8,128)(2,1)}, bf16[512,768]{1,0:T(8,128)(2,1)S(1)}, u32[]{:S(2)}, u32[]{:S(2)}) %collective-permute-start.39) | collective-permute-done | bytes 786464 | tf_op jit(solution)/shard_map/ppermute | solution.py:352
  408.0 2.6 fusion.7
  410.6 8.2 %collective-permute-done.43 = bf16[512,512]{1,0:T(8,128)(2,1)S(1)} collective-permute-done((bf16[512,512]{1,0:T(8,128)(2,1)}, bf16[512,512]{1,0:T(8,128)(2,1)S(1)}, u32[]{:S(2)}, u32[]{:S(2)}) %collective-permute-start.43) | collective-permute-done | bytes 524320 | tf_op jit(solution)/shard_map/ppermute | solution.py:352
  420.8 6.0 %attend_backward.3 = bf16[768,768]{1,0:T(8,128)(2,1)S(1)} custom-call(bf16[768,768]{1,0:T(8,128)(2,1)S(1)} %copy-done.27, bf16[768,512]{1,0:T(8,128)(2,1)S(1)} %add_convert_fusion.7.grad_ref, f32[4,768]{1,0:T(4,128)S(1)} %get-tuple-element.149.lse_ref), custom_call_target="tpu_custom_call" | custom-call | flops 6039797760 | bytes 3145728 | tf_op jit(solution)/shard_map/attend_backward/pallas_call | solution.py:118
  426.9 4.1 convolution_convert_fusion.1
  431.0 6.4 %project.3 = bf16[768,2048]{1,0:T(8,128)(2,1)} custom-call(bf16[768,512]{1,0:T(8,128)(2,1)S(1)} %copy-done.23, bf16[768,512]{1,0:T(8,128)(2,1)S(1)} %copy-done.25, bf16[2048,512]{1,0:T(8,128)(2,1)} %collective-permute-done.16.refs_2_, bf16[2048,512]{1,0:T(8,128)(2,1)S(1)} %collective-permute-done.38.refs_3_), custom_call_target="tpu_custom_call" | custom-call | flops 3221225472 | bytes 6291456 | tf_op jit(solution)/shard_map/project/pallas_call | solution.py:227
  438.2 4.7 collective-permute-start.45
  442.9 4.2 convolution_convert_fusion
  447.2 2.9 add_convert_fusion
  450.2 4.6 collective-permute-done.45
  456.5 4.9 collective-permute-start.50
  465.2 24.2 %collective-permute-done.46 = bf16[512,512]{1,0:T(8,128)(2,1)S(1)} collective-permute-done((bf16[512,512]{1,0:T(8,128)(2,1)S(1)}, bf16[512,512]{1,0:T(8,128)(2,1)S(1)}, u32[]{:S(2)}, u32[]{:S(2)}) %collective-permute-start.46) | collective-permute-done | bytes 524320 | tf_op jit(solution)/shard_map/ppermute | solution.py:352
  491.0 32.5 %collective-permute-start.51 = (bf16[512,768]{1,0:T(8,128)(2,1)S(1)}, bf16[512,768]{1,0:T(8,128)(2,1)S(1)}, u32[]{:S(2)}, u32[]{:S(2)}) collective-permute-start(bf16[512,768]{1,0:T(8,128)(2,1)S(1)} %get-tuple-element.162), channel_id=1, source_target_pairs={{0,8},{4,12},{8,16},{12,20},{1,9},{5,13},{9,17},{13,21},{2,10},{6,... | collective-permute-start | bytes 2359304 | tf_op jit(solution)/shard_map/ppermute | solution.py:352
  524.9 14.0 %collective-permute-done.51 = bf16[512,768]{1,0:T(8,128)(2,1)S(1)} collective-permute-done((bf16[512,768]{1,0:T(8,128)(2,1)S(1)}, bf16[512,768]{1,0:T(8,128)(2,1)S(1)}, u32[]{:S(2)}, u32[]{:S(2)}) %collective-permute-start.51) | collective-permute-done | bytes 786464 | tf_op jit(solution)/shard_map/ppermute | solution.py:352
  540.0 5.3 collective-permute-start.52
  550.2 3.1 add_convert_fusion.4
  553.3 5.9 %collective-permute-done.52 = bf16[512,768]{1,0:T(8,128)(2,1)} collective-permute-done((bf16[512,768]{1,0:T(8,128)(2,1)}, bf16[512,768]{1,0:T(8,128)(2,1)}, u32[]{:S(2)}, u32[]{:S(2)}) %collective-permute-start.52) | collective-permute-done | bytes 786464 | tf_op jit(solution)/shard_map/ppermute | solution.py:352
  559.2 5.0 collective-permute-done.55
  (212 shorter events, 99.0 us)
Async XLA Ops:
  7.2 541.5 %reduce-scatter.3.cloned.1.call-start = ((), (), s32[]{:S(2)}) async-start(), calls=%async_computation.2 | async-start | bytes 3932160 | tf_op jit(solution)/shard_map/reduce_scatter | solution.py:406
  11.1 21.7 %collective-permute-start = (bf16[512,768]{1,0:T(8,128)(2,1)S(1)}, bf16[512,768]{1,0:T(8,128)(2,1)S(1)}, u32[]{:S(2)}, u32[]{:S(2)}) collective-permute-start(bf16[512,768]{1,0:T(8,128)(2,1)S(1)} %pad_maximum_fusion.2.refs_0_), channel_id=1, source_target_pairs={{0,8},{4,12},{8,16},{12,20},{16,24},{20,28},{1,9},{5,13},{9,17},{1... | collective-permute-start | bytes 2359304 | tf_op jit(solution)/shard_map/ppermute | solution.py:289
  16.1 20.9 %collective-permute-start.1 = (bf16[512,768]{1,0:T(8,128)(2,1)S(1)}, bf16[512,768]{1,0:T(8,128)(2,1)S(1)}, u32[]{:S(2)}, u32[]{:S(2)}) collective-permute-start(bf16[512,768]{1,0:T(8,128)(2,1)S(1)} %pad_maximum_fusion.2.refs_0_), channel_id=1, source_target_pairs={{8,0},{12,4},{16,8},{20,12},{24,16},{28,20},{9,1},{13,5},{17,9},{2... | collective-permute-start | bytes 2359304 | tf_op jit(solution)/shard_map/ppermute | solution.py:292
  31.5 43.1 %copy-start.19 = (bf16[768,2048]{1,0:T(8,128)(2,1)}, bf16[768,2048]{1,0:T(8,128)(2,1)S(1)}, u32[]{:S(2)}) copy-start(bf16[768,2048]{1,0:T(8,128)(2,1)S(1)} %get-tuple-element.98) | copy-start | bytes 9437188
  37.0 11.9 %collective-permute-start.2 = (bf16[512,768]{1,0:T(8,128)(2,1)S(1)}, bf16[512,768]{1,0:T(8,128)(2,1)}, u32[]{:S(2)}, u32[]{:S(2)}) collective-permute-start(bf16[512,768]{1,0:T(8,128)(2,1)S(1)} %collective-permute-done.refs_1_), channel_id=1, source_target_pairs={{8,16},{12,20},{16,24},{20,28},{9,17},{13,21},{17,25},{21,29},{10,... | collective-permute-start | bytes 2359304 | tf_op jit(solution)/shard_map/ppermute | solution.py:289
  38.6 24.8 %collective-permute-start.3 = (bf16[512,768]{1,0:T(8,128)(2,1)S(1)}, bf16[512,768]{1,0:T(8,128)(2,1)}, u32[]{:S(2)}, u32[]{:S(2)}) collective-permute-start(bf16[512,768]{1,0:T(8,128)(2,1)S(1)} %collective-permute-done.1.refs_4_), channel_id=1, source_target_pairs={{8,0},{12,4},{16,8},{20,12},{9,1},{13,5},{17,9},{21,13},{10,2},{14... | collective-permute-start | bytes 2359304 | tf_op jit(solution)/shard_map/ppermute | solution.py:292
  40.0 62.8 %copy-start.3 = (bf16[512,512]{1,0:T(8,128)(2,1)}, bf16[512,512]{1,0:T(8,128)(2,1)S(1)}, u32[]{:S(2)}) copy-start(bf16[512,512]{1,0:T(8,128)(2,1)S(1)} %get-tuple-element.114.refs_0_) | copy-start | bytes 1572868
  40.0 26.3 %collective-permute-start.4 = (bf16[512,512]{1,0:T(8,128)(2,1)S(1)}, bf16[512,512]{1,0:T(8,128)(2,1)}, u32[]{:S(2)}, u32[]{:S(2)}) collective-permute-start(bf16[512,512]{1,0:T(8,128)(2,1)S(1)} %get-tuple-element.114.refs_0_), channel_id=1, source_target_pairs={{0,8},{4,12},{8,16},{12,20},{16,24},{20,28},{1,9},{5,13},{9,17},{1... | collective-permute-start | bytes 1572872 | tf_op jit(solution)/shard_map/ppermute | solution.py:289
  47.7 27.0 %collective-permute-start.5 = (bf16[512,512]{1,0:T(8,128)(2,1)S(1)}, bf16[512,512]{1,0:T(8,128)(2,1)}, u32[]{:S(2)}, u32[]{:S(2)}) collective-permute-start(bf16[512,512]{1,0:T(8,128)(2,1)S(1)} %get-tuple-element.114.refs_0_), channel_id=1, source_target_pairs={{8,0},{12,4},{16,8},{20,12},{24,16},{28,20},{9,1},{13,5},{17,9},{2... | collective-permute-start | bytes 1572872 | tf_op jit(solution)/shard_map/ppermute | solution.py:292
  63.4 14.0 %collective-permute-start.6 = (bf16[512,768]{1,0:T(8,128)(2,1)}, bf16[512,768]{1,0:T(8,128)(2,1)}, u32[]{:S(2)}, u32[]{:S(2)}) collective-permute-start(bf16[512,768]{1,0:T(8,128)(2,1)} %collective-permute-done.2.refs_2_), channel_id=1, source_target_pairs={{16,24},{20,28},{17,25},{21,29},{18,26},{22,30},{19,27},{23,31}} | collective-permute-start | bytes 2359304 | tf_op jit(solution)/shard_map/ppermute | solution.py:289
  64.9 26.5 %collective-permute-start.7 = (bf16[512,768]{1,0:T(8,128)(2,1)}, bf16[512,768]{1,0:T(8,128)(2,1)}, u32[]{:S(2)}, u32[]{:S(2)}) collective-permute-start(bf16[512,768]{1,0:T(8,128)(2,1)} %collective-permute-done.3.refs_5_), channel_id=1, source_target_pairs={{8,0},{12,4},{9,1},{13,5},{10,2},{14,6},{11,3},{15,7}} | collective-permute-start | bytes 2359304 | tf_op jit(solution)/shard_map/ppermute | solution.py:292
  74.6 16.9 %collective-permute-start.8 = (bf16[512,512]{1,0:T(8,128)(2,1)}, bf16[512,512]{1,0:T(8,128)(2,1)}, u32[]{:S(2)}, u32[]{:S(2)}) collective-permute-start(bf16[512,512]{1,0:T(8,128)(2,1)} %collective-permute-done.4.refs_1_), channel_id=1, source_target_pairs={{8,16},{12,20},{16,24},{20,28},{9,17},{13,21},{17,25},{21,29},{10,... | collective-permute-start | bytes 1572872 | tf_op jit(solution)/shard_map/ppermute | solution.py:289
  76.1 24.2 %collective-permute-start.9 = (bf16[512,512]{1,0:T(8,128)(2,1)}, bf16[512,512]{1,0:T(8,128)(2,1)}, u32[]{:S(2)}, u32[]{:S(2)}) collective-permute-start(bf16[512,512]{1,0:T(8,128)(2,1)} %collective-permute-done.5.refs_4_), channel_id=1, source_target_pairs={{8,0},{12,4},{16,8},{20,12},{9,1},{13,5},{17,9},{21,13},{10,2},{14... | collective-permute-start | bytes 1572872 | tf_op jit(solution)/shard_map/ppermute | solution.py:292
  102.8 5.7 collective-permute-start.10
  119.6 10.1 %collective-permute-start.11 = (bf16[2048,512]{1,0:T(8,128)(2,1)}, bf16[2048,512]{1,0:T(8,128)(2,1)}, u32[]{:S(2)}, u32[]{:S(2)}) collective-permute-start(bf16[2048,512]{1,0:T(8,128)(2,1)} %convolution_convert_fusion.7), channel_id=1, source_target_pairs={{0,4},{4,0},{8,12},{12,8},{16,20},{20,16},{24,28},{28,24},{1,5},{5... | collective-permute-start | bytes 6291464 | tf_op jit(solution)/shard_map/ppermute | solution.py:268
  119.8 35.1 %collective-permute-start.14 = (bf16[512,768]{1,0:T(8,128)(2,1)S(1)}, bf16[512,768]{1,0:T(8,128)(2,1)}, u32[]{:S(2)}, u32[]{:S(2)}) collective-permute-start(bf16[512,768]{1,0:T(8,128)(2,1)S(1)} %pad_maximum_fusion.3.refs_0_), channel_id=1, source_target_pairs={{0,8},{4,12},{8,16},{12,20},{16,24},{20,28},{1,9},{5,13},{9,17},{1... | collective-permute-start | bytes 2359304 | tf_op jit(solution)/shard_map/ppermute | solution.py:289
  122.2 32.8 %collective-permute-start.15 = (bf16[512,768]{1,0:T(8,128)(2,1)S(1)}, bf16[512,768]{1,0:T(8,128)(2,1)}, u32[]{:S(2)}, u32[]{:S(2)}) collective-permute-start(bf16[512,768]{1,0:T(8,128)(2,1)S(1)} %pad_maximum_fusion.3.refs_0_), channel_id=1, source_target_pairs={{8,0},{12,4},{16,8},{20,12},{24,16},{28,20},{9,1},{13,5},{17,9},{2... | collective-permute-start | bytes 2359304 | tf_op jit(solution)/shard_map/ppermute | solution.py:292
  123.5 9.5 %collective-permute-start.12 = (bf16[512,512]{1,0:T(8,128)(2,1)}, bf16[512,512]{1,0:T(8,128)(2,1)S(1)}, u32[]{:S(2)}, u32[]{:S(2)}) collective-permute-start(bf16[512,512]{1,0:T(8,128)(2,1)} %collective-permute-done.8.refs_2_), channel_id=1, source_target_pairs={{16,24},{20,28},{17,25},{21,29},{18,26},{22,30},{19,27},{23,31}} | collective-permute-start | bytes 1572872 | tf_op jit(solution)/shard_map/ppermute | solution.py:289
  124.2 30.8 %collective-permute-start.13 = (bf16[512,512]{1,0:T(8,128)(2,1)}, bf16[512,512]{1,0:T(8,128)(2,1)S(1)}, u32[]{:S(2)}, u32[]{:S(2)}) collective-permute-start(bf16[512,512]{1,0:T(8,128)(2,1)} %collective-permute-done.9.refs_5_), channel_id=1, source_target_pairs={{8,0},{12,4},{9,1},{13,5},{10,2},{14,6},{11,3},{15,7}} | collective-permute-start | bytes 1572872 | tf_op jit(solution)/shard_map/ppermute | solution.py:292
  156.7 5.7 collective-permute-start.16
  156.8 14.1 %collective-permute-start.17 = (bf16[512,512]{1,0:T(8,128)(2,1)}, bf16[512,512]{1,0:T(8,128)(2,1)S(1)}, u32[]{:S(2)}, u32[]{:S(2)}) collective-permute-start(bf16[512,512]{1,0:T(8,128)(2,1)} %get-tuple-element.113), channel_id=1, source_target_pairs={{0,8},{4,12},{1,9},{5,13},{2,10},{6,14},{3,11},{7,15}} | collective-permute-start | bytes 1572872 | tf_op jit(solution)/shard_map/ppermute | solution.py:352
  182.9 81.4 %collective-permute-start.28 = (bf16[2048,768]{1,0:T(8,128)(2,1)}, bf16[2048,768]{1,0:T(8,128)(2,1)}, u32[]{:S(2)}, u32[]{:S(2)}) collective-permute-start(bf16[2048,768]{1,0:T(8,128)(2,1)} %convolution_convert_fusion.3), channel_id=1, source_target_pairs={{0,4},{4,0},{8,12},{12,8},{16,20},{20,16},{24,28},{28,24},{1,5},{5... | collective-permute-start | bytes 9437192 | tf_op jit(solution)/shard_map/ppermute | solution.py:268
  183.0 16.4 %collective-permute-start.20 = (bf16[512,512]{1,0:T(8,128)(2,1)}, bf16[512,512]{1,0:T(8,128)(2,1)}, u32[]{:S(2)}, u32[]{:S(2)}) collective-permute-start(bf16[512,512]{1,0:T(8,128)(2,1)} %fusion.19), channel_id=1, source_target_pairs={{0,8},{4,12},{8,16},{12,20},{1,9},{5,13},{9,17},{13,21},{2,10},{6,... | collective-permute-start | bytes 1572872 | tf_op jit(solution)/shard_map/ppermute | solution.py:352
  188.0 11.4 %collective-permute-start.22 = (bf16[512,512]{1,0:T(8,128)(2,1)}, bf16[512,512]{1,0:T(8,128)(2,1)}, u32[]{:S(2)}, u32[]{:S(2)}) collective-permute-start(bf16[512,512]{1,0:T(8,128)(2,1)} %get-tuple-element.175), channel_id=1, source_target_pairs={{24,16},{28,20},{25,17},{29,21},{26,18},{30,22},{27,19},{31,23}} | collective-permute-start | bytes 1572872 | tf_op jit(solution)/shard_map/ppermute | solution.py:353
  202.2 13.9 %collective-permute-start.23 = (bf16[512,512]{1,0:T(8,128)(2,1)}, bf16[512,512]{1,0:T(8,128)(2,1)}, u32[]{:S(2)}, u32[]{:S(2)}) collective-permute-start(bf16[512,512]{1,0:T(8,128)(2,1)} %get-tuple-element.174), channel_id=1, source_target_pairs={{16,8},{20,12},{24,16},{28,20},{17,9},{21,13},{25,17},{29,21},{18,... | collective-permute-start | bytes 1572872 | tf_op jit(solution)/shard_map/ppermute | solution.py:353
  203.6 15.8 %collective-permute-start.18 = (bf16[512,768]{1,0:T(8,128)(2,1)}, bf16[512,768]{1,0:T(8,128)(2,1)}, u32[]{:S(2)}, u32[]{:S(2)}) collective-permute-start(bf16[512,768]{1,0:T(8,128)(2,1)} %collective-permute-done.14.refs_1_), channel_id=1, source_target_pairs={{8,16},{12,20},{16,24},{20,28},{9,17},{13,21},{17,25},{21,29},{10,... | collective-permute-start | bytes 2359304 | tf_op jit(solution)/shard_map/ppermute | solution.py:289
  205.2 26.9 %collective-permute-start.19 = (bf16[512,768]{1,0:T(8,128)(2,1)}, bf16[512,768]{1,0:T(8,128)(2,1)}, u32[]{:S(2)}, u32[]{:S(2)}) collective-permute-start(bf16[512,768]{1,0:T(8,128)(2,1)} %collective-permute-done.15.refs_4_), channel_id=1, source_target_pairs={{8,0},{12,4},{16,8},{20,12},{9,1},{13,5},{17,9},{21,13},{10,2},{14... | collective-permute-start | bytes 2359304 | tf_op jit(solution)/shard_map/ppermute | solution.py:292
  206.4 28.4 %collective-permute-start.21 = (bf16[512,512]{1,0:T(8,128)(2,1)}, bf16[512,512]{1,0:T(8,128)(2,1)}, u32[]{:S(2)}, u32[]{:S(2)}) collective-permute-start(bf16[512,512]{1,0:T(8,128)(2,1)} %get-tuple-element.173), channel_id=1, source_target_pairs={{0,8},{4,12},{8,16},{12,20},{16,24},{20,28},{1,9},{5,13},{9,17},{1... | collective-permute-start | bytes 1572872 | tf_op jit(solution)/shard_map/ppermute | solution.py:352
  218.2 25.1 %collective-permute-start.24 = (bf16[512,512]{1,0:T(8,128)(2,1)}, bf16[512,512]{1,0:T(8,128)(2,1)}, u32[]{:S(2)}, u32[]{:S(2)}) collective-permute-start(bf16[512,512]{1,0:T(8,128)(2,1)} %fusion.16), channel_id=1, source_target_pairs={{8,0},{12,4},{16,8},{20,12},{24,16},{28,20},{9,1},{13,5},{17,9},{2... | collective-permute-start | bytes 1572872 | tf_op jit(solution)/shard_map/ppermute | solution.py:353
  232.0 13.8 %collective-permute-start.25 = (bf16[512,768]{1,0:T(8,128)(2,1)}, bf16[512,768]{1,0:T(8,128)(2,1)}, u32[]{:S(2)}, u32[]{:S(2)}) collective-permute-start(bf16[512,768]{1,0:T(8,128)(2,1)} %collective-permute-done.18.refs_2_), channel_id=1, source_target_pairs={{16,24},{20,28},{17,25},{21,29},{18,26},{22,30},{19,27},{23,31}} | collective-permute-start | bytes 2359304 | tf_op jit(solution)/shard_map/ppermute | solution.py:289
  233.6 25.0 %collective-permute-start.26 = (bf16[512,768]{1,0:T(8,128)(2,1)}, bf16[512,768]{1,0:T(8,128)(2,1)}, u32[]{:S(2)}, u32[]{:S(2)}) collective-permute-start(bf16[512,768]{1,0:T(8,128)(2,1)} %collective-permute-done.19.refs_5_), channel_id=1, source_target_pairs={{8,0},{12,4},{9,1},{13,5},{10,2},{14,6},{11,3},{15,7}} | collective-permute-start | bytes 2359304 | tf_op jit(solution)/shard_map/ppermute | solution.py:292
  261.3 12.0 %collective-permute-start.27 = (bf16[2048,768]{1,0:T(8,128)(2,1)S(1)}, bf16[2048,768]{1,0:T(8,128)(2,1)S(1)}, u32[]{:S(2)}, u32[]{:S(2)}) collective-permute-start(bf16[2048,768]{1,0:T(8,128)(2,1)S(1)} %collect.6), channel_id=1, source_target_pairs={{0,4},{4,0},{8,12},{12,8},{16,20},{20,16},{24,28},{28,24},{1,5},{5... | collective-permute-start | bytes 9437192 | tf_op jit(solution)/shard_map/ppermute | solution.py:268
  267.2 105.8 %copy-start.33 = (bf16[2048,768]{1,0:T(8,128)(2,1)}, bf16[2048,768]{1,0:T(8,128)(2,1)S(1)}, u32[]{:S(2)}) copy-start(bf16[2048,768]{1,0:T(8,128)(2,1)S(1)} %add_convert_fusion.1) | copy-start | bytes 9437188
  267.3 2.2 collective-permute-start.40
  268.0 19.0 %collective-permute-start.33 = (bf16[512,768]{1,0:T(8,128)(2,1)S(1)}, bf16[512,768]{1,0:T(8,128)(2,1)S(1)}, u32[]{:S(2)}, u32[]{:S(2)}) collective-permute-start(bf16[512,768]{1,0:T(8,128)(2,1)S(1)} %get-tuple-element.168), channel_id=1, source_target_pairs={{0,8},{4,12},{1,9},{5,13},{2,10},{6,14},{3,11},{7,15}} | collective-permute-start | bytes 2359304 | tf_op jit(solution)/shard_map/ppermute | solution.py:352
  269.8 17.2 %collective-permute-start.41 = (bf16[512,768]{1,0:T(8,128)(2,1)S(1)}, bf16[512,768]{1,0:T(8,128)(2,1)S(1)}, u32[]{:S(2)}, u32[]{:S(2)}) collective-permute-start(bf16[512,768]{1,0:T(8,128)(2,1)S(1)} %fusion.5), channel_id=1, source_target_pairs={{16,8},{20,12},{24,16},{28,20},{17,9},{21,13},{25,17},{29,21},{18,... | collective-permute-start | bytes 2359304 | tf_op jit(solution)/shard_map/ppermute | solution.py:353
  293.5 80.7 %copy-start.24 = (bf16[768,512]{1,0:T(8,128)(2,1)}, bf16[768,512]{1,0:T(8,128)(2,1)S(1)}, u32[]{:S(2)}) copy-start(bf16[768,512]{1,0:T(8,128)(2,1)S(1)} %get-tuple-element.138.refs_1_) | copy-start | bytes 2359300
  293.5 64.2 %copy-start.20 = (bf16[768,2048]{1,0:T(8,128)(2,1)S(1)}, bf16[768,2048]{1,0:T(8,128)(2,1)}, u32[]{:S(2)}) copy-start(bf16[768,2048]{1,0:T(8,128)(2,1)} %copy-done.19) | copy-start | bytes 9437188
  295.4 64.2 %collective-permute-start.34 = (bf16[2048,512]{1,0:T(8,128)(2,1)S(1)}, bf16[2048,512]{1,0:T(8,128)(2,1)S(1)}, u32[]{:S(2)}, u32[]{:S(2)}) collective-permute-start(bf16[2048,512]{1,0:T(8,128)(2,1)S(1)} %convolution_convert_fusion.5), channel_id=1, source_target_pairs={{0,4},{4,0},{8,12},{12,8},{16,20},{20,16},{24,28},{28,24},{1,5},{5... | collective-permute-start | bytes 6291464 | tf_op jit(solution)/shard_map/ppermute | solution.py:268
  295.5 33.9 %collective-permute-start.29 = (bf16[512,512]{1,0:T(8,128)(2,1)S(1)}, bf16[512,512]{1,0:T(8,128)(2,1)S(1)}, u32[]{:S(2)}, u32[]{:S(2)}) collective-permute-start(bf16[512,512]{1,0:T(8,128)(2,1)S(1)} %get-tuple-element.128.refs_0_), channel_id=1, source_target_pairs={{0,8},{4,12},{8,16},{12,20},{16,24},{20,28},{1,9},{5,13},{9,17},{1... | collective-permute-start | bytes 1572872 | tf_op jit(solution)/shard_map/ppermute | solution.py:289
  317.6 15.9 %collective-permute-start.30 = (bf16[512,512]{1,0:T(8,128)(2,1)S(1)}, bf16[512,512]{1,0:T(8,128)(2,1)S(1)}, u32[]{:S(2)}, u32[]{:S(2)}) collective-permute-start(bf16[512,512]{1,0:T(8,128)(2,1)S(1)} %get-tuple-element.128.refs_0_), channel_id=1, source_target_pairs={{8,0},{12,4},{16,8},{20,12},{24,16},{28,20},{9,1},{13,5},{17,9},{2... | collective-permute-start | bytes 1572872 | tf_op jit(solution)/shard_map/ppermute | solution.py:292
  333.6 2.0 collective-permute-start.31
  334.2 16.7 %collective-permute-start.32 = (bf16[512,512]{1,0:T(8,128)(2,1)S(1)}, bf16[512,512]{1,0:T(8,128)(2,1)S(1)}, u32[]{:S(2)}, u32[]{:S(2)}) collective-permute-start(bf16[512,512]{1,0:T(8,128)(2,1)S(1)} %collective-permute-done.30.refs_4_), channel_id=1, source_target_pairs={{8,0},{12,4},{16,8},{20,12},{9,1},{13,5},{17,9},{21,13},{10,2},{14... | collective-permute-start | bytes 1572872 | tf_op jit(solution)/shard_map/ppermute | solution.py:292
  350.9 23.2 %collective-permute-start.36 = (bf16[512,512]{1,0:T(8,128)(2,1)S(1)}, bf16[512,512]{1,0:T(8,128)(2,1)S(1)}, u32[]{:S(2)}, u32[]{:S(2)}) collective-permute-start(bf16[512,512]{1,0:T(8,128)(2,1)S(1)} %collective-permute-done.31.refs_2_), channel_id=1, source_target_pairs={{16,24},{20,28},{17,25},{21,29},{18,26},{22,30},{19,27},{23,31}} | collective-permute-start | bytes 1572872 | tf_op jit(solution)/shard_map/ppermute | solution.py:289
  351.6 22.5 %collective-permute-start.37 = (bf16[512,512]{1,0:T(8,128)(2,1)S(1)}, bf16[512,512]{1,0:T(8,128)(2,1)S(1)}, u32[]{:S(2)}, u32[]{:S(2)}) collective-permute-start(bf16[512,512]{1,0:T(8,128)(2,1)S(1)} %collective-permute-done.32.refs_5_), channel_id=1, source_target_pairs={{8,0},{12,4},{9,1},{13,5},{10,2},{14,6},{11,3},{15,7}} | collective-permute-start | bytes 1572872 | tf_op jit(solution)/shard_map/ppermute | solution.py:292
  352.9 20.1 %collective-permute-start.35 = (bf16[512,768]{1,0:T(8,128)(2,1)S(1)}, bf16[512,768]{1,0:T(8,128)(2,1)S(1)}, u32[]{:S(2)}, u32[]{:S(2)}) collective-permute-start(bf16[512,768]{1,0:T(8,128)(2,1)S(1)} %get-tuple-element.166), channel_id=1, source_target_pairs={{0,8},{4,12},{8,16},{12,20},{1,9},{5,13},{9,17},{13,21},{2,10},{6,... | collective-permute-start | bytes 2359304 | tf_op jit(solution)/shard_map/ppermute | solution.py:352
  381.6 167.2 %reduce-scatter.5.cloned.1.call-start = ((), (), s32[]{:S(2)}) async-start(), calls=%async_computation.3 | async-start | bytes 3932160 | tf_op jit(solution)/shard_map/reduce_scatter | solution.py:406
  383.2 14.3 %collective-permute-start.38 = (bf16[2048,512]{1,0:T(8,128)(2,1)S(1)}, bf16[2048,512]{1,0:T(8,128)(2,1)S(1)}, u32[]{:S(2)}, u32[]{:S(2)}) collective-permute-start(bf16[2048,512]{1,0:T(8,128)(2,1)S(1)} %copy-done.2), channel_id=1, source_target_pairs={{0,4},{4,0},{8,12},{12,8},{16,20},{20,16},{24,28},{28,24},{1,5},{5... | collective-permute-start | bytes 6291464 | tf_op jit(solution)/shard_map/ppermute | solution.py:268
  383.3 24.7 %collective-permute-start.42 = (bf16[512,768]{1,0:T(8,128)(2,1)S(1)}, bf16[512,768]{1,0:T(8,128)(2,1)S(1)}, u32[]{:S(2)}, u32[]{:S(2)}) collective-permute-start(bf16[512,768]{1,0:T(8,128)(2,1)S(1)} %copy-done.42), channel_id=1, source_target_pairs={{8,0},{12,4},{16,8},{20,12},{24,16},{28,20},{9,1},{13,5},{17,9},{2... | collective-permute-start | bytes 2359304 | tf_op jit(solution)/shard_map/ppermute | solution.py:353
  384.9 23.2 %collective-permute-start.39 = (bf16[512,768]{1,0:T(8,128)(2,1)}, bf16[512,768]{1,0:T(8,128)(2,1)S(1)}, u32[]{:S(2)}, u32[]{:S(2)}) collective-permute-start(bf16[512,768]{1,0:T(8,128)(2,1)} %fusion.9), channel_id=1, source_target_pairs={{0,8},{4,12},{8,16},{12,20},{16,24},{20,28},{1,9},{5,13},{9,17},{1... | collective-permute-start | bytes 2359304 | tf_op jit(solution)/shard_map/ppermute | solution.py:352
  389.9 28.9 %collective-permute-start.43 = (bf16[512,512]{1,0:T(8,128)(2,1)}, bf16[512,512]{1,0:T(8,128)(2,1)S(1)}, u32[]{:S(2)}, u32[]{:S(2)}) collective-permute-start(bf16[512,512]{1,0:T(8,128)(2,1)} %get-tuple-element.172), channel_id=1, source_target_pairs={{0,8},{4,12},{1,9},{5,13},{2,10},{6,14},{3,11},{7,15}} | collective-permute-start | bytes 1572872 | tf_op jit(solution)/shard_map/ppermute | solution.py:352
  431.0 16.2 %collective-permute-start.44 = (bf16[2048,768]{1,0:T(8,128)(2,1)}, bf16[2048,768]{1,0:T(8,128)(2,1)}, u32[]{:S(2)}, u32[]{:S(2)}) collective-permute-start(bf16[2048,768]{1,0:T(8,128)(2,1)} %convolution_convert_fusion.1), channel_id=1, source_target_pairs={{0,4},{4,0},{8,12},{12,8},{16,20},{20,16},{24,28},{28,24},{1,5},{5... | collective-permute-start | bytes 9437192 | tf_op jit(solution)/shard_map/ppermute | solution.py:268
  437.4 18.1 %collective-permute-start.47 = (bf16[512,512]{1,0:T(8,128)(2,1)}, bf16[512,512]{1,0:T(8,128)(2,1)S(1)}, u32[]{:S(2)}, u32[]{:S(2)}) collective-permute-start(bf16[512,512]{1,0:T(8,128)(2,1)} %get-tuple-element.171), channel_id=1, source_target_pairs={{24,16},{28,20},{25,17},{29,21},{26,18},{30,22},{27,19},{31,23}} | collective-permute-start | bytes 1572872 | tf_op jit(solution)/shard_map/ppermute | solution.py:353
  438.2 16.5 %collective-permute-start.45 = (bf16[512,512]{1,0:T(8,128)(2,1)}, bf16[512,512]{1,0:T(8,128)(2,1)S(1)}, u32[]{:S(2)}, u32[]{:S(2)}) collective-permute-start(bf16[512,512]{1,0:T(8,128)(2,1)} %fusion.14), channel_id=1, source_target_pairs={{0,8},{4,12},{8,16},{12,20},{1,9},{5,13},{9,17},{13,21},{2,10},{6,... | collective-permute-start | bytes 1572872 | tf_op jit(solution)/shard_map/ppermute | solution.py:352
  454.8 9.5 %collective-permute-start.53 = (bf16[512,768]{1,0:T(8,128)(2,1)S(1)}, bf16[512,768]{1,0:T(8,128)(2,1)S(1)}, u32[]{:S(2)}, u32[]{:S(2)}) collective-permute-start(bf16[512,768]{1,0:T(8,128)(2,1)S(1)} %get-tuple-element.163), channel_id=1, source_target_pairs={{24,16},{28,20},{25,17},{29,21},{26,18},{30,22},{27,19},{31,23}} | collective-permute-start | bytes 2359304 | tf_op jit(solution)/shard_map/ppermute | solution.py:353
  455.8 7.0 %collective-permute-start.48 = (bf16[512,512]{1,0:T(8,128)(2,1)S(1)}, bf16[512,512]{1,0:T(8,128)(2,1)S(1)}, u32[]{:S(2)}, u32[]{:S(2)}) collective-permute-start(bf16[512,512]{1,0:T(8,128)(2,1)S(1)} %get-tuple-element.170), channel_id=1, source_target_pairs={{16,8},{20,12},{24,16},{28,20},{17,9},{21,13},{25,17},{29,21},{18,... | collective-permute-start | bytes 1572872 | tf_op jit(solution)/shard_map/ppermute | solution.py:353
  456.5 33.1 %collective-permute-start.50 = (bf16[512,768]{1,0:T(8,128)(2,1)S(1)}, bf16[512,768]{1,0:T(8,128)(2,1)S(1)}, u32[]{:S(2)}, u32[]{:S(2)}) collective-permute-start(bf16[512,768]{1,0:T(8,128)(2,1)S(1)} %get-tuple-element.164), channel_id=1, source_target_pairs={{0,8},{4,12},{1,9},{5,13},{2,10},{6,14},{3,11},{7,15}} | collective-permute-start | bytes 2359304 | tf_op jit(solution)/shard_map/ppermute | solution.py:352
  461.4 27.9 %collective-permute-start.46 = (bf16[512,512]{1,0:T(8,128)(2,1)S(1)}, bf16[512,512]{1,0:T(8,128)(2,1)S(1)}, u32[]{:S(2)}, u32[]{:S(2)}) collective-permute-start(bf16[512,512]{1,0:T(8,128)(2,1)S(1)} %get-tuple-element.169), channel_id=1, source_target_pairs={{0,8},{4,12},{8,16},{12,20},{16,24},{20,28},{1,9},{5,13},{9,17},{1... | collective-permute-start | bytes 1572872 | tf_op jit(solution)/shard_map/ppermute | solution.py:352
  462.9 26.5 %collective-permute-start.49 = (bf16[512,512]{1,0:T(8,128)(2,1)S(1)}, bf16[512,512]{1,0:T(8,128)(2,1)S(1)}, u32[]{:S(2)}, u32[]{:S(2)}) collective-permute-start(bf16[512,512]{1,0:T(8,128)(2,1)S(1)} %fusion.11), channel_id=1, source_target_pairs={{8,0},{12,4},{16,8},{20,12},{24,16},{28,20},{9,1},{13,5},{17,9},{2... | collective-permute-start | bytes 1572872 | tf_op jit(solution)/shard_map/ppermute | solution.py:353
  464.5 25.2 %collective-permute-start.54 = (bf16[512,768]{1,0:T(8,128)(2,1)S(1)}, bf16[512,768]{1,0:T(8,128)(2,1)S(1)}, u32[]{:S(2)}, u32[]{:S(2)}) collective-permute-start(bf16[512,768]{1,0:T(8,128)(2,1)S(1)} %fusion), channel_id=1, source_target_pairs={{16,8},{20,12},{24,16},{28,20},{17,9},{21,13},{25,17},{29,21},{18,... | collective-permute-start | bytes 2359304 | tf_op jit(solution)/shard_map/ppermute | solution.py:353
  489.6 33.9 %copy-start.38 = (f32[512,512]{1,0:T(8,128)S(1)}, f32[512,512]{1,0:T(8,128)}, u32[]{:S(2)}) copy-start(f32[512,512]{1,0:T(8,128)} %fusion.18) | copy-start | bytes 3145732
  491.0 47.9 %collective-permute-start.51 = (bf16[512,768]{1,0:T(8,128)(2,1)S(1)}, bf16[512,768]{1,0:T(8,128)(2,1)S(1)}, u32[]{:S(2)}, u32[]{:S(2)}) collective-permute-start(bf16[512,768]{1,0:T(8,128)(2,1)S(1)} %get-tuple-element.162), channel_id=1, source_target_pairs={{0,8},{4,12},{8,16},{12,20},{1,9},{5,13},{9,17},{13,21},{2,10},{6,... | collective-permute-start | bytes 2359304 | tf_op jit(solution)/shard_map/ppermute | solution.py:352
  540.0 19.3 %collective-permute-start.52 = (bf16[512,768]{1,0:T(8,128)(2,1)}, bf16[512,768]{1,0:T(8,128)(2,1)}, u32[]{:S(2)}, u32[]{:S(2)}) collective-permute-start(bf16[512,768]{1,0:T(8,128)(2,1)} %fusion.4), channel_id=1, source_target_pairs={{0,8},{4,12},{8,16},{12,20},{16,24},{20,28},{1,9},{5,13},{9,17},{1... | collective-permute-start | bytes 2359304 | tf_op jit(solution)/shard_map/ppermute | solution.py:352
  545.3 19.0 %collective-permute-start.55 = (bf16[512,768]{1,0:T(8,128)(2,1)}, bf16[512,768]{1,0:T(8,128)(2,1)}, u32[]{:S(2)}, u32[]{:S(2)}) collective-permute-start(bf16[512,768]{1,0:T(8,128)(2,1)} %get-tuple-element.161), channel_id=1, source_target_pairs={{8,0},{12,4},{16,8},{20,12},{24,16},{28,20},{9,1},{13,5},{17,9},{2... | collective-permute-start | bytes 2359304 | tf_op jit(solution)/shard_map/ppermute | solution.py:353
  (40 other events, 286.5 us)
Sparse Core Ops, SparseCore 0:
  381.7 44.0 reduce-scatter.2
  437.5 44.0 reduce-scatter.4

commit v4 on v3

--- a/solution.py
+++ b/solution.py
@@ -12,6 +12,7 @@
 MASKED = -1e30
 F32 = jnp.float32
 BF16 = jnp.bfloat16
+SHORT = pl.CostEstimate(flops=1, bytes_accessed=1, transcendentals=0)
 
 
 def normalize(rows, gain):
@@ -75,11 +76,7 @@
         in_specs=[vmem],
         out_specs=(vmem, vmem),
         compiler_params=pltpu.CompilerParams(vmem_limit_bytes=40 * 2**20),
-        cost_estimate=pl.CostEstimate(
-            flops=8 * members * length * length * width,
-            bytes_accessed=8 * length * members * width,
-            transcendentals=members * length * length,
-        ),
+        cost_estimate=SHORT,
         name="attend_forward",
     )(qkv)
 
@@ -122,11 +119,7 @@
         out_specs=vmem,
         scratch_shapes=[pltpu.VMEM((length, width), F32), pltpu.VMEM((length, width), F32)],
         compiler_params=pltpu.CompilerParams(vmem_limit_bytes=40 * 2**20),
-        cost_estimate=pl.CostEstimate(
-            flops=20 * members * length * length * width,
-            bytes_accessed=8 * length * members * width,
-            transcendentals=members * length * length,
-        ),
+        cost_estimate=SHORT,
         name="attend_backward",
     )(qkv, grad_mixed, lse)
 
@@ -171,11 +164,7 @@
         ],
         out_specs=(half,) * 4,
         compiler_params=pltpu.CompilerParams(vmem_limit_bytes=32 * 2**20),
-        cost_estimate=pl.CostEstimate(
-            flops=8 * length * features,
-            bytes_accessed=8 * length * features,
-            transcendentals=length,
-        ),
+        cost_estimate=SHORT,
         name="norm_and_split",
     )(core.reshape(1), activations, gain.astype(F32).reshape(1, -1), cotangent)
 
@@ -203,9 +192,7 @@
         in_specs=[pl.BlockSpec(memory_space=pltpu.SMEM)] + [vmem] * (len(ups) + len(downs)),
         out_specs=vmem,
         compiler_params=pltpu.CompilerParams(vmem_limit_bytes=24 * 2**20),
-        cost_estimate=pl.CostEstimate(
-            flops=0, bytes_accessed=6 * chips * rows * cols, transcendentals=0
-        ),
+        cost_estimate=SHORT,
         name="collect",
     )(chip.reshape(1), *ups, *downs)
 
@@ -232,11 +219,7 @@
         + [pl.BlockSpec((step, span), lambda i: (i, 0))] * count,
         out_specs=pl.BlockSpec((length, step), lambda i: (0, i)),
         compiler_params=pltpu.CompilerParams(vmem_limit_bytes=32 * 2**20),
-        cost_estimate=pl.CostEstimate(
-            flops=2 * count * length * span * features,
-            bytes_accessed=4 * length * features,
-            transcendentals=0,
-        ),
+        cost_estimate=SHORT,
         name="project",
     )(*mixed, *sides)
 
@@ -247,8 +230,11 @@
 
     def __call__(self, compute, *operands):
         result = compute(*self.after(*operands))
-        self.last = jax.tree.leaves(result)[0]
-        return result
+        leaves, form = jax.tree.flatten(result)
+        if len(leaves) > 1:
+            leaves = lax.optimization_barrier(tuple(leaves))
+        self.last = leaves[0]
+        return jax.tree.unflatten(form, leaves)
 
     def after(self, *operands):
         if self.last is None:
@@ -260,7 +246,8 @@
     def wait(self, *arrays):
         if self.last is None:
             return arrays
-        self.last, *arrays = lax.optimization_barrier((self.last, *arrays))
+        arrays = lax.optimization_barrier((self.last, *arrays))[1:]
+        self.last = arrays[0]
         return arrays
 
 

time: 582 us -> 492 us (0.85)
  waiting for transfers between devices: 248 us -> 199 us
  starting transfers between devices: 157 us -> 114 us
    ppermute x12, waiting for transfers between devices: 117 us -> 85.3 us  [hop(): lax.ppermute(down, 'wide', [(w, w - 2) for w in range(2, 2 * (chips - t +...]
    ppermute x12, starting transfers between devices: 46.8 us -> 24.9 us  [hop(): lax.ppermute(up, 'wide', [(w, w + 2) for w in range(2 * (t - 1), 2 * (chi...]
    ppermute x12, starting transfers between devices: 80.5 us -> 60.6 us  [advance(): self.up = lax.ppermute(up, 'wide', [(w, w + 2) for w in range(2 * t)])]
    ppermute x12, waiting for transfers between devices: 103 us -> 88.1 us  [advance(): self.up = lax.ppermute(up, 'wide', [(w, w + 2) for w in range(2 * t)])]
    ppermute x12, waiting for transfers between devices: 11.9 us -> 0.85 us  [hop(): lax.ppermute(up, 'wide', [(w, w + 2) for w in range(2 * (t - 1), 2 * (chi...]
    convert_element_type x6 -> x0, other arithmetic: 9.22 us -> none  [messages(): up = (up.astype(F32) + arrived[0].astype(F32)).astype(BF16)]
    ppermute x12, waiting for transfers between devices: 13.4 us -> 21.8 us  [advance(): lax.ppermute(down, 'wide', [(w, w - 2) for w in range(2 * far, 2 * chips)])]
    unnamed x90 -> x114, local copies, waits for them, and re-layouts: 13.6 us -> 18.4 us
  transfers between devices with their start and end apart: 58 -> 58, of which waited for: 25 -> 27; matrix products, arithmetic and copies ran while one was open for 12% -> 15% of each run, Pallas kernels for 4% -> 5%
where the time goes in v4:
time: 492 us; the launch traced here: 488 us
  waiting for transfers between devices  199 us (40%)
  starting transfers between devices  114 us (23%)
  matrix products  50.8 us (10%)
  Pallas kernels  47.3 us (10%)
  other arithmetic  34 us (7%)
  local copies, waits for them, and re-layouts  26.9 us (5%)
  between operations  15.8 us (3%)
    ppermute x12, waiting for transfers between devices, advance(): self.up = lax.ppermute(up, 'wide', [(w, w + 2) for w in range(2 * t)])  88.1 us
    ppermute x12, waiting for transfers between devices, hop(): lax.ppermute(down, 'wide', [(w, w - 2) for w in range(2, 2 * (chips - t +...  85.3 us
    ppermute x12, starting transfers between devices, advance(): self.up = lax.ppermute(up, 'wide', [(w, w + 2) for w in range(2 * t)])  60.6 us
    dot_general x8, matrix products, row_product(): lax.dot_general(a, b, (((0,), (0,)), ((), ())), preferred_element_type=F32)  27.8 us
    ppermute x12, starting transfers between devices, hop(): lax.ppermute(up, 'wide', [(w, w + 2) for w in range(2 * (t - 1), 2 * (chi...  24.9 us
    dot_general x8, matrix products, nn(): lax.dot_general(a, b, (((1,), (0,)), ((), ())), preferred_element_type=F32)  23 us
    ppermute x12, waiting for transfers between devices, advance(): lax.ppermute(down, 'wide', [(w, w - 2) for w in range(2 * far, 2 * chips)])  21.8 us
    unnamed x114, local copies, waits for them, and re-layouts  18.4 us
  transfers between devices with their start and end apart: 58, of which 27 were waited for; matrix products, arithmetic and copies ran while one was open for 15% of the time, Pallas kernels for 5%

profile of v4, /device:TPU:0, one launch (start us, length us, event | category | flops | bytes accessed | tf_op | source)
XLA Modules:
  0.0 487.9 jit_solution(7123127156555937832)
XLA Ops:
  10.5 5.0 %collective-permute-start = (bf16[512,768]{1,0:T(8,128)(2,1)S(1)}, bf16[512,768]{1,0:T(8,128)(2,1)S(1)}, u32[]{:S(2)}, u32[]{:S(2)}) collective-permute-start(bf16[512,768]{1,0:T(8,128)(2,1)S(1)} %pad_maximum_fusion.2.refs_0_), channel_id=1, source_target_pairs={{0,8},{4,12},{8,16},{12,20},{16,24},{20,28},{1,9},{5,13},{9,17},{1... | collective-permute-start | bytes 2359304 | tf_op jit(solution)/shard_map/ppermute | solution.py:276
  16.8 2.8 copy-done
  19.6 6.1 %norm_and_split.1 = (bf16[768,2048]{1,0:T(8,128)(2,1)S(1)}, bf16[768,2048]{1,0:T(8,128)(2,1)S(1)}, bf16[768,2048]{1,0:T(8,128)(2,1)S(1)}, bf16[768,2048]{1,0:T(8,128)(2,1)S(1)}) custom-call(s32[1]{0:T(128)} %bitcast.core_ref, bf16[768,4096]{1,0:T(8,128)(2,1)S(1)} %copy-done, f32[1,4096]{1,0:T(1,128)S(1)} %bitcast.115, bf16[768,4096]{1,0:T(8,128)(2,1)} %grad_ref.1), custom_call_target="tpu_custom_call" | custom-call | flops 1 | bytes 1 | tf_op jit(solution)/shard_map/norm_and_split/pallas_call | solution.py:155
  32.5 3.8 collective-permute-done.1.refs_4_
  39.2 7.7 %collective-permute-start.4 = (bf16[512,512]{1,0:T(8,128)(2,1)S(1)}, bf16[512,512]{1,0:T(8,128)(2,1)}, u32[]{:S(2)}, u32[]{:S(2)}) collective-permute-start(bf16[512,512]{1,0:T(8,128)(2,1)S(1)} %get-tuple-element.130.refs_0_), channel_id=1, source_target_pairs={{0,8},{4,12},{8,16},{12,20},{16,24},{20,28},{1,9},{5,13},{9,17},{1... | collective-permute-start | bytes 1572872 | tf_op jit(solution)/shard_map/ppermute | solution.py:276
  49.0 12.9 %collective-permute-done.3.refs_5_ = bf16[512,768]{1,0:T(8,128)(2,1)} collective-permute-done((bf16[512,768]{1,0:T(8,128)(2,1)S(1)}, bf16[512,768]{1,0:T(8,128)(2,1)}, u32[]{:S(2)}, u32[]{:S(2)}) %collective-permute-start.3) | collective-permute-done | bytes 786464 | tf_op jit(solution)/shard_map/ppermute | solution.py:279
  64.7 8.4 %collective-permute-done.5.refs_4_ = bf16[512,512]{1,0:T(8,128)(2,1)} collective-permute-done((bf16[512,512]{1,0:T(8,128)(2,1)S(1)}, bf16[512,512]{1,0:T(8,128)(2,1)}, u32[]{:S(2)}, u32[]{:S(2)}) %collective-permute-start.5) | collective-permute-done | bytes 524320 | tf_op jit(solution)/shard_map/ppermute | solution.py:279
  75.9 14.1 %collective-permute-done.7.refs_6_ = bf16[512,768]{1,0:T(8,128)(2,1)} collective-permute-done((bf16[512,768]{1,0:T(8,128)(2,1)}, bf16[512,768]{1,0:T(8,128)(2,1)}, u32[]{:S(2)}, u32[]{:S(2)}) %collective-permute-start.7) | collective-permute-done | bytes 786464 | tf_op jit(solution)/shard_map/ppermute | solution.py:279
  90.0 8.8 %collective-permute-done.9.refs_5_ = bf16[512,512]{1,0:T(8,128)(2,1)} collective-permute-done((bf16[512,512]{1,0:T(8,128)(2,1)}, bf16[512,512]{1,0:T(8,128)(2,1)}, u32[]{:S(2)}, u32[]{:S(2)}) %collective-permute-start.9) | collective-permute-done | bytes 524320 | tf_op jit(solution)/shard_map/ppermute | solution.py:279
  101.4 2.6 fusion.26
  104.0 2.7 collective-permute-done.10
  106.8 2.6 add_convert_fusion.6.qkv_ref
  109.4 5.2 %attend_forward.2 = (bf16[768,512]{1,0:T(8,128)(2,1)S(1)}, f32[4,768]{1,0:T(4,128)S(1)}) custom-call(bf16[768,768]{1,0:T(8,128)(2,1)S(1)} %add_convert_fusion.6.qkv_ref), custom_call_target="tpu_custom_call" | custom-call | flops 1 | bytes 1 | tf_op jit(solution)/shard_map/attend_forward/pallas_call | solution.py:70
  114.6 3.2 convolution_convert_fusion.7
  123.3 3.7 convolution_convert_fusion.6
  127.1 2.2 add_convert_fusion.3
  130.4 22.6 %collective-permute-done.13.refs_6_ = bf16[512,512]{1,0:T(8,128)(2,1)S(1)} collective-permute-done((bf16[512,512]{1,0:T(8,128)(2,1)}, bf16[512,512]{1,0:T(8,128)(2,1)S(1)}, u32[]{:S(2)}, u32[]{:S(2)}) %collective-permute-start.13) | collective-permute-done | bytes 524320 | tf_op jit(solution)/shard_map/ppermute | solution.py:279
  158.3 3.7 fusion.27
  164.1 3.4 add_convert_fusion.8.grad_ref
  167.5 2.2 collective-permute-done.17
  171.1 6.0 %attend_backward.2 = bf16[768,768]{1,0:T(8,128)(2,1)S(1)} custom-call(bf16[768,768]{1,0:T(8,128)(2,1)S(1)} %add_convert_fusion.6.qkv_ref, bf16[768,512]{1,0:T(8,128)(2,1)S(1)} %add_convert_fusion.8.grad_ref, f32[4,768]{1,0:T(4,128)S(1)} %get-tuple-element.137.lse_ref), custom_call_target="tpu_custom_call" | custom-call | flops 1 | bytes 1 | tf_op jit(solution)/shard_map/attend_backward/pallas_call | solution.py:115
  177.2 7.5 %collective-permute-done.20.refs_5_ = bf16[512,768]{1,0:T(8,128)(2,1)S(1)} collective-permute-done((bf16[512,768]{1,0:T(8,128)(2,1)}, bf16[512,768]{1,0:T(8,128)(2,1)S(1)}, u32[]{:S(2)}, u32[]{:S(2)}) %collective-permute-start.20) | collective-permute-done | bytes 786464 | tf_op jit(solution)/shard_map/ppermute | solution.py:279
  184.7 4.1 convolution_convert_fusion.3
  192.4 2.6 collective-permute-start.24
  196.3 7.1 %collective-permute-done.21 = bf16[512,512]{1,0:T(8,128)(2,1)S(1)} collective-permute-done((bf16[512,512]{1,0:T(8,128)(2,1)}, bf16[512,512]{1,0:T(8,128)(2,1)S(1)}, u32[]{:S(2)}, u32[]{:S(2)}) %collective-permute-start.21) | collective-permute-done | bytes 524320 | tf_op jit(solution)/shard_map/ppermute | solution.py:339
  206.2 2.5 fusion.15
  208.7 4.6 convolution_convert_fusion.2
  214.1 5.7 %collective-permute-start.26 = (bf16[512,512]{1,0:T(8,128)(2,1)S(1)}, bf16[512,512]{1,0:T(8,128)(2,1)}, u32[]{:S(2)}, u32[]{:S(2)}) collective-permute-start(bf16[512,512]{1,0:T(8,128)(2,1)S(1)} %get-tuple-element.143), channel_id=1, source_target_pairs={{0,8},{4,12},{8,16},{12,20},{16,24},{20,28},{1,9},{5,13},{9,17},{1... | collective-permute-start | bytes 1572872 | tf_op jit(solution)/shard_map/ppermute | solution.py:339
  221.2 2.9 add_convert_fusion.1
  226.9 2.7 collective-permute-done.26
  231.0 8.9 %collective-permute-done.27 = bf16[512,512]{1,0:T(8,128)(2,1)} collective-permute-done((bf16[512,512]{1,0:T(8,128)(2,1)}, bf16[512,512]{1,0:T(8,128)(2,1)}, u32[]{:S(2)}, u32[]{:S(2)}) %collective-permute-start.27) | collective-permute-done | bytes 524320 | tf_op jit(solution)/shard_map/ppermute | solution.py:340
  239.9 2.5 fusion.19
  243.2 7.2 %collective-permute-done.31.refs_5_ = bf16[512,512]{1,0:T(8,128)(2,1)} collective-permute-done((bf16[512,512]{1,0:T(8,128)(2,1)}, bf16[512,512]{1,0:T(8,128)(2,1)}, u32[]{:S(2)}, u32[]{:S(2)}) %collective-permute-start.31) | collective-permute-done | bytes 524320 | tf_op jit(solution)/shard_map/ppermute | solution.py:279
  255.1 2.6 fusion.28
  258.0 2.6 add_convert_fusion.5.qkv_ref
  260.6 10.9 %collective-permute-done.33 = bf16[512,768]{1,0:T(8,128)(2,1)S(1)} collective-permute-done((bf16[512,768]{1,0:T(8,128)(2,1)S(1)}, bf16[512,768]{1,0:T(8,128)(2,1)S(1)}, u32[]{:S(2)}, u32[]{:S(2)}) %collective-permute-start.33) | collective-permute-done | bytes 786464 | tf_op jit(solution)/shard_map/ppermute | solution.py:339
  271.9 5.2 %attend_forward.3 = (bf16[768,512]{1,0:T(8,128)(2,1)S(1)}, f32[4,768]{1,0:T(4,128)S(1)}) custom-call(bf16[768,768]{1,0:T(8,128)(2,1)S(1)} %add_convert_fusion.5.qkv_ref), custom_call_target="tpu_custom_call" | custom-call | flops 1 | bytes 1 | tf_op jit(solution)/shard_map/attend_forward/pallas_call | solution.py:70
  281.0 4.6 collective-permute-start.36
  290.3 12.6 %collective-permute-done.36 = bf16[512,768]{1,0:T(8,128)(2,1)S(1)} collective-permute-done((bf16[512,768]{1,0:T(8,128)(2,1)S(1)}, bf16[512,768]{1,0:T(8,128)(2,1)S(1)}, u32[]{:S(2)}, u32[]{:S(2)}) %collective-permute-start.36) | collective-permute-done | bytes 786464 | tf_op jit(solution)/shard_map/ppermute | solution.py:339
  306.0 5.0 %project.2 = bf16[768,2048]{1,0:T(8,128)(2,1)} custom-call(bf16[768,512]{1,0:T(8,128)(2,1)S(1)} %copy-done.4, bf16[768,512]{1,0:T(8,128)(2,1)S(1)} %get-tuple-element.164.refs_1_, bf16[2048,512]{1,0:T(8,128)(2,1)S(1)} %collect.5.refs_2_, bf16[2048,512]{1,0:T(8,128)(2,1)S(1)} %collect.7.refs_3_), custom_call_target="tpu_custom_call" | custom-call | flops 1 | bytes 1 | tf_op jit(solution)/shard_map/project/pallas_call | solution.py:214
  314.0 6.6 %collective-permute-start.41 = (bf16[512,768]{1,0:T(8,128)(2,1)}, bf16[512,768]{1,0:T(8,128)(2,1)S(1)}, u32[]{:S(2)}, u32[]{:S(2)}) collective-permute-start(bf16[512,768]{1,0:T(8,128)(2,1)} %get-tuple-element.169), channel_id=1, source_target_pairs={{0,8},{4,12},{8,16},{12,20},{16,24},{20,28},{1,9},{5,13},{9,17},{1... | collective-permute-start | bytes 2359304 | tf_op jit(solution)/shard_map/ppermute | solution.py:339
  323.8 3.7 fusion.29
  330.0 8.7 %collective-permute-done.41 = bf16[512,768]{1,0:T(8,128)(2,1)S(1)} collective-permute-done((bf16[512,768]{1,0:T(8,128)(2,1)}, bf16[512,768]{1,0:T(8,128)(2,1)S(1)}, u32[]{:S(2)}, u32[]{:S(2)}) %collective-permute-start.41) | collective-permute-done | bytes 786464 | tf_op jit(solution)/shard_map/ppermute | solution.py:339
  338.8 5.3 %collective-permute-done.42 = bf16[512,768]{1,0:T(8,128)(2,1)S(1)} collective-permute-done((bf16[512,768]{1,0:T(8,128)(2,1)}, bf16[512,768]{1,0:T(8,128)(2,1)S(1)}, u32[]{:S(2)}, u32[]{:S(2)}) %collective-permute-start.42) | collective-permute-done | bytes 786464 | tf_op jit(solution)/shard_map/ppermute | solution.py:340
  344.0 2.5 fusion.5
  346.6 2.7 collective-permute-done.43
  350.6 6.1 %attend_backward.3 = bf16[768,768]{1,0:T(8,128)(2,1)S(1)} custom-call(bf16[768,768]{1,0:T(8,128)(2,1)S(1)} %add_convert_fusion.5.qkv_ref, bf16[768,512]{1,0:T(8,128)(2,1)S(1)} %add_convert_fusion.7.grad_ref, f32[4,768]{1,0:T(4,128)S(1)} %get-tuple-element.182.lse_ref), custom_call_target="tpu_custom_call" | custom-call | flops 1 | bytes 1 | tf_op jit(solution)/shard_map/attend_backward/pallas_call | solution.py:115
  356.7 4.0 convolution_convert_fusion.1
  360.7 6.4 %project.3 = bf16[768,2048]{1,0:T(8,128)(2,1)} custom-call(bf16[768,512]{1,0:T(8,128)(2,1)S(1)} %copy-done.5, bf16[768,512]{1,0:T(8,128)(2,1)S(1)} %copy-done.7, bf16[2048,512]{1,0:T(8,128)(2,1)} %collective-permute-done.16.refs_2_, bf16[2048,512]{1,0:T(8,128)(2,1)S(1)} %collective-permute-done.40.refs_3_), custom_call_target="tpu_custom_call" | custom-call | flops 1 | bytes 1 | tf_op jit(solution)/shard_map/project/pallas_call | solution.py:214
  367.1 4.7 collective-permute-start.46
  371.8 4.6 convolution_convert_fusion
  377.1 2.9 add_convert_fusion
  380.1 3.6 collective-permute-done.46
  384.0 13.0 %collective-permute-start.48 = (bf16[512,512]{1,0:T(8,128)(2,1)S(1)}, bf16[512,512]{1,0:T(8,128)(2,1)S(1)}, u32[]{:S(2)}, u32[]{:S(2)}) collective-permute-start(bf16[512,512]{1,0:T(8,128)(2,1)S(1)} %get-tuple-element.190), channel_id=1, source_target_pairs={{0,8},{4,12},{8,16},{12,20},{16,24},{20,28},{1,9},{5,13},{9,17},{1... | collective-permute-start | bytes 1572872 | tf_op jit(solution)/shard_map/ppermute | solution.py:339
  398.3 4.6 collective-permute-start.50
  403.6 5.7 %collective-permute-done.48 = bf16[512,512]{1,0:T(8,128)(2,1)S(1)} collective-permute-done((bf16[512,512]{1,0:T(8,128)(2,1)S(1)}, bf16[512,512]{1,0:T(8,128)(2,1)S(1)}, u32[]{:S(2)}, u32[]{:S(2)}) %collective-permute-start.48) | collective-permute-done | bytes 524320 | tf_op jit(solution)/shard_map/ppermute | solution.py:339
  409.3 2.6 collective-permute-done.49
  412.1 12.5 %collective-permute-done.50 = bf16[512,768]{1,0:T(8,128)(2,1)S(1)} collective-permute-done((bf16[512,768]{1,0:T(8,128)(2,1)S(1)}, bf16[512,768]{1,0:T(8,128)(2,1)S(1)}, u32[]{:S(2)}, u32[]{:S(2)}) %collective-permute-start.50) | collective-permute-done | bytes 786464 | tf_op jit(solution)/shard_map/ppermute | solution.py:339
  425.1 4.4 collective-permute-start.52
  431.7 13.3 %collective-permute-done.52 = bf16[512,768]{1,0:T(8,128)(2,1)S(1)} collective-permute-done((bf16[512,768]{1,0:T(8,128)(2,1)S(1)}, bf16[512,768]{1,0:T(8,128)(2,1)S(1)}, u32[]{:S(2)}, u32[]{:S(2)}) %collective-permute-start.52) | collective-permute-done | bytes 786464 | tf_op jit(solution)/shard_map/ppermute | solution.py:339
  446.6 9.2 %collective-permute-start.54 = (bf16[512,768]{1,0:T(8,128)(2,1)}, bf16[512,768]{1,0:T(8,128)(2,1)}, u32[]{:S(2)}, u32[]{:S(2)}) collective-permute-start(bf16[512,768]{1,0:T(8,128)(2,1)} %get-tuple-element.199), channel_id=1, source_target_pairs={{0,8},{4,12},{8,16},{12,20},{16,24},{20,28},{1,9},{5,13},{9,17},{1... | collective-permute-start | bytes 2359304 | tf_op jit(solution)/shard_map/ppermute | solution.py:339
  460.7 3.1 add_convert_fusion.4
  463.8 6.1 %collective-permute-done.54 = bf16[512,768]{1,0:T(8,128)(2,1)} collective-permute-done((bf16[512,768]{1,0:T(8,128)(2,1)}, bf16[512,768]{1,0:T(8,128)(2,1)}, u32[]{:S(2)}, u32[]{:S(2)}) %collective-permute-start.54) | collective-permute-done | bytes 786464 | tf_op jit(solution)/shard_map/ppermute | solution.py:339
  469.9 5.0 %collective-permute-done.55 = bf16[512,768]{1,0:T(8,128)(2,1)} collective-permute-done((bf16[512,768]{1,0:T(8,128)(2,1)}, bf16[512,768]{1,0:T(8,128)(2,1)}, u32[]{:S(2)}, u32[]{:S(2)}) %collective-permute-start.55) | collective-permute-done | bytes 786464 | tf_op jit(solution)/shard_map/ppermute | solution.py:340
  (232 shorter events, 99.5 us)
Async XLA Ops:
  7.2 452.0 %reduce-scatter.3.cloned.1.call-start = ((), (), s32[]{:S(2)}) async-start(), calls=%async_computation.2 | async-start | bytes 3932160 | tf_op jit(solution)/shard_map/reduce_scatter | solution.py:393
  10.5 22.1 %collective-permute-start = (bf16[512,768]{1,0:T(8,128)(2,1)S(1)}, bf16[512,768]{1,0:T(8,128)(2,1)S(1)}, u32[]{:S(2)}, u32[]{:S(2)}) collective-permute-start(bf16[512,768]{1,0:T(8,128)(2,1)S(1)} %pad_maximum_fusion.2.refs_0_), channel_id=1, source_target_pairs={{0,8},{4,12},{8,16},{12,20},{16,24},{20,28},{1,9},{5,13},{9,17},{1... | collective-permute-start | bytes 2359304 | tf_op jit(solution)/shard_map/ppermute | solution.py:276
  15.5 20.9 %collective-permute-start.1 = (bf16[512,768]{1,0:T(8,128)(2,1)S(1)}, bf16[512,768]{1,0:T(8,128)(2,1)S(1)}, u32[]{:S(2)}, u32[]{:S(2)}) collective-permute-start(bf16[512,768]{1,0:T(8,128)(2,1)S(1)} %pad_maximum_fusion.2.refs_0_), channel_id=1, source_target_pairs={{8,0},{12,4},{16,8},{20,12},{24,16},{28,20},{9,1},{13,5},{17,9},{2... | collective-permute-start | bytes 2359304 | tf_op jit(solution)/shard_map/ppermute | solution.py:279
  36.4 12.7 %collective-permute-start.2 = (bf16[512,768]{1,0:T(8,128)(2,1)S(1)}, bf16[512,768]{1,0:T(8,128)(2,1)S(1)}, u32[]{:S(2)}, u32[]{:S(2)}) collective-permute-start(bf16[512,768]{1,0:T(8,128)(2,1)S(1)} %collective-permute-done.refs_1_), channel_id=1, source_target_pairs={{8,16},{12,20},{16,24},{20,28},{9,17},{13,21},{17,25},{21,29},{10,... | collective-permute-start | bytes 2359304 | tf_op jit(solution)/shard_map/ppermute | solution.py:276
  37.1 24.8 %collective-permute-start.3 = (bf16[512,768]{1,0:T(8,128)(2,1)S(1)}, bf16[512,768]{1,0:T(8,128)(2,1)}, u32[]{:S(2)}, u32[]{:S(2)}) collective-permute-start(bf16[512,768]{1,0:T(8,128)(2,1)S(1)} %collective-permute-done.1.refs_4_), channel_id=1, source_target_pairs={{8,0},{12,4},{16,8},{20,12},{9,1},{13,5},{17,9},{21,13},{10,2},{14... | collective-permute-start | bytes 2359304 | tf_op jit(solution)/shard_map/ppermute | solution.py:279
  39.2 25.5 %collective-permute-start.4 = (bf16[512,512]{1,0:T(8,128)(2,1)S(1)}, bf16[512,512]{1,0:T(8,128)(2,1)}, u32[]{:S(2)}, u32[]{:S(2)}) collective-permute-start(bf16[512,512]{1,0:T(8,128)(2,1)S(1)} %get-tuple-element.130.refs_0_), channel_id=1, source_target_pairs={{0,8},{4,12},{8,16},{12,20},{16,24},{20,28},{1,9},{5,13},{9,17},{1... | collective-permute-start | bytes 1572872 | tf_op jit(solution)/shard_map/ppermute | solution.py:276
  46.9 26.2 %collective-permute-start.5 = (bf16[512,512]{1,0:T(8,128)(2,1)S(1)}, bf16[512,512]{1,0:T(8,128)(2,1)}, u32[]{:S(2)}, u32[]{:S(2)}) collective-permute-start(bf16[512,512]{1,0:T(8,128)(2,1)S(1)} %get-tuple-element.130.refs_0_), channel_id=1, source_target_pairs={{8,0},{12,4},{16,8},{20,12},{24,16},{28,20},{9,1},{13,5},{17,9},{2... | collective-permute-start | bytes 1572872 | tf_op jit(solution)/shard_map/ppermute | solution.py:279
  61.9 14.0 %collective-permute-start.6 = (bf16[512,768]{1,0:T(8,128)(2,1)S(1)}, bf16[512,768]{1,0:T(8,128)(2,1)}, u32[]{:S(2)}, u32[]{:S(2)}) collective-permute-start(bf16[512,768]{1,0:T(8,128)(2,1)S(1)} %collective-permute-done.2.refs_2_), channel_id=1, source_target_pairs={{16,24},{20,28},{17,25},{21,29},{18,26},{22,30},{19,27},{23,31}} | collective-permute-start | bytes 2359304 | tf_op jit(solution)/shard_map/ppermute | solution.py:276
  63.4 26.5 %collective-permute-start.7 = (bf16[512,768]{1,0:T(8,128)(2,1)}, bf16[512,768]{1,0:T(8,128)(2,1)}, u32[]{:S(2)}, u32[]{:S(2)}) collective-permute-start(bf16[512,768]{1,0:T(8,128)(2,1)} %collective-permute-done.3.refs_5_), channel_id=1, source_target_pairs={{8,0},{12,4},{9,1},{13,5},{10,2},{14,6},{11,3},{15,7}} | collective-permute-start | bytes 2359304 | tf_op jit(solution)/shard_map/ppermute | solution.py:279
  73.1 16.9 %collective-permute-start.8 = (bf16[512,512]{1,0:T(8,128)(2,1)}, bf16[512,512]{1,0:T(8,128)(2,1)}, u32[]{:S(2)}, u32[]{:S(2)}) collective-permute-start(bf16[512,512]{1,0:T(8,128)(2,1)} %collective-permute-done.4.refs_1_), channel_id=1, source_target_pairs={{8,16},{12,20},{16,24},{20,28},{9,17},{13,21},{17,25},{21,29},{10,... | collective-permute-start | bytes 1572872 | tf_op jit(solution)/shard_map/ppermute | solution.py:276
  74.6 24.2 %collective-permute-start.9 = (bf16[512,512]{1,0:T(8,128)(2,1)}, bf16[512,512]{1,0:T(8,128)(2,1)}, u32[]{:S(2)}, u32[]{:S(2)}) collective-permute-start(bf16[512,512]{1,0:T(8,128)(2,1)} %collective-permute-done.5.refs_4_), channel_id=1, source_target_pairs={{8,0},{12,4},{16,8},{20,12},{9,1},{13,5},{17,9},{21,13},{10,2},{14... | collective-permute-start | bytes 1572872 | tf_op jit(solution)/shard_map/ppermute | solution.py:279
  101.0 5.7 %collective-permute-start.10 = (bf16[2048,768]{1,0:T(8,128)(2,1)S(1)}, bf16[2048,768]{1,0:T(8,128)(2,1)S(1)}, u32[]{:S(2)}, u32[]{:S(2)}) collective-permute-start(bf16[2048,768]{1,0:T(8,128)(2,1)S(1)} %collect.4), channel_id=1, source_target_pairs={{0,4},{4,0},{8,12},{12,8},{16,20},{20,16},{24,28},{28,24},{1,5},{5... | collective-permute-start | bytes 9437192 | tf_op jit(solution)/shard_map/ppermute | solution.py:255
  117.8 9.3 %collective-permute-start.11 = (bf16[2048,512]{1,0:T(8,128)(2,1)}, bf16[2048,512]{1,0:T(8,128)(2,1)}, u32[]{:S(2)}, u32[]{:S(2)}) collective-permute-start(bf16[2048,512]{1,0:T(8,128)(2,1)} %convolution_convert_fusion.7), channel_id=1, source_target_pairs={{0,4},{4,0},{8,12},{12,8},{16,20},{20,16},{24,28},{28,24},{1,5},{5... | collective-permute-start | bytes 6291464 | tf_op jit(solution)/shard_map/ppermute | solution.py:255
  118.0 12.4 %collective-permute-start.12 = (bf16[512,512]{1,0:T(8,128)(2,1)}, bf16[512,512]{1,0:T(8,128)(2,1)S(1)}, u32[]{:S(2)}, u32[]{:S(2)}) collective-permute-start(bf16[512,512]{1,0:T(8,128)(2,1)} %collective-permute-done.8.refs_2_), channel_id=1, source_target_pairs={{16,24},{20,28},{17,25},{21,29},{18,26},{22,30},{19,27},{23,31}} | collective-permute-start | bytes 1572872 | tf_op jit(solution)/shard_map/ppermute | solution.py:276
  118.7 34.3 %collective-permute-start.14 = (bf16[512,768]{1,0:T(8,128)(2,1)S(1)}, bf16[512,768]{1,0:T(8,128)(2,1)S(1)}, u32[]{:S(2)}, u32[]{:S(2)}) collective-permute-start(bf16[512,768]{1,0:T(8,128)(2,1)S(1)} %pad_maximum_fusion.3.refs_0_), channel_id=1, source_target_pairs={{0,8},{4,12},{8,16},{12,20},{16,24},{20,28},{1,9},{5,13},{9,17},{1... | collective-permute-start | bytes 2359304 | tf_op jit(solution)/shard_map/ppermute | solution.py:276
  120.2 33.7 %collective-permute-start.15 = (bf16[512,768]{1,0:T(8,128)(2,1)S(1)}, bf16[512,768]{1,0:T(8,128)(2,1)}, u32[]{:S(2)}, u32[]{:S(2)}) collective-permute-start(bf16[512,768]{1,0:T(8,128)(2,1)S(1)} %pad_maximum_fusion.3.refs_0_), channel_id=1, source_target_pairs={{8,0},{12,4},{16,8},{20,12},{24,16},{28,20},{9,1},{13,5},{17,9},{2... | collective-permute-start | bytes 2359304 | tf_op jit(solution)/shard_map/ppermute | solution.py:279
  121.5 31.5 %collective-permute-start.13 = (bf16[512,512]{1,0:T(8,128)(2,1)}, bf16[512,512]{1,0:T(8,128)(2,1)S(1)}, u32[]{:S(2)}, u32[]{:S(2)}) collective-permute-start(bf16[512,512]{1,0:T(8,128)(2,1)} %collective-permute-done.9.refs_5_), channel_id=1, source_target_pairs={{8,0},{12,4},{9,1},{13,5},{10,2},{14,6},{11,3},{15,7}} | collective-permute-start | bytes 1572872 | tf_op jit(solution)/shard_map/ppermute | solution.py:279
  129.3 26.3 %copy-start.41 = (bf16[2048,512]{1,0:T(8,128)(2,1)}, bf16[2048,512]{1,0:T(8,128)(2,1)S(1)}, u32[]{:S(2)}) copy-start(bf16[2048,512]{1,0:T(8,128)(2,1)S(1)} %add_convert_fusion.3) | copy-start | bytes 6291460
  129.3 24.6 %copy-start.13 = (bf16[512,512]{1,0:T(8,128)(2,1)S(1)}, bf16[512,512]{1,0:T(8,128)(2,1)}, u32[]{:S(2)}) copy-start(bf16[512,512]{1,0:T(8,128)(2,1)} %copy-done.12) | copy-start | bytes 1572868
  155.6 8.5 %collective-permute-start.16 = (bf16[2048,512]{1,0:T(8,128)(2,1)S(1)}, bf16[2048,512]{1,0:T(8,128)(2,1)}, u32[]{:S(2)}, u32[]{:S(2)}) collective-permute-start(bf16[2048,512]{1,0:T(8,128)(2,1)S(1)} %collect.5.refs_2_), channel_id=1, source_target_pairs={{0,4},{4,0},{8,12},{12,8},{16,20},{20,16},{24,28},{28,24},{1,5},{5... | collective-permute-start | bytes 6291464 | tf_op jit(solution)/shard_map/ppermute | solution.py:255
  155.7 14.1 %collective-permute-start.17 = (bf16[512,512]{1,0:T(8,128)(2,1)}, bf16[512,512]{1,0:T(8,128)(2,1)S(1)}, u32[]{:S(2)}, u32[]{:S(2)}) collective-permute-start(bf16[512,512]{1,0:T(8,128)(2,1)} %get-tuple-element.125), channel_id=1, source_target_pairs={{0,8},{4,12},{1,9},{5,13},{2,10},{6,14},{3,11},{7,15}} | collective-permute-start | bytes 1572872 | tf_op jit(solution)/shard_map/ppermute | solution.py:339
  157.6 19.6 %collective-permute-start.19 = (bf16[512,768]{1,0:T(8,128)(2,1)}, bf16[512,768]{1,0:T(8,128)(2,1)S(1)}, u32[]{:S(2)}, u32[]{:S(2)}) collective-permute-start(bf16[512,768]{1,0:T(8,128)(2,1)} %copy-done.16), channel_id=1, source_target_pairs={{8,16},{12,20},{16,24},{20,28},{9,17},{13,21},{17,25},{21,29},{10,... | collective-permute-start | bytes 2359304 | tf_op jit(solution)/shard_map/ppermute | solution.py:276
  162.0 7.8 %collective-permute-start.18 = (bf16[512,512]{1,0:T(8,128)(2,1)S(1)}, bf16[512,512]{1,0:T(8,128)(2,1)S(1)}, u32[]{:S(2)}, u32[]{:S(2)}) collective-permute-start(bf16[512,512]{1,0:T(8,128)(2,1)S(1)} %copy-done.54), channel_id=1, source_target_pairs={{24,16},{28,20},{25,17},{29,21},{26,18},{30,22},{27,19},{31,23}} | collective-permute-start | bytes 1572872 | tf_op jit(solution)/shard_map/ppermute | solution.py:340
  162.8 21.9 %collective-permute-start.20 = (bf16[512,768]{1,0:T(8,128)(2,1)}, bf16[512,768]{1,0:T(8,128)(2,1)S(1)}, u32[]{:S(2)}, u32[]{:S(2)}) collective-permute-start(bf16[512,768]{1,0:T(8,128)(2,1)} %collective-permute-done.15.refs_4_), channel_id=1, source_target_pairs={{8,0},{12,4},{16,8},{20,12},{9,1},{13,5},{17,9},{21,13},{10,2},{14... | collective-permute-start | bytes 2359304 | tf_op jit(solution)/shard_map/ppermute | solution.py:279
  188.7 31.0 %collective-permute-start.23 = (bf16[2048,768]{1,0:T(8,128)(2,1)}, bf16[2048,768]{1,0:T(8,128)(2,1)}, u32[]{:S(2)}, u32[]{:S(2)}) collective-permute-start(bf16[2048,768]{1,0:T(8,128)(2,1)} %convolution_convert_fusion.3), channel_id=1, source_target_pairs={{0,4},{4,0},{8,12},{12,8},{16,20},{20,16},{24,28},{28,24},{1,5},{5... | collective-permute-start | bytes 9437192 | tf_op jit(solution)/shard_map/ppermute | solution.py:255
  188.8 14.6 %collective-permute-start.21 = (bf16[512,512]{1,0:T(8,128)(2,1)}, bf16[512,512]{1,0:T(8,128)(2,1)S(1)}, u32[]{:S(2)}, u32[]{:S(2)}) collective-permute-start(bf16[512,512]{1,0:T(8,128)(2,1)} %get-tuple-element.135), channel_id=1, source_target_pairs={{0,8},{4,12},{8,16},{12,20},{1,9},{5,13},{9,17},{13,21},{2,10},{6,... | collective-permute-start | bytes 1572872 | tf_op jit(solution)/shard_map/ppermute | solution.py:339
  190.9 14.1 %collective-permute-start.22 = (bf16[512,512]{1,0:T(8,128)(2,1)}, bf16[512,512]{1,0:T(8,128)(2,1)}, u32[]{:S(2)}, u32[]{:S(2)}) collective-permute-start(bf16[512,512]{1,0:T(8,128)(2,1)} %get-tuple-element.142), channel_id=1, source_target_pairs={{16,8},{20,12},{24,16},{28,20},{17,9},{21,13},{25,17},{29,21},{18,... | collective-permute-start | bytes 1572872 | tf_op jit(solution)/shard_map/ppermute | solution.py:340
  192.4 21.7 %collective-permute-start.24 = (bf16[512,512]{1,0:T(8,128)(2,1)S(1)}, bf16[512,512]{1,0:T(8,128)(2,1)}, u32[]{:S(2)}, u32[]{:S(2)}) collective-permute-start(bf16[512,512]{1,0:T(8,128)(2,1)S(1)} %copy-done.10), channel_id=1, source_target_pairs={{0,8},{4,12},{8,16},{12,20},{16,24},{20,28},{1,9},{5,13},{9,17},{1... | collective-permute-start | bytes 1572872 | tf_op jit(solution)/shard_map/ppermute | solution.py:276
  195.0 30.3 %collective-permute-start.25 = (bf16[512,512]{1,0:T(8,128)(2,1)S(1)}, bf16[512,512]{1,0:T(8,128)(2,1)}, u32[]{:S(2)}, u32[]{:S(2)}) collective-permute-start(bf16[512,512]{1,0:T(8,128)(2,1)S(1)} %copy-done.10), channel_id=1, source_target_pairs={{8,0},{12,4},{16,8},{20,12},{24,16},{28,20},{9,1},{13,5},{17,9},{2... | collective-permute-start | bytes 1572872 | tf_op jit(solution)/shard_map/ppermute | solution.py:279
  203.4 39.0 %collective-permute-start.28 = (bf16[512,768]{1,0:T(8,128)(2,1)}, bf16[512,768]{1,0:T(8,128)(2,1)}, u32[]{:S(2)}, u32[]{:S(2)}) collective-permute-start(bf16[512,768]{1,0:T(8,128)(2,1)} %copy-done.18), channel_id=1, source_target_pairs={{16,24},{20,28},{17,25},{21,29},{18,26},{22,30},{19,27},{23,31}} | collective-permute-start | bytes 2359304 | tf_op jit(solution)/shard_map/ppermute | solution.py:276
  205.0 37.5 %collective-permute-start.29 = (bf16[512,768]{1,0:T(8,128)(2,1)}, bf16[512,768]{1,0:T(8,128)(2,1)}, u32[]{:S(2)}, u32[]{:S(2)}) collective-permute-start(bf16[512,768]{1,0:T(8,128)(2,1)} %copy-done.20), channel_id=1, source_target_pairs={{8,0},{12,4},{9,1},{13,5},{10,2},{14,6},{11,3},{15,7}} | collective-permute-start | bytes 2359304 | tf_op jit(solution)/shard_map/ppermute | solution.py:279
  214.1 15.5 %collective-permute-start.26 = (bf16[512,512]{1,0:T(8,128)(2,1)S(1)}, bf16[512,512]{1,0:T(8,128)(2,1)}, u32[]{:S(2)}, u32[]{:S(2)}) collective-permute-start(bf16[512,512]{1,0:T(8,128)(2,1)S(1)} %get-tuple-element.143), channel_id=1, source_target_pairs={{0,8},{4,12},{8,16},{12,20},{16,24},{20,28},{1,9},{5,13},{9,17},{1... | collective-permute-start | bytes 1572872 | tf_op jit(solution)/shard_map/ppermute | solution.py:339
  219.8 20.1 %collective-permute-start.27 = (bf16[512,512]{1,0:T(8,128)(2,1)}, bf16[512,512]{1,0:T(8,128)(2,1)}, u32[]{:S(2)}, u32[]{:S(2)}) collective-permute-start(bf16[512,512]{1,0:T(8,128)(2,1)} %get-tuple-element.150), channel_id=1, source_target_pairs={{8,0},{12,4},{16,8},{20,12},{24,16},{28,20},{9,1},{13,5},{17,9},{2... | collective-permute-start | bytes 1572872 | tf_op jit(solution)/shard_map/ppermute | solution.py:340
  224.1 26.3 %copy-start.9 = (bf16[512,768]{1,0:T(8,128)(2,1)S(1)}, bf16[512,768]{1,0:T(8,128)(2,1)}, u32[]{:S(2)}) copy-start(bf16[512,768]{1,0:T(8,128)(2,1)} %copy-done.8) | copy-start | bytes 2359300
  226.2 16.2 %collective-permute-start.30 = (bf16[512,512]{1,0:T(8,128)(2,1)}, bf16[512,512]{1,0:T(8,128)(2,1)S(1)}, u32[]{:S(2)}, u32[]{:S(2)}) collective-permute-start(bf16[512,512]{1,0:T(8,128)(2,1)} %collective-permute-done.24.refs_1_), channel_id=1, source_target_pairs={{8,16},{12,20},{16,24},{20,28},{9,17},{13,21},{17,25},{21,29},{10,... | collective-permute-start | bytes 1572872 | tf_op jit(solution)/shard_map/ppermute | solution.py:276
  229.6 20.8 %collective-permute-start.31 = (bf16[512,512]{1,0:T(8,128)(2,1)}, bf16[512,512]{1,0:T(8,128)(2,1)}, u32[]{:S(2)}, u32[]{:S(2)}) collective-permute-start(bf16[512,512]{1,0:T(8,128)(2,1)} %collective-permute-done.25.refs_4_), channel_id=1, source_target_pairs={{8,0},{12,4},{16,8},{20,12},{9,1},{13,5},{17,9},{21,13},{10,2},{14... | collective-permute-start | bytes 1572872 | tf_op jit(solution)/shard_map/ppermute | solution.py:279
  230.9 19.5 %copy-start.17 = (bf16[512,768]{1,0:T(8,128)(2,1)S(1)}, bf16[512,768]{1,0:T(8,128)(2,1)}, u32[]{:S(2)}) copy-start(bf16[512,768]{1,0:T(8,128)(2,1)} %copy-done.16) | copy-start | bytes 2359300
  230.9 19.5 %copy-start.19 = (bf16[512,768]{1,0:T(8,128)(2,1)S(1)}, bf16[512,768]{1,0:T(8,128)(2,1)}, u32[]{:S(2)}) copy-start(bf16[512,768]{1,0:T(8,128)(2,1)} %copy-done.18) | copy-start | bytes 2359300
  252.3 5.7 %collective-permute-start.32 = (bf16[2048,768]{1,0:T(8,128)(2,1)S(1)}, bf16[2048,768]{1,0:T(8,128)(2,1)S(1)}, u32[]{:S(2)}, u32[]{:S(2)}) collective-permute-start(bf16[2048,768]{1,0:T(8,128)(2,1)S(1)} %collect.6), channel_id=1, source_target_pairs={{0,4},{4,0},{8,12},{12,8},{16,20},{20,16},{24,28},{28,24},{1,5},{5... | collective-permute-start | bytes 9437192 | tf_op jit(solution)/shard_map/ppermute | solution.py:255
  252.3 19.1 %collective-permute-start.33 = (bf16[512,768]{1,0:T(8,128)(2,1)S(1)}, bf16[512,768]{1,0:T(8,128)(2,1)S(1)}, u32[]{:S(2)}, u32[]{:S(2)}) collective-permute-start(bf16[512,768]{1,0:T(8,128)(2,1)S(1)} %copy-done.52), channel_id=1, source_target_pairs={{0,8},{4,12},{1,9},{5,13},{2,10},{6,14},{3,11},{7,15}} | collective-permute-start | bytes 2359304 | tf_op jit(solution)/shard_map/ppermute | solution.py:339
  254.4 17.1 %collective-permute-start.34 = (bf16[512,768]{1,0:T(8,128)(2,1)S(1)}, bf16[512,768]{1,0:T(8,128)(2,1)S(1)}, u32[]{:S(2)}, u32[]{:S(2)}) collective-permute-start(bf16[512,768]{1,0:T(8,128)(2,1)S(1)} %copy-done.51), channel_id=1, source_target_pairs={{24,16},{28,20},{25,17},{29,21},{26,18},{30,22},{27,19},{31,23}} | collective-permute-start | bytes 2359304 | tf_op jit(solution)/shard_map/ppermute | solution.py:340
  277.1 28.9 %copy-start.6 = (bf16[768,512]{1,0:T(8,128)(2,1)}, bf16[768,512]{1,0:T(8,128)(2,1)S(1)}, u32[]{:S(2)}) copy-start(bf16[768,512]{1,0:T(8,128)(2,1)S(1)} %get-tuple-element.164.refs_1_) | copy-start | bytes 2359300
  279.0 9.5 %collective-permute-start.35 = (bf16[2048,512]{1,0:T(8,128)(2,1)S(1)}, bf16[2048,512]{1,0:T(8,128)(2,1)S(1)}, u32[]{:S(2)}, u32[]{:S(2)}) collective-permute-start(bf16[2048,512]{1,0:T(8,128)(2,1)S(1)} %convolution_convert_fusion.5), channel_id=1, source_target_pairs={{0,4},{4,0},{8,12},{12,8},{16,20},{20,16},{24,28},{28,24},{1,5},{5... | collective-permute-start | bytes 6291464 | tf_op jit(solution)/shard_map/ppermute | solution.py:255
  279.0 25.4 %collective-permute-start.38 = (bf16[512,512]{1,0:T(8,128)(2,1)S(1)}, bf16[512,512]{1,0:T(8,128)(2,1)S(1)}, u32[]{:S(2)}, u32[]{:S(2)}) collective-permute-start(bf16[512,512]{1,0:T(8,128)(2,1)S(1)} %copy-done.23), channel_id=1, source_target_pairs={{16,24},{20,28},{17,25},{21,29},{18,26},{22,30},{19,27},{23,31}} | collective-permute-start | bytes 1572872 | tf_op jit(solution)/shard_map/ppermute | solution.py:276
  279.7 24.7 %collective-permute-start.39 = (bf16[512,512]{1,0:T(8,128)(2,1)}, bf16[512,512]{1,0:T(8,128)(2,1)S(1)}, u32[]{:S(2)}, u32[]{:S(2)}) collective-permute-start(bf16[512,512]{1,0:T(8,128)(2,1)} %collective-permute-done.31.refs_5_), channel_id=1, source_target_pairs={{8,0},{12,4},{9,1},{13,5},{10,2},{14,6},{11,3},{15,7}} | collective-permute-start | bytes 1572872 | tf_op jit(solution)/shard_map/ppermute | solution.py:279
  281.0 21.8 %collective-permute-start.36 = (bf16[512,768]{1,0:T(8,128)(2,1)S(1)}, bf16[512,768]{1,0:T(8,128)(2,1)S(1)}, u32[]{:S(2)}, u32[]{:S(2)}) collective-permute-start(bf16[512,768]{1,0:T(8,128)(2,1)S(1)} %get-tuple-element.160), channel_id=1, source_target_pairs={{0,8},{4,12},{8,16},{12,20},{1,9},{5,13},{9,17},{13,21},{2,10},{6,... | collective-permute-start | bytes 2359304 | tf_op jit(solution)/shard_map/ppermute | solution.py:339
  285.7 17.2 %collective-permute-start.37 = (bf16[512,768]{1,0:T(8,128)(2,1)S(1)}, bf16[512,768]{1,0:T(8,128)(2,1)S(1)}, u32[]{:S(2)}, u32[]{:S(2)}) collective-permute-start(bf16[512,768]{1,0:T(8,128)(2,1)S(1)} %get-tuple-element.168), channel_id=1, source_target_pairs={{16,8},{20,12},{24,16},{28,20},{17,9},{21,13},{25,17},{29,21},{18,... | collective-permute-start | bytes 2359304 | tf_op jit(solution)/shard_map/ppermute | solution.py:340
  312.4 146.8 %reduce-scatter.5.cloned.1.call-start = ((), (), s32[]{:S(2)}) async-start(), calls=%async_computation.3 | async-start | bytes 3932160 | tf_op jit(solution)/shard_map/reduce_scatter | solution.py:393
  314.0 14.2 %collective-permute-start.40 = (bf16[2048,512]{1,0:T(8,128)(2,1)S(1)}, bf16[2048,512]{1,0:T(8,128)(2,1)S(1)}, u32[]{:S(2)}, u32[]{:S(2)}) collective-permute-start(bf16[2048,512]{1,0:T(8,128)(2,1)S(1)} %copy-done.2), channel_id=1, source_target_pairs={{0,4},{4,0},{8,12},{12,8},{16,20},{20,16},{24,28},{28,24},{1,5},{5... | collective-permute-start | bytes 6291464 | tf_op jit(solution)/shard_map/ppermute | solution.py:255
  314.0 24.8 %collective-permute-start.41 = (bf16[512,768]{1,0:T(8,128)(2,1)}, bf16[512,768]{1,0:T(8,128)(2,1)S(1)}, u32[]{:S(2)}, u32[]{:S(2)}) collective-permute-start(bf16[512,768]{1,0:T(8,128)(2,1)} %get-tuple-element.169), channel_id=1, source_target_pairs={{0,8},{4,12},{8,16},{12,20},{16,24},{20,28},{1,9},{5,13},{9,17},{1... | collective-permute-start | bytes 2359304 | tf_op jit(solution)/shard_map/ppermute | solution.py:339
  320.6 28.7 %collective-permute-start.43 = (bf16[512,512]{1,0:T(8,128)(2,1)}, bf16[512,512]{1,0:T(8,128)(2,1)S(1)}, u32[]{:S(2)}, u32[]{:S(2)}) collective-permute-start(bf16[512,512]{1,0:T(8,128)(2,1)} %get-tuple-element.166), channel_id=1, source_target_pairs={{0,8},{4,12},{1,9},{5,13},{2,10},{6,14},{3,11},{7,15}} | collective-permute-start | bytes 1572872 | tf_op jit(solution)/shard_map/ppermute | solution.py:339
  322.5 21.5 %collective-permute-start.42 = (bf16[512,768]{1,0:T(8,128)(2,1)}, bf16[512,768]{1,0:T(8,128)(2,1)S(1)}, u32[]{:S(2)}, u32[]{:S(2)}) collective-permute-start(bf16[512,768]{1,0:T(8,128)(2,1)} %get-tuple-element.177), channel_id=1, source_target_pairs={{8,0},{12,4},{16,8},{20,12},{24,16},{28,20},{9,1},{13,5},{17,9},{2... | collective-permute-start | bytes 2359304 | tf_op jit(solution)/shard_map/ppermute | solution.py:340
  327.5 21.8 %collective-permute-start.44 = (bf16[512,512]{1,0:T(8,128)(2,1)S(1)}, bf16[512,512]{1,0:T(8,128)(2,1)S(1)}, u32[]{:S(2)}, u32[]{:S(2)}) collective-permute-start(bf16[512,512]{1,0:T(8,128)(2,1)S(1)} %copy-done.53), channel_id=1, source_target_pairs={{24,16},{28,20},{25,17},{29,21},{26,18},{30,22},{27,19},{31,23}} | collective-permute-start | bytes 1572872 | tf_op jit(solution)/shard_map/ppermute | solution.py:340
  360.7 16.4 %collective-permute-start.45 = (bf16[2048,768]{1,0:T(8,128)(2,1)}, bf16[2048,768]{1,0:T(8,128)(2,1)}, u32[]{:S(2)}, u32[]{:S(2)}) collective-permute-start(bf16[2048,768]{1,0:T(8,128)(2,1)} %convolution_convert_fusion.1), channel_id=1, source_target_pairs={{0,4},{4,0},{8,12},{12,8},{16,20},{20,16},{24,28},{28,24},{1,5},{5... | collective-permute-start | bytes 9437192 | tf_op jit(solution)/shard_map/ppermute | solution.py:255
  367.1 16.6 %collective-permute-start.46 = (bf16[512,512]{1,0:T(8,128)(2,1)}, bf16[512,512]{1,0:T(8,128)(2,1)S(1)}, u32[]{:S(2)}, u32[]{:S(2)}) collective-permute-start(bf16[512,512]{1,0:T(8,128)(2,1)} %get-tuple-element.180), channel_id=1, source_target_pairs={{0,8},{4,12},{8,16},{12,20},{1,9},{5,13},{9,17},{13,21},{2,10},{6,... | collective-permute-start | bytes 1572872 | tf_op jit(solution)/shard_map/ppermute | solution.py:339
  376.4 7.3 %collective-permute-start.47 = (bf16[512,512]{1,0:T(8,128)(2,1)S(1)}, bf16[512,512]{1,0:T(8,128)(2,1)S(1)}, u32[]{:S(2)}, u32[]{:S(2)}) collective-permute-start(bf16[512,512]{1,0:T(8,128)(2,1)S(1)} %copy-done.55), channel_id=1, source_target_pairs={{16,8},{20,12},{24,16},{28,20},{17,9},{21,13},{25,17},{29,21},{18,... | collective-permute-start | bytes 1572872 | tf_op jit(solution)/shard_map/ppermute | solution.py:340
  384.0 25.3 %collective-permute-start.48 = (bf16[512,512]{1,0:T(8,128)(2,1)S(1)}, bf16[512,512]{1,0:T(8,128)(2,1)S(1)}, u32[]{:S(2)}, u32[]{:S(2)}) collective-permute-start(bf16[512,512]{1,0:T(8,128)(2,1)S(1)} %get-tuple-element.190), channel_id=1, source_target_pairs={{0,8},{4,12},{8,16},{12,20},{16,24},{20,28},{1,9},{5,13},{9,17},{1... | collective-permute-start | bytes 1572872 | tf_op jit(solution)/shard_map/ppermute | solution.py:339
  397.0 14.9 %collective-permute-start.49 = (bf16[512,512]{1,0:T(8,128)(2,1)S(1)}, bf16[512,512]{1,0:T(8,128)(2,1)S(1)}, u32[]{:S(2)}, u32[]{:S(2)}) collective-permute-start(bf16[512,512]{1,0:T(8,128)(2,1)S(1)} %get-tuple-element.192), channel_id=1, source_target_pairs={{8,0},{12,4},{16,8},{20,12},{24,16},{28,20},{9,1},{13,5},{17,9},{2... | collective-permute-start | bytes 1572872 | tf_op jit(solution)/shard_map/ppermute | solution.py:340
  398.3 26.4 %collective-permute-start.50 = (bf16[512,768]{1,0:T(8,128)(2,1)S(1)}, bf16[512,768]{1,0:T(8,128)(2,1)S(1)}, u32[]{:S(2)}, u32[]{:S(2)}) collective-permute-start(bf16[512,768]{1,0:T(8,128)(2,1)S(1)} %get-tuple-element.187), channel_id=1, source_target_pairs={{0,8},{4,12},{1,9},{5,13},{2,10},{6,14},{3,11},{7,15}} | collective-permute-start | bytes 2359304 | tf_op jit(solution)/shard_map/ppermute | solution.py:339
  402.9 21.8 %collective-permute-start.51 = (bf16[512,768]{1,0:T(8,128)(2,1)S(1)}, bf16[512,768]{1,0:T(8,128)(2,1)S(1)}, u32[]{:S(2)}, u32[]{:S(2)}) collective-permute-start(bf16[512,768]{1,0:T(8,128)(2,1)S(1)} %get-tuple-element.194), channel_id=1, source_target_pairs={{24,16},{28,20},{25,17},{29,21},{26,18},{30,22},{27,19},{31,23}} | collective-permute-start | bytes 2359304 | tf_op jit(solution)/shard_map/ppermute | solution.py:340
  425.1 19.9 %collective-permute-start.52 = (bf16[512,768]{1,0:T(8,128)(2,1)S(1)}, bf16[512,768]{1,0:T(8,128)(2,1)S(1)}, u32[]{:S(2)}, u32[]{:S(2)}) collective-permute-start(bf16[512,768]{1,0:T(8,128)(2,1)S(1)} %get-tuple-element.195), channel_id=1, source_target_pairs={{0,8},{4,12},{8,16},{12,20},{1,9},{5,13},{9,17},{13,21},{2,10},{6,... | collective-permute-start | bytes 2359304 | tf_op jit(solution)/shard_map/ppermute | solution.py:339
  429.5 15.5 %collective-permute-start.53 = (bf16[512,768]{1,0:T(8,128)(2,1)S(1)}, bf16[512,768]{1,0:T(8,128)(2,1)S(1)}, u32[]{:S(2)}, u32[]{:S(2)}) collective-permute-start(bf16[512,768]{1,0:T(8,128)(2,1)S(1)} %get-tuple-element.198), channel_id=1, source_target_pairs={{16,8},{20,12},{24,16},{28,20},{17,9},{21,13},{25,17},{29,21},{18,... | collective-permute-start | bytes 2359304 | tf_op jit(solution)/shard_map/ppermute | solution.py:340
  446.6 23.3 %collective-permute-start.54 = (bf16[512,768]{1,0:T(8,128)(2,1)}, bf16[512,768]{1,0:T(8,128)(2,1)}, u32[]{:S(2)}, u32[]{:S(2)}) collective-permute-start(bf16[512,768]{1,0:T(8,128)(2,1)} %get-tuple-element.199), channel_id=1, source_target_pairs={{0,8},{4,12},{8,16},{12,20},{16,24},{20,28},{1,9},{5,13},{9,17},{1... | collective-permute-start | bytes 2359304 | tf_op jit(solution)/shard_map/ppermute | solution.py:339
  455.8 19.1 %collective-permute-start.55 = (bf16[512,768]{1,0:T(8,128)(2,1)}, bf16[512,768]{1,0:T(8,128)(2,1)}, u32[]{:S(2)}, u32[]{:S(2)}) collective-permute-start(bf16[512,768]{1,0:T(8,128)(2,1)} %get-tuple-element.202), channel_id=1, source_target_pairs={{8,0},{12,4},{16,8},{20,12},{24,16},{28,20},{9,1},{13,5},{17,9},{2... | collective-permute-start | bytes 2359304 | tf_op jit(solution)/shard_map/ppermute | solution.py:340
  (52 other events, 407.5 us)
Sparse Core Ops, SparseCore 0:
  312.5 46.0 reduce-scatter.2
  367.3 45.9 reduce-scatter.4
